TPU v7x, 32 devices: a whole 2x2x4 slice. The times are simulated.
32 devices in a mesh: groups: 2 (over y), tok: 4 (over z), ffn: 2 (over x), rep: 2 (over core).
Axes of the slice: x: 2, y: 2, z: 4, core: 2. Of those that a mesh axis runs over, the one named last changes fastest.
Arguments:
- queries: bfloat16 [64, 4096], P(('groups', 'tok', 'ffn'), 'rep'), parts along dimension 0, may hold values from -100 to 100
- new_key: bfloat16 [64, 512], P(('groups', 'tok', 'ffn'), 'rep'), parts along dimension 0, may hold values from -100 to 100
- new_value: bfloat16 [64, 512], P(('groups', 'tok', 'ffn'), 'rep'), parts along dimension 0, may hold values from -6 to 6
- key_cache: bfloat16 [64, 512, 512], P(('groups', 'tok', 'ffn'), None, 'rep'), parts along dimension 0, may hold values from -4 to 4
- value_cache: bfloat16 [64, 512, 512], P(('groups', 'tok', 'ffn'), None, 'rep'), parts along dimension 0, may hold values from -6 to 6
- lengths: int32 [64], P(('groups', 'tok', 'ffn')), parts along dimension 0, may hold values from 1 to 512
- slot_of: int32 [64], P('groups'), parts along dimension 0, may hold values from 0 to 31, each once
- residual_in: bfloat16 [64, 8192], P('groups', 'tok'), parts along dimension 0, may hold values from -100 to 100
- out_weight: bfloat16 [4, 1024, 8192], P('rep', 'ffn', 'tok'), may hold values from -0.5 to 0.5
- norm_gain: float32 [8192], P('tok'), may hold values from 0.5 to 1.5
- gate_weight: bfloat16 [8192, 14336], P('tok', ('ffn', 'rep')), may hold values from -0.0625 to 0.0625
- up_weight: bfloat16 [8192, 14336], P('tok', ('ffn', 'rep')), may hold values from -0.0625 to 0.0625
- down_weight: bfloat16 [14336, 8192], P(('ffn', 'rep'), 'tok'), may hold values from -0.046875 to 0.046875
Outputs:
- layer_out: bfloat16 [64, 8192], P(('groups', 'ffn', 'rep'), 'tok'), parts along dimension 0
There are 2 independent parts, one for each index of `groups`. A program takes and returns all parts, laid end to end along the dimension named above; an argument that names none is the same for every part. Nothing has to cross between parts.
Inputs may be any that keep to these rules, and one draw needn't show every extreme that they name: Each of 0 to 31 once; request i's queries, keys, values and length sit in row slot_of[i].
All inputs are finite; a program needn't handle non-finite values.
Results may differ from a plain program's by a relative error of at most 0.01.
Values may be sent and summed in bfloat16 or wider, within the bound.
No kernel may reach another device: no remote copies, remote signals or barrier semaphores. Data moves between devices by JAX's collectives and lax.ppermute only.
A program may use at most 128 MiB of HBM per device.

v0:
```python
import jax
import jax.numpy as jnp
from jax import lax
from jax.sharding import PartitionSpec as P

D = 8192
HEAD_DIM = 128


def shards(
    queries,
    new_key,
    new_value,
    key_cache,
    value_cache,
    lengths,
    slot_of,
    residual_in,
    out_weight,
    norm_gain,
    gate_weight,
    up_weight,
    down_weight,
):
    req_rows = queries.shape[0]
    kv_here = key_cache.shape[2] // HEAD_DIM
    group_size = queries.shape[1] // key_cache.shape[2]
    cache_span = key_cache.shape[1]
    score_scale = HEAD_DIM ** (-0.5)
    heads_q = queries.reshape(req_rows, kv_here, group_size, HEAD_DIM)
    keys_here = key_cache.reshape(req_rows, cache_span, kv_here, HEAD_DIM)
    values_here = value_cache.reshape(req_rows, cache_span, kv_here, HEAD_DIM)
    own_key = new_key.reshape(req_rows, kv_here, HEAD_DIM)
    own_value = new_value.reshape(req_rows, kv_here, HEAD_DIM)
    scores = (
        jnp.einsum("rgqd,rpgd->rgqp", heads_q, keys_here, preferred_element_type=jnp.float32)
        * score_scale
    )
    own_score = (
        jnp.einsum("rgqd,rgd->rgq", heads_q, own_key, preferred_element_type=jnp.float32)
        * score_scale
    )
    positions = lax.broadcasted_iota(jnp.int32, (req_rows, cache_span), 1)
    live_mask = positions < lengths[:, None]
    masked = jnp.where(live_mask[:, None, None, :], scores, -jnp.inf)
    row_top = jnp.maximum(jnp.max(masked, axis=-1), own_score)
    exp_cache = jnp.exp(masked - row_top[..., None])
    exp_own = jnp.exp(own_score - row_top)
    weight_sum = jnp.sum(exp_cache, axis=-1) + exp_own
    prob_cache = (exp_cache / weight_sum[..., None]).astype(jnp.bfloat16)
    prob_own = (exp_own / weight_sum).astype(jnp.bfloat16)
    attended = jnp.einsum(
        "rgqp,rpgd->rgqd", prob_cache, values_here, preferred_element_type=jnp.float32
    )
    attended = (
        attended
        + prob_own.astype(jnp.float32)[..., None] * own_value.astype(jnp.float32)[:, :, None, :]
    )
    attended = attended.astype(jnp.bfloat16).reshape(req_rows, kv_here, group_size * HEAD_DIM)
    feat_width = out_weight.shape[1]
    gathered = lax.all_gather(attended, ("tok", "ffn"), axis=0, tiled=True)
    head_block = lax.dynamic_slice_in_dim(
        gathered, lax.axis_index("ffn") * feat_width, feat_width, 2
    )
    ordered = head_block[slot_of].reshape(head_block.shape[0], kv_here * feat_width)
    local_proj = jnp.dot(
        ordered,
        out_weight.reshape(kv_here * feat_width, out_weight.shape[2]),
        preferred_element_type=jnp.float32,
    )
    projected = lax.psum(local_proj, ("ffn", "rep"))
    mid_state = (residual_in.astype(jnp.float32) + projected).astype(jnp.bfloat16)
    mid_float = mid_state.astype(jnp.float32)
    square_sum = lax.psum(jnp.sum(mid_float * mid_float, axis=1), "tok")
    inv_rms = lax.rsqrt(square_sum / D + 1e-05)
    normed = (mid_float * inv_rms[:, None] * norm_gain[None, :]).astype(jnp.bfloat16)
    gate_part = jnp.dot(normed, gate_weight, preferred_element_type=jnp.float32)
    up_part = jnp.dot(normed, up_weight, preferred_element_type=jnp.float32)
    gate, up_sum = (
        lax.psum(gate_part.astype(jnp.bfloat16), "tok").astype(jnp.float32),
        lax.psum(up_part.astype(jnp.bfloat16), "tok").astype(jnp.float32),
    )
    hidden = (jax.nn.silu(gate) * up_sum).astype(jnp.bfloat16)
    out_rows = hidden.shape[0] // lax.axis_size(("ffn", "rep"))
    own_share = lax.psum_scatter(
        jnp.dot(hidden, down_weight, preferred_element_type=jnp.float32).astype(jnp.bfloat16),
        ("ffn", "rep"),
        scatter_dimension=0,
        tiled=True,
    ).astype(jnp.float32)
    row_base = lax.axis_index(("ffn", "rep")) * out_rows
    state_rows = lax.dynamic_slice_in_dim(mid_float, row_base, out_rows, 0)
    return (state_rows + own_share).astype(jnp.bfloat16)


def solution(mesh):
    placed = (
        P(("groups", "tok", "ffn"), "rep"),
        P(("groups", "tok", "ffn"), "rep"),
        P(("groups", "tok", "ffn"), "rep"),
        P(("groups", "tok", "ffn"), None, "rep"),
        P(("groups", "tok", "ffn"), None, "rep"),
        P(("groups", "tok", "ffn")),
        P("groups"),
        P("groups", "tok"),
        P("rep", "ffn", "tok"),
        P("tok"),
        P("tok", ("ffn", "rep")),
        P("tok", ("ffn", "rep")),
        P(("ffn", "rep"), "tok"),
    )
    return jax.shard_map(
        shards,
        mesh=mesh,
        in_specs=placed,
        out_specs=P(("groups", "ffn", "rep"), "tok"),
        check_vma=False,
    )
```

profile of v0, /device:TPU:0, one launch (start us, length us, event | category | flops | bytes accessed | tf_op | source)
XLA Modules:
  0.0 179.5 jit_solution(2184682262506558719)
XLA Ops:
  6.5 0.0 copy-start
  6.5 0.0 all-reduce.4.cloned.1.call-start
  6.5 0.7 compare_select_fusion
  7.3 0.7 iota_compare_fusion
  8.0 0.7 reshape.64
  8.7 0.7 reshape.50
  9.4 0.8 fusion.18
  10.2 0.0 copy-done
  10.2 1.2 fusion.27
  11.4 0.2 fusion.14
  11.7 1.5 fusion.1
  13.2 0.0 slice-start
  13.2 0.0 copy-start.1
  13.2 32.4 %all_gather.3 = bf16[32,2,1024]{2,1,0:T(2,128)(2,1)S(1)} all-gather(bf16[4,2,1024]{2,1,0:T(2,128)(2,1)S(1)} %reshape.49), channel_id=1, replica_groups=mesh['groups'=2,'tok'=4,'ffn'=2,'rep'=2] {'tok','ffn'}, dimensions={0}, use_global_device_ids=true | all-gather | bytes 147456 | tf_op jit(solution)/shard_map/all_gather | solution.py:61
  45.7 0.7 gather_fusion
  46.4 3.7 %convolution_bitcast_fusion = f32[32,2048]{1,0:T(8,128)} fusion(bf16[2,512,2048]{2,1,0:T(8,128)(2,1)} %param.21, bf16[32,2,512]{2,1,0:T(2,128)(2,1)S(1)} %gather_fusion), kind=kOutput, calls=%fused_computation.3 | convolution fusion | flops 134217728 | bytes 4521984 | tf_op jit(solution)/shard_map/dot_general | solution.py:66
  50.1 0.0 all-reduce.4.cloned.1.call-update
  50.1 0.0 all-reduce.6.cloned.1.call-start
  50.2 33.0 %all-reduce.4.cloned.1.call-done = f32[32,2048]{1,0:T(8,128)} async-done(((f32[32,2048]{1,0:T(8,128)}), f32[32,2048]{1,0:T(8,128)}) %all-reduce.4.cloned.1.call-update) | async-done | bytes 262160 | tf_op jit(solution)/shard_map/psum | solution.py:71
  83.2 1.1 multiply_reduce_fusion
  84.3 11.7 %psum.29 = f32[32]{0:T(128)S(1)} all-reduce(f32[32]{0:T(128)S(1)} %get-tuple-element.7), channel_id=1, replica_groups=mesh['groups'=2,'tok'=4,'ffn'=2,'rep'=2] {'tok'}, use_global_device_ids=true, to_apply=%region_4.5 | all-reduce | flops 32 | bytes 256 | tf_op jit(solution)/shard_map/psum | solution.py:74
  96.0 0.0 slice-start.1
  96.0 0.0 slice-start.2
  96.0 0.0 slice-start.3
  96.0 8.7 %convolution_convert_fusion = bf16[32,3584]{1,0:T(8,128)(2,1)} fusion(bf16[2048,3584]{1,0:T(8,128)(2,1)} %param.24, f32[32,2048]{1,0:T(8,128)S(1)} %get-tuple-element.8, f32[2048]{0:T(1024)} %param.22, f32[32]{0:T(128)S(1)} %add_rsqrt_fusion), kind=kOutput, calls=%fused_computation.1 | convolution fusion | flops 470073344 | bytes 15179904 | tf_op jit(solution)/shard_map/dot_general | solution.py:78
  104.7 0.0 slice-done
  104.7 0.0 copy-done.1
  104.7 0.0 slice-done.1
  104.7 0.0 slice-done.2
  104.7 0.1 slice-done.3
  104.8 3.4 %convolution_convert_fusion.1 = bf16[32,3584]{1,0:T(8,128)(2,1)} fusion(bf16[2048,3584]{1,0:T(8,128)(2,1)S(1)} %bitcast.37, f32[32,2048]{1,0:T(8,128)S(1)} %get-tuple-element.8, f32[2048]{0:T(1024)S(1)} %copy-done.1, f32[32]{0:T(128)S(1)} %add_rsqrt_fusion), kind=kOutput, calls=%fused_computation.2 | convolution fusion | flops 470073344 | bytes 15179904 | tf_op jit(solution)/shard_map/dot_general | solution.py:77
  108.2 0.0 all-reduce.6.cloned.1.call-update
  108.2 0.0 reduce-scatter.2.cloned.1.call-start
  108.3 35.3 %all-reduce.6.cloned.1.call-done = (bf16[32,3584]{1,0:T(8,128)(2,1)}, bf16[32,3584]{1,0:T(8,128)(2,1)}) async-done(((bf16[32,3584]{1,0:T(8,128)(2,1)}, bf16[32,3584]{1,0:T(8,128)(2,1)}), (bf16[32,3584]{1,0:T(8,128)(2,1)}, bf16[32,3584]{1,0:T(8,128)(2,1)})) %all-reduce.6.cloned.1.call-update) | async-done | bytes 458768 | tf_op jit(solution)/shard_map/psum | solution.py:81
  143.6 8.7 %convolution_convert_fusion.2 = bf16[32,2048]{1,0:T(8,128)(2,1)} fusion(bf16[3584,2048]{1,0:T(8,128)(2,1)} %param.25, bf16[32,3584]{1,0:T(8,128)(2,1)} %get-tuple-element.5, bf16[32,3584]{1,0:T(8,128)(2,1)} %get-tuple-element.6), kind=kOutput, calls=%fused_computation.4 | convolution fusion | flops 470745088 | bytes 15269888 | tf_op jit(solution)/shard_map/dot_general | solution.py:86
  152.3 0.0 reduce-scatter.2.cloned.1.call-update
  152.3 19.3 %reduce-scatter.2.cloned.1.call-done = bf16[8,2048]{1,0:T(8,128)(2,1)} async-done(((bf16[32,2048]{1,0:T(8,128)(2,1)}), bf16[8,2048]{1,0:T(8,128)(2,1)}) %reduce-scatter.2.cloned.1.call-update) | async-done | bytes 32784 | tf_op jit(solution)/shard_map/reduce_scatter | solution.py:85
  171.6 1.4 add_convert_fusion.1
  (7 shorter events, 0.1 us)
Async XLA Ops:
  6.5 3.7 %copy-start = (bf16[4,512,256]{2,1,0:T(8,128)(2,1)S(1)}, bf16[4,512,256]{2,1,0:T(8,128)(2,1)}, u32[]{:S(2)}) copy-start(bf16[4,512,256]{2,1,0:T(8,128)(2,1)} %param.16) | copy-start | bytes 3145732
  6.5 76.6 %all-reduce.4.cloned.1.call-start = ((), (), s32[]{:S(2)}) async-start(), calls=%async_computation.1 | async-start | bytes 524288 | tf_op jit(solution)/shard_map/psum | solution.py:71
  13.2 91.5 %slice-start = ((s8[14680064]{0:T(1024)(128)(4,1)}), s8[2097152]{0:T(1024)(128)(4,1)S(1)}, s32[]{:S(2)}) async-start(s8[14680064]{0:T(1024)(128)(4,1)} %bitcast.36), calls=%async_computation.4 | async-start | bytes 4194304
  13.2 91.5 %copy-start.1 = (f32[2048]{0:T(1024)S(1)}, f32[2048]{0:T(1024)}, u32[]{:S(2)}) copy-start(f32[2048]{0:T(1024)} %param.22) | copy-start | bytes 24580
  50.1 93.4 %all-reduce.6.cloned.1.call-start = ((), (), s32[]{:S(2)}) async-start(), calls=%async_computation.3 | async-start | bytes 917504 | tf_op jit(solution)/shard_map/psum | solution.py:81
  96.0 8.7 %slice-start.1 = ((s8[14680064]{0:T(1024)(128)(4,1)}), s8[4194304]{0:T(1024)(128)(4,1)S(1)}, s32[]{:S(2)}) async-start(s8[14680064]{0:T(1024)(128)(4,1)} %bitcast.36), calls=%async_computation.5 | async-start | bytes 8388608
  96.0 8.7 %slice-start.2 = ((s8[14680064]{0:T(1024)(128)(4,1)}), s8[4194304]{0:T(1024)(128)(4,1)S(1)}, s32[]{:S(2)}) async-start(s8[14680064]{0:T(1024)(128)(4,1)} %bitcast.36), calls=%async_computation.6 | async-start | bytes 8388608
  96.0 8.8 %slice-start.3 = ((s8[14680064]{0:T(1024)(128)(4,1)}), s8[4194304]{0:T(1024)(128)(4,1)S(1)}, s32[]{:S(2)}) async-start(s8[14680064]{0:T(1024)(128)(4,1)} %bitcast.36), calls=%async_computation.7 | async-start | bytes 8388608
  108.2 63.3 %reduce-scatter.2.cloned.1.call-start = ((), (), s32[]{:S(2)}) async-start(), calls=%async_computation.2 | async-start | bytes 163840 | tf_op jit(solution)/shard_map/reduce_scatter | solution.py:85
Sparse Core Ops, SparseCore 0:
  50.3 32.8 all-reduce.3
  108.4 35.1 all-reduce.5
  152.4 19.1 reduce-scatter.1
where the time goes:
time: 180 us; the launch traced here: 179 us
  waiting for transfers between devices  87.6 us (49%)
  blocking collectives  44.1 us (24%)
  matrix products  28 us (16%)
  between operations  13.2 us (7%)
  other arithmetic  4.2 us (2%)
  local copies, waits for them, and re-layouts  2.26 us (1%)
    psum x1, waiting for transfers between devices, shards(): lax.psum(up_part.astype(jnp.bfloat16), 'tok').astype(jnp.float32)  35.3 us
    psum x1, waiting for transfers between devices, shards(): projected = lax.psum(local_proj, ('ffn', 'rep'))  33 us
    all_gather x1, blocking collectives, shards(): gathered = lax.all_gather(attended, ('tok', 'ffn'), axis=0, tiled=True)  32.4 us
    reduce_scatter x1, waiting for transfers between devices, shards(): lax.psum_scatter(jnp.dot(hidden, down_weight, preferred_element_type=jnp....  19.3 us
    psum x1, blocking collectives, shards(): square_sum = lax.psum(jnp.sum(mid_float * mid_float, axis=1), 'tok')  11.7 us
    dot_general x1, matrix products, shards(): up_part = jnp.dot(normed, up_weight, preferred_element_type=jnp.float32)  8.72 us
    dot_general x1, matrix products, shards(): jnp.dot(hidden, down_weight, preferred_element_type=jnp.float32)  8.71 us
    dot_general x1, matrix products, shards(): jnp.dot(ordered, out_weight.reshape(kv_here * feat_width, out_weight.shap...  3.71 us
  transfers between devices with their start and end apart: 3, of which 3 were waited for; matrix products, arithmetic and copies ran while one was open for 0% of the time, Pallas kernels for 0%

commit v1 on v0

v1 whole, which is shorter than its diff:
```python
import functools

import jax
import jax.numpy as jnp
from jax import lax
from jax.experimental import pallas as pl
from jax.experimental.pallas import tpu as pltpu
from jax.sharding import PartitionSpec as P

HEAD_DIM = 128
F32 = jnp.float32
BF16 = jnp.bfloat16
MIB = 2**20
VMEM = pl.BlockSpec(memory_space=pltpu.VMEM)
SMEM = pl.BlockSpec(memory_space=pltpu.SMEM)
HBM = pl.BlockSpec(memory_space=pl.ANY)


def swap(extent, step):
    return [(a, a ^ step) for a in range(extent)]


def column_step(width):
    for step in (896, 512, 256, 128):
        if width % step == 0:
            return step
    return width


def attend(
    copies, lens, queries, new_key, new_value, keys, values, out, key_buf, value_buf, sems
):
    slots, span, width = key_buf.shape
    kv_here = width // HEAD_DIM
    group = queries.shape[1] // width
    rows = group * slots
    loads = []
    for s in range(slots):
        loads.append(pltpu.make_async_copy(keys.at[s], key_buf.at[s], sems.at[0, s]))
    for s in range(slots):
        loads.append(pltpu.make_async_copy(values.at[s], value_buf.at[s], sems.at[1, s]))
    for load in loads:
        load.start()
    scale = HEAD_DIM ** (-0.5)
    slot_id = lax.rem(lax.broadcasted_iota(jnp.int32, (rows, 1), 0), slots)
    live_len = jnp.zeros((rows, 1), jnp.int32)
    for s in range(slots):
        live_len = jnp.where(slot_id == s, lens[s], live_len)
    live = lax.broadcasted_iota(jnp.int32, (rows, span), 1) < live_len
    q_all = queries[...].astype(F32)
    own_k = new_key[...].astype(F32)
    own_v = new_value[...].astype(F32)
    heads_q, own_score = [], []
    for g in range(kv_here):
        cols = slice(g * HEAD_DIM, (g + 1) * HEAD_DIM)
        first = g * group
        q = jnp.concatenate(
            [
                q_all[:, (first + h) * HEAD_DIM : (first + h + 1) * HEAD_DIM]
                for h in range(group)
            ],
            axis=0,
        )
        k = jnp.concatenate([own_k[:, cols]] * group, axis=0)
        own_score.append(jnp.sum(q * k, axis=1, keepdims=True) * scale)
        heads_q.append(q.astype(BF16))
    scores = [jnp.zeros((rows, span), F32) for _ in range(kv_here)]
    for s in range(slots):
        loads[s].wait()
        for g in range(kv_here):
            here = lax.dot_general(
                heads_q[g],
                key_buf[s, :, g * HEAD_DIM : (g + 1) * HEAD_DIM],
                (((1,), (1,)), ((), ())),
                preferred_element_type=F32,
            )
            scores[g] = jnp.where(slot_id == s, here, scores[g])
    probs, totals = [], []
    for g in range(kv_here):
        masked = jnp.where(live, scores[g] * scale, -jnp.inf)
        top = jnp.maximum(jnp.max(masked, axis=1, keepdims=True), own_score[g])
        exp_cache = jnp.exp(masked - top)
        exp_own = jnp.exp(own_score[g] - top)
        total = jnp.sum(exp_cache, axis=1, keepdims=True) + exp_own
        probs.append((exp_cache / total).astype(BF16))
        own = jnp.concatenate(
            [own_v[:, g * HEAD_DIM : (g + 1) * HEAD_DIM]] * group, axis=0
        )
        totals.append((exp_own / total).astype(BF16).astype(F32) * own)
    for s in range(slots):
        loads[slots + s].wait()
        for g in range(kv_here):
            here = jnp.where(slot_id == s, probs[g], jnp.zeros_like(probs[g]))
            totals[g] += jnp.dot(
                here,
                value_buf[s, :, g * HEAD_DIM : (g + 1) * HEAD_DIM],
                preferred_element_type=F32,
            )
    width_out = out.shape[2]
    heads_out = width_out // HEAD_DIM
    parts = group // heads_out
    for f in range(parts):
        block = jnp.concatenate(
            [
                jnp.concatenate(
                    [totals[g][h * slots : (h + 1) * slots] for g in range(kv_here)], axis=0
                )
                for h in range(f * heads_out, (f + 1) * heads_out)
            ],
            axis=1,
        ).astype(BF16)
        for t in range(copies):
            out[t * parts + f] = block


def project(slots, slot_of, heads, weight, out):
    requests = slot_of.shape[1]
    blocks, rows, width = heads.shape
    kv_here = weight.shape[0]
    table = heads[...].astype(F32).reshape(blocks * rows, width).astype(BF16)
    slot = slot_of[...]
    where_from = (slot // slots) * rows + lax.rem(slot, slots)
    row = lax.broadcasted_iota(jnp.int32, (blocks * rows, requests), 0)
    ordered = []
    for g in range(kv_here):
        pick = (row == where_from + g * slots).astype(F32).astype(BF16)
        ordered.append(
            lax.dot_general(
                pick, table, (((0,), (0,)), ((), ())), preferred_element_type=F32
            ).astype(BF16)
        )
    step = column_step(out.shape[1])
    for c in range(0, out.shape[1], step):
        total = jnp.zeros((requests, step), F32)
        for g in range(kv_here):
            total += jnp.dot(
                ordered[g], weight[g, :, c : c + step], preferred_element_type=F32
            )
        out[:, c : c + step] = total.astype(BF16)


def gate_and_up(others, *refs):
    place, residual, gain, here = refs[:4]
    arrived = refs[4 : 4 + others]
    gate_weight, up_weight, mid_out = refs[4 + others : 7 + others]
    parts = refs[7 + others : -2]
    ordered, squares = refs[-2:]
    blocks, rows, _ = ordered.shape
    width = gate_weight.shape[1]
    mid = residual[...].astype(F32) + here[...].astype(F32)
    for other in arrived:
        mid += other[...].astype(F32)
    mid = mid.astype(BF16).astype(F32)
    share = mid_out.shape[1]
    for j in range(mid_out.shape[0]):
        mid_out[j] = mid[j * share : (j + 1) * share].astype(BF16)
    square = jnp.broadcast_to(jnp.sum(mid * mid, axis=1, keepdims=True), (mid.shape[0], 128))
    scaled = mid * gain[...]
    for k in range(blocks):
        ordered[k] = scaled[k * rows : (k + 1) * rows]
        squares[k] = square[k * rows : (k + 1) * rows]
    mine = place[0]
    left = jnp.concatenate([ordered[mine ^ k] for k in range(blocks)], axis=0).astype(BF16)
    lane = lax.broadcasted_iota(jnp.int32, (rows, 128), 1)
    for k in range(blocks):
        value = squares[mine ^ k]
        high = value.astype(BF16).astype(F32)
        middle = (value - high).astype(BF16).astype(F32)
        low = value - high - middle
        stat = jnp.where(lane == 0, high, jnp.where(lane == 1, middle, low))
        parts[k][:, 2 * width :] = jnp.where(lane < 3, stat, 0.0).astype(BF16)
    step = column_step(width)
    for base, weight in ((0, gate_weight), (width, up_weight)):
        for c in range(0, width, step):
            total = jnp.dot(left, weight[:, c : c + step], preferred_element_type=F32)
            for k in range(blocks):
                parts[k][:, base + c : base + c + step] = total[
                    k * rows : (k + 1) * rows
                ].astype(BF16)


def activate(features, *refs):
    out = refs[-1]
    width = out.shape[1]
    total = refs[0][...].astype(F32)
    for part in refs[1:-1]:
        total += part[...].astype(F32)
    square = jnp.sum(total[:, 2 * width :], axis=1, keepdims=True)
    inv_rms = lax.rsqrt(square / features + 1e-05)
    gate = total[:, :width] * inv_rms
    up = total[:, width : 2 * width] * inv_rms
    out[...] = (gate / (1.0 + jnp.exp(-gate)) * up).astype(BF16)


def down(blocks, *refs):
    place = refs[0]
    parts = refs[1 : 1 + blocks]
    weight = refs[1 + blocks]
    outs = refs[2 + blocks : -1]
    ordered = refs[-1]
    rows = parts[0].shape[0]
    share = outs[0].shape[0]
    for k in range(blocks):
        at = pl.multiple_of((place[0] ^ k) * rows, 8)
        ordered[pl.ds(at, rows)] = parts[k][...].astype(F32)
    left = jnp.concatenate(
        [
            ordered[pl.ds(pl.multiple_of((place[1] ^ j) * share, 8), share)]
            for j in range(len(outs))
        ],
        axis=0,
    ).astype(BF16)
    width = weight.shape[1]
    step = column_step(width)
    for c in range(0, width, step):
        total = jnp.dot(left, weight[:, c : c + step], preferred_element_type=F32)
        for j, out in enumerate(outs):
            out[:, c : c + step] = total[j * share : (j + 1) * share].astype(BF16)


def finish(place, mid, *refs):
    out = refs[-1]
    total = mid[place[1]].astype(F32)
    for part in refs[:-1]:
        total += part[...].astype(F32)
    out[...] = total.astype(BF16)


def like(*shape):
    return jax.ShapeDtypeStruct(shape, BF16)


def limit(mib):
    return pltpu.CompilerParams(vmem_limit_bytes=mib * MIB)


def shards(
    queries,
    new_key,
    new_value,
    key_cache,
    value_cache,
    lengths,
    slot_of,
    residual_in,
    out_weight,
    norm_gain,
    gate_weight,
    up_weight,
    down_weight,
):
    tok, ffn, rep = (lax.axis_size(a) for a in ("tok", "ffn", "rep"))
    sums = ffn * rep
    slots, span, kv_width = key_cache.shape
    kv_here = kv_width // HEAD_DIM
    requests, features = residual_in.shape
    hidden_here = gate_weight.shape[1]
    feat_width = out_weight.shape[1]
    place = jnp.stack([lax.axis_index("tok"), lax.axis_index(("ffn", "rep"))]).astype(jnp.int32)
    in_vmem = functools.partial(pltpu.with_memory_space_constraint, memory_space=pltpu.VMEM)
    out_weight, gate_weight, up_weight, down_weight = (
        in_vmem(w) for w in (out_weight, gate_weight, up_weight, down_weight)
    )

    attended = pl.pallas_call(
        functools.partial(attend, tok),
        out_shape=like(tok * ffn, slots * kv_here, feat_width),
        in_specs=[SMEM, VMEM, VMEM, VMEM, HBM, HBM],
        out_specs=VMEM,
        scratch_shapes=[
            pltpu.VMEM(key_cache.shape, BF16),
            pltpu.VMEM(value_cache.shape, BF16),
            pltpu.SemaphoreType.DMA((2, slots)),
        ],
        compiler_params=limit(8),
        name="attend",
    )(lengths, queries, new_key, new_value, key_cache, value_cache)
    gathered = lax.all_to_all(attended, ("tok", "ffn"), 0, 0)

    partial = pl.pallas_call(
        functools.partial(project, slots),
        out_shape=like(requests, features),
        in_specs=[VMEM, VMEM, VMEM],
        out_specs=VMEM,
        compiler_params=limit(8),
        name="project",
    )(slot_of.reshape(1, requests), gathered, out_weight)
    here = partial
    for k in range(1, rep):
        here = here + lax.ppermute(partial, "rep", swap(rep, k))
    arrived = [lax.ppermute(here, "ffn", swap(ffn, k)) for k in range(1, ffn)]

    rows = requests // tok
    share = requests // sums
    mid, *parts = pl.pallas_call(
        functools.partial(gate_and_up, len(arrived)),
        out_shape=[like(sums, share, features)] + [like(rows, 2 * hidden_here + 128)] * tok,
        in_specs=[SMEM] + [VMEM] * (5 + len(arrived)),
        out_specs=[VMEM] * (1 + tok),
        scratch_shapes=[
            pltpu.VMEM((tok, rows, features), F32),
            pltpu.VMEM((tok, rows, 128), F32),
        ],
        compiler_params=limit(8),
        name="gate_and_up",
    )(place, residual_in, norm_gain.reshape(1, features), here, *arrived, gate_weight, up_weight)
    order = sorted(range(1, tok), reverse=True)
    got = [parts[0]] + [lax.ppermute(parts[k], "tok", swap(tok, k)) for k in order]

    hidden = pl.pallas_call(
        functools.partial(activate, features * tok),
        out_shape=like(rows, hidden_here),
        in_specs=[VMEM] * tok,
        out_specs=VMEM,
        compiler_params=limit(8),
        name="activate",
    )(*got)
    pieces = {k: lax.ppermute(hidden, "tok", swap(tok, k)) for k in order}

    downs = pl.pallas_call(
        functools.partial(down, tok),
        out_shape=[like(share, features)] * sums,
        in_specs=[SMEM] + [VMEM] * (1 + tok),
        out_specs=[VMEM] * sums,
        scratch_shapes=[pltpu.VMEM((requests, hidden_here), F32)],
        compiler_params=limit(8),
        name="down",
    )(place, hidden, *[pieces[k] for k in range(1, tok)], down_weight)
    order = sorted(range(1, sums), reverse=True)
    got = [downs[0]] + [lax.ppermute(downs[j], ("ffn", "rep"), swap(sums, j)) for j in order]

    return pl.pallas_call(
        finish,
        out_shape=like(share, features),
        in_specs=[SMEM] + [VMEM] * (1 + sums),
        out_specs=VMEM,
        compiler_params=limit(8),
        name="finish",
    )(place, mid, *got)


def solution(mesh):
    placed = (
        P(("groups", "tok", "ffn"), "rep"),
        P(("groups", "tok", "ffn"), "rep"),
        P(("groups", "tok", "ffn"), "rep"),
        P(("groups", "tok", "ffn"), None, "rep"),
        P(("groups", "tok", "ffn"), None, "rep"),
        P(("groups", "tok", "ffn")),
        P("groups"),
        P("groups", "tok"),
        P("rep", "ffn", "tok"),
        P("tok"),
        P("tok", ("ffn", "rep")),
        P("tok", ("ffn", "rep")),
        P(("ffn", "rep"), "tok"),
    )
    return jax.shard_map(
        shards,
        mesh=mesh,
        in_specs=placed,
        out_specs=P(("groups", "ffn", "rep"), "tok"),
        check_vma=False,
    )
```

time: 180 us -> 78.5 us (0.44)
  waiting for transfers between devices: 87.6 us -> 19.1 us
  blocking collectives: 44.1 us -> 14 us
  matrix products: 28 us -> 0 us
  local copies, waits for them, and re-layouts: 2.26 us -> 20 us
  Pallas kernels: 0 us -> 13.5 us
  between operations: 13.2 us -> 0.09 us
  starting transfers between devices: 0.09 us -> 11.3 us
  other arithmetic: 4.2 us -> 0.11 us
    psum x2 -> x0, waiting for transfers between devices: 68.2 us -> none  [the longest x1 35.3 us: shards(): lax.psum(up_part.astype(jnp.bfloat16), 'tok').astype(jnp.float32)]
    all_gather x1 -> x0, blocking collectives: 32.4 us -> none  [shards(): gathered = lax.all_gather(attended, ('tok', 'ffn'), axis=0, tiled=True)]
    dot_general x7 -> x0, matrix products: 28 us -> none  [the longest x1 8.72 us: shards(): up_part = jnp.dot(normed, up_weight, preferred_element_type=jnp.float32)]
    unnamed x12 -> x32, local copies, waits for them, and re-layouts: 0.13 us -> 20 us
    reduce_scatter x1 -> x0, waiting for transfers between devices: 19.3 us -> none  [shards(): lax.psum_scatter(jnp.dot(hidden, down_weight, preferred_element_type=jnp....]
    ppermute x0 -> x11, waiting for transfers between devices: none -> 19.1 us  [the longest x3 7.5 us: shards(): lax.ppermute(parts[k], 'tok', swap(tok, k))]
    all_to_all x0 -> x1, blocking collectives: none -> 14 us  [shards(): gathered = lax.all_to_all(attended, ('tok', 'ffn'), 0, 0)]
    pallas_call x0 -> x6, Pallas kernels: none -> 13.5 us  [the longest x1 5.42 us: shards(): pl.pallas_call(functools.partial(gate_and_up, len(arrived)), out_shape=[l...]
  transfers between devices with their start and end apart: 3 -> 11, of which waited for: 3 -> 8; matrix products, arithmetic and copies ran while one was open for 0% -> 0% of each run, Pallas kernels for 0% -> 0%
where the time goes in v1:
time: 78.5 us; the launch traced here: 77.9 us
  local copies, waits for them, and re-layouts  20 us (25%)
  waiting for transfers between devices  19.1 us (24%)
  blocking collectives  14 us (18%)
  Pallas kernels  13.5 us (17%)
  starting transfers between devices  11.3 us (14%)
    unnamed x32, local copies, waits for them, and re-layouts  20 us
    all_to_all x1, blocking collectives, shards(): gathered = lax.all_to_all(attended, ('tok', 'ffn'), 0, 0)  14 us
    ppermute x3, waiting for transfers between devices, shards(): lax.ppermute(parts[k], 'tok', swap(tok, k))  7.5 us
    pallas_call x1, Pallas kernels, shards(): pl.pallas_call(functools.partial(gate_and_up, len(arrived)), out_shape=[l...  5.42 us
    ppermute x1, waiting for transfers between devices, shards(): arrived = [lax.ppermute(here, 'ffn', swap(ffn, k)) for k in range(1, ffn)]  5.09 us
    ppermute x3, starting transfers between devices, shards(): lax.ppermute(parts[k], 'tok', swap(tok, k))  4.45 us
    ppermute x3, starting transfers between devices, shards(): pieces = {k: lax.ppermute(hidden, 'tok', swap(tok, k)) for k in order}  4.45 us
    pallas_call x1, Pallas kernels, shards(): pl.pallas_call(functools.partial(down, tok), out_shape=[like(share, featu...  3.17 us
  transfers between devices with their start and end apart: 11, of which 8 were waited for; matrix products, arithmetic and copies ran while one was open for 0% of the time, Pallas kernels for 0%

profile of v1, /device:TPU:0, one launch (start us, length us, event | category | flops | bytes accessed | tf_op | source)
XLA Modules:
  0.0 77.9 jit_solution(3007310084054185855)
XLA Ops:
  0.0 0.0 copy-start.3
  0.0 1.2 %copy-done.3 = bf16[4,512,256]{2,1,0:T(8,128)(2,1)S(1)} copy-done((bf16[4,512,256]{2,1,0:T(8,128)(2,1)S(1)}, bf16[4,512,256]{2,1,0:T(8,128)(2,1)}, u32[]{:S(2)}) %copy-start.3) | copy-done | bytes 1048600
  1.2 0.0 copy-start.4
  1.2 1.2 %copy-done.4 = bf16[4,512,256]{2,1,0:T(8,128)(2,1)S(1)} copy-done((bf16[4,512,256]{2,1,0:T(8,128)(2,1)S(1)}, bf16[4,512,256]{2,1,0:T(8,128)(2,1)}, u32[]{:S(2)}) %copy-start.4) | copy-done | bytes 1048600
  2.5 0.0 copy-start.6
  2.5 0.7 copy-done.6
  3.2 0.0 copy-start.8
  3.2 0.7 copy-done.8
  3.9 0.0 copy-start.9
  3.9 0.7 copy-done.9
  4.5 0.0 copy-start.10
  4.5 0.7 copy-done.10
  5.2 2.5 %attend.1 = bf16[8,8,512]{2,1,0:T(8,128)(2,1)S(1)} custom-call(s32[4]{0:T(128)S(1)} %copy-done.10, bf16[4,2048]{1,0:T(4,128)(2,1)S(1)} %copy-done.6, bf16[4,256]{1,0:T(4,128)(2,1)S(1)} %copy-done.8, bf16[4,256]{1,0:T(4,128)(2,1)S(1)} %copy-done.9, bf16[4,512,256]{2,1,0:T(8,128)(2,1)S(1)} %copy-done.3, bf16[4,512,256]{2,1,0:T(8,128)(2,1)S(1)} %copy-done.4), custom_call_target="tpu_custom_call" | custom-call | tf_op jit(solution)/shard_map/attend/pallas_call | solution.py:265
  7.7 14.0 %all_to_all.5.heads = bf16[8,8,512]{2,1,0:T(8,128)(2,1)S(1)} all-to-all(bf16[8,8,512]{2,1,0:T(8,128)(2,1)S(1)} %attend.1), channel_id=1, replica_groups=mesh['groups'=2,'tok'=4,'ffn'=2,'rep'=2] {'tok','ffn'}, dimensions={0} | all-to-all | bytes 131072 | tf_op jit(solution)/shard_map/all_to_all | solution.py:278
  21.7 0.0 copy-start.2
  21.7 2.2 %copy-done.2 = bf16[2,512,2048]{2,1,0:T(8,128)(2,1)S(1)} copy-done((bf16[2,512,2048]{2,1,0:T(8,128)(2,1)S(1)}, bf16[2,512,2048]{2,1,0:T(8,128)(2,1)}, u32[]{:S(2)}) %copy-start.2) | copy-done | bytes 4194328
  23.8 0.0 copy-start.11
  23.8 0.7 copy-done.11
  24.5 0.0 slice-start
  24.5 1.0 %project.1 = bf16[32,2048]{1,0:T(8,128)(2,1)S(1)} custom-call(s32[1,32]{1,0:T(1,128)S(1)} %bitcast.7, bf16[8,8,512]{2,1,0:T(8,128)(2,1)S(1)} %all_to_all.5.heads, bf16[2,512,2048]{2,1,0:T(8,128)(2,1)S(1)} %copy-done.2), custom_call_target="tpu_custom_call" | custom-call | tf_op jit(solution)/shard_map/project/pallas_call | solution.py:280
  25.5 0.0 collective-permute-start
  25.5 1.3 %collective-permute-done = bf16[32,2048]{1,0:T(8,128)(2,1)S(1)} collective-permute-done((bf16[32,2048]{1,0:T(8,128)(2,1)S(1)}, bf16[32,2048]{1,0:T(8,128)(2,1)S(1)}, u32[]{:S(2)}, u32[]{:S(2)}) %collective-permute-start) | collective-permute-done | bytes 131104 | tf_op jit(solution)/shard_map/ppermute | solution.py:290
  26.9 0.5 collective-permute-start.1
  27.3 0.1 pad_add_fusion.refs_0_.place
  27.4 5.1 %collective-permute-done.1.refs_4_ = bf16[32,2048]{1,0:T(8,128)(2,1)S(1)} collective-permute-done((bf16[32,2048]{1,0:T(8,128)(2,1)S(1)}, bf16[32,2048]{1,0:T(8,128)(2,1)S(1)}, u32[]{:S(2)}, u32[]{:S(2)}) %collective-permute-start.1) | collective-permute-done | bytes 131104 | tf_op jit(solution)/shard_map/ppermute | solution.py:291
  32.5 0.0 copy-start
  32.5 5.2 %copy-done = bf16[2048,3584]{1,0:T(8,128)(2,1)S(1)} copy-done((bf16[2048,3584]{1,0:T(8,128)(2,1)S(1)}, bf16[2048,3584]{1,0:T(8,128)(2,1)}, u32[]{:S(2)}) %copy-start) | copy-done | bytes 14680088
  37.7 0.0 copy-start.1
  37.7 5.2 %copy-done.1 = bf16[2048,3584]{1,0:T(8,128)(2,1)S(1)} copy-done((bf16[2048,3584]{1,0:T(8,128)(2,1)S(1)}, bf16[2048,3584]{1,0:T(8,128)(2,1)}, u32[]{:S(2)}) %copy-start.1) | copy-done | bytes 14680088
  42.9 0.0 copy-start.5
  42.9 0.9 %copy-done.5 = bf16[32,2048]{1,0:T(8,128)(2,1)S(1)} copy-done((bf16[32,2048]{1,0:T(8,128)(2,1)S(1)}, bf16[32,2048]{1,0:T(8,128)(2,1)}, u32[]{:S(2)}) %copy-start.5) | copy-done | bytes 131096
  43.8 0.0 copy-start.7
  43.8 0.7 copy-done.7
  44.5 0.0 slice-start.1
  44.5 0.0 slice-start.2
  44.5 0.0 slice-start.3
  44.5 5.4 %gate_and_up.1 = (bf16[4,8,2048]{2,1,0:T(8,128)(2,1)S(1)}, bf16[8,7296]{1,0:T(8,128)(2,1)S(1)}, bf16[8,7296]{1,0:T(8,128)(2,1)S(1)}, bf16[8,7296]{1,0:T(8,128)(2,1)S(1)}, bf16[8,7296]{1,0:T(8,128)(2,1)S(1)}) custom-call(s32[2]{0:T(128)S(1)} %pad_add_fusion.refs_0_.place, bf16[32,2048]{1,0:T(8,128)(2,1)S(1)} %copy-done.5, f32[1,2048]{1,0:T(1,128)S(1)} %bitcast.6, ...), custom_call_target="tpu_custom_call" | custom-call | tf_op jit(solution)/shard_map/gate_and_up/pallas_call | solution.py:295
  49.9 0.6 collective-permute-start.2
  50.5 1.1 %collective-permute-start.3 = (bf16[8,7296]{1,0:T(8,128)(2,1)S(1)}, bf16[8,7296]{1,0:T(8,128)(2,1)S(1)}, u32[]{:S(2)}, u32[]{:S(2)}) collective-permute-start(bf16[8,7296]{1,0:T(8,128)(2,1)S(1)} %get-tuple-element.17), channel_id=1, source_target_pairs={{0,8},{4,12},{8,0},{12,4},{1,9},{5,13},{9,1},{13,5},{2,10},{6,14},... | collective-permute-start | bytes 350216 | tf_op jit(solution)/shard_map/ppermute | solution.py:308
  51.6 2.7 %collective-permute-start.4 = (bf16[8,7296]{1,0:T(8,128)(2,1)S(1)}, bf16[8,7296]{1,0:T(8,128)(2,1)S(1)}, u32[]{:S(2)}, u32[]{:S(2)}) collective-permute-start(bf16[8,7296]{1,0:T(8,128)(2,1)S(1)} %get-tuple-element.18), channel_id=1, source_target_pairs={{0,4},{4,0},{8,12},{12,8},{1,5},{5,1},{9,13},{13,9},{2,6},{6,2},{1... | collective-permute-start | bytes 350216 | tf_op jit(solution)/shard_map/ppermute | solution.py:308
  54.3 3.5 %collective-permute-done.2.refs_1_ = bf16[8,7296]{1,0:T(8,128)(2,1)S(1)} collective-permute-done((bf16[8,7296]{1,0:T(8,128)(2,1)S(1)}, bf16[8,7296]{1,0:T(8,128)(2,1)S(1)}, u32[]{:S(2)}, u32[]{:S(2)}) %collective-permute-start.2) | collective-permute-done | bytes 116768 | tf_op jit(solution)/shard_map/ppermute | solution.py:308
  57.9 4.0 %collective-permute-done.3.refs_2_ = bf16[8,7296]{1,0:T(8,128)(2,1)S(1)} collective-permute-done((bf16[8,7296]{1,0:T(8,128)(2,1)S(1)}, bf16[8,7296]{1,0:T(8,128)(2,1)S(1)}, u32[]{:S(2)}, u32[]{:S(2)}) %collective-permute-start.3) | collective-permute-done | bytes 116768 | tf_op jit(solution)/shard_map/ppermute | solution.py:308
  61.8 0.0 collective-permute-done.4.refs_3_
  61.8 0.2 activate.1.refs_1_
  62.0 1.5 %collective-permute-start.7 = (bf16[8,3584]{1,0:T(8,128)(2,1)S(1)}, bf16[8,3584]{1,0:T(8,128)(2,1)S(1)}, u32[]{:S(2)}, u32[]{:S(2)}) collective-permute-start(bf16[8,3584]{1,0:T(8,128)(2,1)S(1)} %activate.1.refs_1_), channel_id=1, source_target_pairs={{0,12},{4,8},{8,4},{12,0},{1,13},{5,9},{9,5},{13,1},{2,14},{6,10},... | collective-permute-start | bytes 172040 | tf_op jit(solution)/shard_map/ppermute | solution.py:318
  63.5 0.0 collective-permute-start.6
  63.5 3.0 %collective-permute-start.5 = (bf16[8,3584]{1,0:T(8,128)(2,1)S(1)}, bf16[8,3584]{1,0:T(8,128)(2,1)S(1)}, u32[]{:S(2)}, u32[]{:S(2)}) collective-permute-start(bf16[8,3584]{1,0:T(8,128)(2,1)S(1)} %activate.1.refs_1_), channel_id=1, source_target_pairs={{0,4},{4,0},{8,12},{12,8},{1,5},{5,1},{9,13},{13,9},{2,6},{6,2},{1... | collective-permute-start | bytes 172040 | tf_op jit(solution)/shard_map/ppermute | solution.py:318
  66.5 1.6 %collective-permute-done.7.refs_4_ = bf16[8,3584]{1,0:T(8,128)(2,1)S(1)} collective-permute-done((bf16[8,3584]{1,0:T(8,128)(2,1)S(1)}, bf16[8,3584]{1,0:T(8,128)(2,1)S(1)}, u32[]{:S(2)}, u32[]{:S(2)}) %collective-permute-start.7) | collective-permute-done | bytes 57376 | tf_op jit(solution)/shard_map/ppermute | solution.py:318
  68.1 1.2 %collective-permute-done.6.refs_3_ = bf16[8,3584]{1,0:T(8,128)(2,1)S(1)} collective-permute-done((bf16[8,3584]{1,0:T(8,128)(2,1)S(1)}, bf16[8,3584]{1,0:T(8,128)(2,1)S(1)}, u32[]{:S(2)}, u32[]{:S(2)}) %collective-permute-start.6) | collective-permute-done | bytes 57376 | tf_op jit(solution)/shard_map/ppermute | solution.py:318
  69.3 0.0 collective-permute-done.5.refs_2_
  69.3 0.0 slice-done
  69.3 0.0 slice-done.1
  69.3 0.0 slice-done.2
  69.4 0.0 slice-done.3
  69.4 3.2 %down.1 = (bf16[8,2048]{1,0:T(8,128)(2,1)S(1)}, bf16[8,2048]{1,0:T(8,128)(2,1)S(1)}, bf16[8,2048]{1,0:T(8,128)(2,1)S(1)}, bf16[8,2048]{1,0:T(8,128)(2,1)S(1)}) custom-call(s32[2]{0:T(128)S(1)} %pad_add_fusion.refs_0_.place, bf16[8,3584]{1,0:T(8,128)(2,1)S(1)} %activate.1.refs_1_, bf16[8,3584]{1,0:T(8,128)(2,1)S(1)} %collective-permute-done.5.refs_2_, ...), custom_call_target="tpu_custom_call" | custom-call | tf_op jit(solution)/shard_map/down/pallas_call | solution.py:320
  72.5 0.0 collective-permute-start.8
  72.6 1.1 %collective-permute-start.9 = (bf16[8,2048]{1,0:T(8,128)(2,1)S(1)}, bf16[8,2048]{1,0:T(8,128)(2,1)S(1)}, u32[]{:S(2)}, u32[]{:S(2)}) collective-permute-start(bf16[8,2048]{1,0:T(8,128)(2,1)S(1)} %get-tuple-element.21), channel_id=1, source_target_pairs={{0,2},{1,3},{2,0},{3,1},{4,6},{5,7},{6,4},{7,5},{8,10},{9,11},{10,... | collective-permute-start | bytes 98312 | tf_op jit(solution)/shard_map/ppermute | solution.py:330
  73.7 0.7 collective-permute-start.10
  74.4 1.5 %collective-permute-done.8.refs_1_ = bf16[8,2048]{1,0:T(8,128)(2,1)S(1)} collective-permute-done((bf16[8,2048]{1,0:T(8,128)(2,1)S(1)}, bf16[8,2048]{1,0:T(8,128)(2,1)S(1)}, u32[]{:S(2)}, u32[]{:S(2)}) %collective-permute-start.8) | collective-permute-done | bytes 32800 | tf_op jit(solution)/shard_map/ppermute | solution.py:330
  75.9 0.9 %collective-permute-done.9.refs_2_ = bf16[8,2048]{1,0:T(8,128)(2,1)S(1)} collective-permute-done((bf16[8,2048]{1,0:T(8,128)(2,1)S(1)}, bf16[8,2048]{1,0:T(8,128)(2,1)S(1)}, u32[]{:S(2)}, u32[]{:S(2)}) %collective-permute-start.9) | collective-permute-done | bytes 32800 | tf_op jit(solution)/shard_map/ppermute | solution.py:330
  76.8 0.0 collective-permute-done.10.refs_3_
  76.8 1.2 %finish.1 = bf16[8,2048]{1,0:T(8,128)(2,1)} custom-call(s32[2]{0:T(128)S(1)} %pad_add_fusion.refs_0_.place, bf16[4,8,2048]{2,1,0:T(8,128)(2,1)S(1)} %get-tuple-element.14.mid, bf16[8,2048]{1,0:T(8,128)(2,1)S(1)} %get-tuple-element.19.refs_0_, bf16[8,2048]{1,0:T(8,128)(2,1)S(1)} %collective-permute-done.8.refs_1_, ...), custom_call_target="tpu_custom_call" | custom-call | tf_op jit(solution)/shard_map/finish/pallas_call | solution.py:332
  (2 shorter events, 0.0 us)
Async XLA Ops:
  0.0 1.2 %copy-start.3 = (bf16[4,512,256]{2,1,0:T(8,128)(2,1)S(1)}, bf16[4,512,256]{2,1,0:T(8,128)(2,1)}, u32[]{:S(2)}) copy-start(bf16[4,512,256]{2,1,0:T(8,128)(2,1)} %keys.1) | copy-start | bytes 3145732
  1.2 1.2 %copy-start.4 = (bf16[4,512,256]{2,1,0:T(8,128)(2,1)S(1)}, bf16[4,512,256]{2,1,0:T(8,128)(2,1)}, u32[]{:S(2)}) copy-start(bf16[4,512,256]{2,1,0:T(8,128)(2,1)} %values.1) | copy-start | bytes 3145732
  2.5 0.7 copy-start.6
  3.2 0.7 copy-start.8
  3.9 0.7 copy-start.9
  4.5 0.7 copy-start.10
  21.7 2.2 %copy-start.2 = (bf16[2,512,2048]{2,1,0:T(8,128)(2,1)S(1)}, bf16[2,512,2048]{2,1,0:T(8,128)(2,1)}, u32[]{:S(2)}) copy-start(bf16[2,512,2048]{2,1,0:T(8,128)(2,1)} %weight.1) | copy-start | bytes 12582916
  23.8 0.7 copy-start.11
  24.5 44.8 %slice-start = ((s8[14680064]{0:T(1024)(128)(4,1)}), s8[2097152]{0:T(1024)(128)(4,1)S(1)}, s32[]{:S(2)}) async-start(s8[14680064]{0:T(1024)(128)(4,1)} %bitcast.4), calls=%async_computation.1 | async-start | bytes 4194304
  25.5 1.4 %collective-permute-start = (bf16[32,2048]{1,0:T(8,128)(2,1)S(1)}, bf16[32,2048]{1,0:T(8,128)(2,1)S(1)}, u32[]{:S(2)}, u32[]{:S(2)}) collective-permute-start(bf16[32,2048]{1,0:T(8,128)(2,1)S(1)} %project.1), channel_id=1, source_target_pairs={{0,1},{1,0},{2,3},{3,2},{4,5},{5,4},{6,7},{7,6},{8,9},{9,8},{10,11... | collective-permute-start | bytes 393224 | tf_op jit(solution)/shard_map/ppermute | solution.py:290
  26.9 5.6 %collective-permute-start.1 = (bf16[32,2048]{1,0:T(8,128)(2,1)S(1)}, bf16[32,2048]{1,0:T(8,128)(2,1)S(1)}, u32[]{:S(2)}, u32[]{:S(2)}) collective-permute-start(bf16[32,2048]{1,0:T(8,128)(2,1)S(1)} %add.7.refs_3_), channel_id=1, source_target_pairs={{0,2},{2,0},{1,3},{3,1},{4,6},{6,4},{5,7},{7,5},{8,10},{10,8},{9,1... | collective-permute-start | bytes 393224 | tf_op jit(solution)/shard_map/ppermute | solution.py:291
  32.5 5.2 %copy-start = (bf16[2048,3584]{1,0:T(8,128)(2,1)S(1)}, bf16[2048,3584]{1,0:T(8,128)(2,1)}, u32[]{:S(2)}) copy-start(bf16[2048,3584]{1,0:T(8,128)(2,1)} %refs_5_.2) | copy-start | bytes 44040196
  37.7 5.2 %copy-start.1 = (bf16[2048,3584]{1,0:T(8,128)(2,1)S(1)}, bf16[2048,3584]{1,0:T(8,128)(2,1)}, u32[]{:S(2)}) copy-start(bf16[2048,3584]{1,0:T(8,128)(2,1)} %refs_6_.1) | copy-start | bytes 44040196
  42.9 0.9 %copy-start.5 = (bf16[32,2048]{1,0:T(8,128)(2,1)S(1)}, bf16[32,2048]{1,0:T(8,128)(2,1)}, u32[]{:S(2)}) copy-start(bf16[32,2048]{1,0:T(8,128)(2,1)} %refs_1_.1) | copy-start | bytes 393220
  43.8 0.7 copy-start.7
  44.5 24.9 %slice-start.1 = ((s8[14680064]{0:T(1024)(128)(4,1)}), s8[4194304]{0:T(1024)(128)(4,1)S(1)}, s32[]{:S(2)}) async-start(s8[14680064]{0:T(1024)(128)(4,1)} %bitcast.4), calls=%async_computation.2 | async-start | bytes 8388608
  44.5 24.9 %slice-start.2 = ((s8[14680064]{0:T(1024)(128)(4,1)}), s8[4194304]{0:T(1024)(128)(4,1)S(1)}, s32[]{:S(2)}) async-start(s8[14680064]{0:T(1024)(128)(4,1)} %bitcast.4), calls=%async_computation.3 | async-start | bytes 8388608
  44.5 24.9 %slice-start.3 = ((s8[14680064]{0:T(1024)(128)(4,1)}), s8[4194304]{0:T(1024)(128)(4,1)S(1)}, s32[]{:S(2)}) async-start(s8[14680064]{0:T(1024)(128)(4,1)} %bitcast.4), calls=%async_computation.4 | async-start | bytes 8388608
  49.9 8.0 %collective-permute-start.2 = (bf16[8,7296]{1,0:T(8,128)(2,1)S(1)}, bf16[8,7296]{1,0:T(8,128)(2,1)S(1)}, u32[]{:S(2)}, u32[]{:S(2)}) collective-permute-start(bf16[8,7296]{1,0:T(8,128)(2,1)S(1)} %get-tuple-element.16), channel_id=1, source_target_pairs={{0,12},{4,8},{8,4},{12,0},{1,13},{5,9},{9,5},{13,1},{2,14},{6,10},... | collective-permute-start | bytes 350216 | tf_op jit(solution)/shard_map/ppermute | solution.py:308
  50.5 11.3 %collective-permute-start.3 = (bf16[8,7296]{1,0:T(8,128)(2,1)S(1)}, bf16[8,7296]{1,0:T(8,128)(2,1)S(1)}, u32[]{:S(2)}, u32[]{:S(2)}) collective-permute-start(bf16[8,7296]{1,0:T(8,128)(2,1)S(1)} %get-tuple-element.17), channel_id=1, source_target_pairs={{0,8},{4,12},{8,0},{12,4},{1,9},{5,13},{9,1},{13,5},{2,10},{6,14},... | collective-permute-start | bytes 350216 | tf_op jit(solution)/shard_map/ppermute | solution.py:308
  51.6 10.2 %collective-permute-start.4 = (bf16[8,7296]{1,0:T(8,128)(2,1)S(1)}, bf16[8,7296]{1,0:T(8,128)(2,1)S(1)}, u32[]{:S(2)}, u32[]{:S(2)}) collective-permute-start(bf16[8,7296]{1,0:T(8,128)(2,1)S(1)} %get-tuple-element.18), channel_id=1, source_target_pairs={{0,4},{4,0},{8,12},{12,8},{1,5},{5,1},{9,13},{13,9},{2,6},{6,2},{1... | collective-permute-start | bytes 350216 | tf_op jit(solution)/shard_map/ppermute | solution.py:308
  62.0 6.1 %collective-permute-start.7 = (bf16[8,3584]{1,0:T(8,128)(2,1)S(1)}, bf16[8,3584]{1,0:T(8,128)(2,1)S(1)}, u32[]{:S(2)}, u32[]{:S(2)}) collective-permute-start(bf16[8,3584]{1,0:T(8,128)(2,1)S(1)} %activate.1.refs_1_), channel_id=1, source_target_pairs={{0,12},{4,8},{8,4},{12,0},{1,13},{5,9},{9,5},{13,1},{2,14},{6,10},... | collective-permute-start | bytes 172040 | tf_op jit(solution)/shard_map/ppermute | solution.py:318
  63.5 5.8 %collective-permute-start.6 = (bf16[8,3584]{1,0:T(8,128)(2,1)S(1)}, bf16[8,3584]{1,0:T(8,128)(2,1)S(1)}, u32[]{:S(2)}, u32[]{:S(2)}) collective-permute-start(bf16[8,3584]{1,0:T(8,128)(2,1)S(1)} %activate.1.refs_1_), channel_id=1, source_target_pairs={{0,8},{4,12},{8,0},{12,4},{1,9},{5,13},{9,1},{13,5},{2,10},{6,14},... | collective-permute-start | bytes 172040 | tf_op jit(solution)/shard_map/ppermute | solution.py:318
  63.5 5.8 %collective-permute-start.5 = (bf16[8,3584]{1,0:T(8,128)(2,1)S(1)}, bf16[8,3584]{1,0:T(8,128)(2,1)S(1)}, u32[]{:S(2)}, u32[]{:S(2)}) collective-permute-start(bf16[8,3584]{1,0:T(8,128)(2,1)S(1)} %activate.1.refs_1_), channel_id=1, source_target_pairs={{0,4},{4,0},{8,12},{12,8},{1,5},{5,1},{9,13},{13,9},{2,6},{6,2},{1... | collective-permute-start | bytes 172040 | tf_op jit(solution)/shard_map/ppermute | solution.py:318
  72.5 3.4 %collective-permute-start.8 = (bf16[8,2048]{1,0:T(8,128)(2,1)S(1)}, bf16[8,2048]{1,0:T(8,128)(2,1)S(1)}, u32[]{:S(2)}, u32[]{:S(2)}) collective-permute-start(bf16[8,2048]{1,0:T(8,128)(2,1)S(1)} %get-tuple-element.20), channel_id=1, source_target_pairs={{0,3},{1,2},{2,1},{3,0},{4,7},{5,6},{6,5},{7,4},{8,11},{9,10},{10,... | collective-permute-start | bytes 98312 | tf_op jit(solution)/shard_map/ppermute | solution.py:330
  72.6 4.2 %collective-permute-start.9 = (bf16[8,2048]{1,0:T(8,128)(2,1)S(1)}, bf16[8,2048]{1,0:T(8,128)(2,1)S(1)}, u32[]{:S(2)}, u32[]{:S(2)}) collective-permute-start(bf16[8,2048]{1,0:T(8,128)(2,1)S(1)} %get-tuple-element.21), channel_id=1, source_target_pairs={{0,2},{1,3},{2,0},{3,1},{4,6},{5,7},{6,4},{7,5},{8,10},{9,11},{10,... | collective-permute-start | bytes 98312 | tf_op jit(solution)/shard_map/ppermute | solution.py:330
  73.7 3.1 %collective-permute-start.10 = (bf16[8,2048]{1,0:T(8,128)(2,1)S(1)}, bf16[8,2048]{1,0:T(8,128)(2,1)S(1)}, u32[]{:S(2)}, u32[]{:S(2)}) collective-permute-start(bf16[8,2048]{1,0:T(8,128)(2,1)S(1)} %get-tuple-element.22), channel_id=1, source_target_pairs={{0,1},{1,0},{2,3},{3,2},{4,5},{5,4},{6,7},{7,6},{8,9},{9,8},{10,11... | collective-permute-start | bytes 98312 | tf_op jit(solution)/shard_map/ppermute | solution.py:330

commit v2 on v1

--- a/solution.py
+++ b/solution.py
@@ -13,7 +13,8 @@
 MIB = 2**20
 VMEM = pl.BlockSpec(memory_space=pltpu.VMEM)
 SMEM = pl.BlockSpec(memory_space=pltpu.SMEM)
-HBM = pl.BlockSpec(memory_space=pl.ANY)
+ANY = pl.BlockSpec(memory_space=pl.ANY)
+HBM = ANY
 
 
 def swap(extent, step):
@@ -28,19 +29,26 @@
 
 
 def attend(
-    copies, lens, queries, new_key, new_value, keys, values, out, key_buf, value_buf, sems
+    copies, lens_in, queries_in, new_key_in, new_value_in, keys, values, *refs
 ):
+    count = (len(refs) - 8) // 2
+    carried_in, out, carried_out = refs[:count], refs[count], refs[count + 1 : 2 * count + 1]
+    lens, queries, new_key, new_value, key_buf, value_buf, sems = refs[2 * count + 1 :]
     slots, span, width = key_buf.shape
     kv_here = width // HEAD_DIM
     group = queries.shape[1] // width
     rows = group * slots
-    loads = []
-    for s in range(slots):
-        loads.append(pltpu.make_async_copy(keys.at[s], key_buf.at[s], sems.at[0, s]))
-    for s in range(slots):
-        loads.append(pltpu.make_async_copy(values.at[s], value_buf.at[s], sems.at[1, s]))
+    small = [(lens_in, lens), (queries_in, queries), (new_key_in, new_key)]
+    small.append((new_value_in, new_value))
+    pairs = small + [(keys.at[s], key_buf.at[s]) for s in range(slots)]
+    pairs += [(values.at[s], value_buf.at[s]) for s in range(slots)]
+    pairs += list(zip(carried_in, carried_out))
+    loads = [pltpu.make_async_copy(a, b, sems.at[i]) for i, (a, b) in enumerate(pairs)]
     for load in loads:
         load.start()
+    for load in loads[: len(small)]:
+        load.wait()
+    loads = loads[len(small) :]
     scale = HEAD_DIM ** (-0.5)
     slot_id = lax.rem(lax.broadcasted_iota(jnp.int32, (rows, 1), 0), slots)
     live_len = jnp.zeros((rows, 1), jnp.int32)
@@ -111,6 +119,22 @@
         ).astype(BF16)
         for t in range(copies):
             out[t * parts + f] = block
+    for load in loads[2 * slots :]:
+        load.wait()
+
+
+def fetch(first, source, *refs):
+    out, sems = refs[-2:]
+    rows = out.shape[0] // sems.shape[0]
+    loads = []
+    for i in range(sems.shape[0]):
+        at = pl.ds(i * rows, rows)
+        columns = pl.ds(first, out.shape[1])
+        loads.append(pltpu.make_async_copy(source.at[at, columns], out.at[at], sems.at[i]))
+    for load in loads:
+        load.start()
+    for load in loads:
+        load.wait()
 
 
 def project(slots, slot_of, heads, weight, out):
@@ -139,14 +163,14 @@
         out[:, c : c + step] = total.astype(BF16)
 
 
-def gate_and_up(others, *refs):
+def gate(others, *refs):
     place, residual, gain, here = refs[:4]
     arrived = refs[4 : 4 + others]
-    gate_weight, up_weight, mid_out = refs[4 + others : 7 + others]
-    parts = refs[7 + others : -2]
+    weight, mid_out, left_out, stat_out = refs[4 + others : 8 + others]
+    parts = refs[8 + others : -2]
     ordered, squares = refs[-2:]
     blocks, rows, _ = ordered.shape
-    width = gate_weight.shape[1]
+    width = weight.shape[1]
     mid = residual[...].astype(F32) + here[...].astype(F32)
     for other in arrived:
         mid += other[...].astype(F32)
@@ -161,6 +185,7 @@
         squares[k] = square[k * rows : (k + 1) * rows]
     mine = place[0]
     left = jnp.concatenate([ordered[mine ^ k] for k in range(blocks)], axis=0).astype(BF16)
+    left_out[...] = left
     lane = lax.broadcasted_iota(jnp.int32, (rows, 128), 1)
     for k in range(blocks):
         value = squares[mine ^ k]
@@ -168,35 +193,75 @@
         middle = (value - high).astype(BF16).astype(F32)
         low = value - high - middle
         stat = jnp.where(lane == 0, high, jnp.where(lane == 1, middle, low))
-        parts[k][:, 2 * width :] = jnp.where(lane < 3, stat, 0.0).astype(BF16)
+        stat = jnp.where(lane < 3, stat, 0.0).astype(BF16)
+        if k < 2:
+            stat_out[k] = stat
+        else:
+            parts[k][:, width:] = stat
     step = column_step(width)
-    for base, weight in ((0, gate_weight), (width, up_weight)):
-        for c in range(0, width, step):
-            total = jnp.dot(left, weight[:, c : c + step], preferred_element_type=F32)
-            for k in range(blocks):
-                parts[k][:, base + c : base + c + step] = total[
-                    k * rows : (k + 1) * rows
-                ].astype(BF16)
-
-
-def activate(features, *refs):
+    for c in range(0, width, step):
+        total = jnp.dot(left, weight[:, c : c + step], preferred_element_type=F32)
+        for k in range(blocks):
+            parts[k][:, c : c + step] = total[k * rows : (k + 1) * rows].astype(BF16)
+
+
+def up(left, weight, *refs):
+    parts = refs[:-2]
+    buf, sems = refs[-2:]
+    rows, width = parts[0].shape
+    step = column_step(width)
+    loads = []
+    for i, c in enumerate(range(0, width, step)):
+        at = pl.ds(c, step)
+        loads.append(pltpu.make_async_copy(weight.at[:, at], buf.at[:, at], sems.at[i]))
+    for load in loads:
+        load.start()
+    rhs = left[...]
+    for i, c in enumerate(range(0, width, step)):
+        loads[i].wait()
+        total = jnp.dot(rhs, buf[:, c : c + step], preferred_element_type=F32)
+        for k, part in enumerate(parts):
+            part[:, c : c + step] = total[k * rows : (k + 1) * rows].astype(BF16)
+
+
+def join(up_part, gate_part, stat, *refs):
+    out = refs[-1]
+    width = up_part.shape[1]
+    out[:, :width] = up_part[...]
+    out[:, width : 2 * width] = gate_part[...]
+    out[:, 2 * width :] = stat[1]
+
+
+def activate(features, near, *refs):
     out = refs[-1]
     width = out.shape[1]
-    total = refs[0][...].astype(F32)
-    for part in refs[1:-1]:
-        total += part[...].astype(F32)
-    square = jnp.sum(total[:, 2 * width :], axis=1, keepdims=True)
+    own_up, own_gate, own_stat = refs[:3]
+    both, refs = refs[3 : 2 + near], refs[2 + near : -1]
+    far = len(refs) // 2
+    ups, gates = refs[:far], refs[far : 2 * far]
+    up_sum = own_up[...].astype(F32)
+    gate_sum = own_gate[...].astype(F32)
+    stat = own_stat[0].astype(F32)
+    for part in both:
+        up_sum += part[:, :width].astype(F32)
+        gate_sum += part[:, width : 2 * width].astype(F32)
+        stat += part[:, 2 * width :].astype(F32)
+    for part in ups:
+        up_sum += part[...].astype(F32)
+    for part in gates:
+        gate_sum += part[:, :width].astype(F32)
+        stat += part[:, width:].astype(F32)
+    square = jnp.sum(stat, axis=1, keepdims=True)
     inv_rms = lax.rsqrt(square / features + 1e-05)
-    gate = total[:, :width] * inv_rms
-    up = total[:, width : 2 * width] * inv_rms
-    out[...] = (gate / (1.0 + jnp.exp(-gate)) * up).astype(BF16)
-
-
-def down(blocks, *refs):
+    gated = gate_sum * inv_rms
+    out[...] = (gated / (1.0 + jnp.exp(-gated)) * (up_sum * inv_rms)).astype(BF16)
+
+
+def down(blocks, pieces, *refs):
     place = refs[0]
     parts = refs[1 : 1 + blocks]
-    weight = refs[1 + blocks]
-    outs = refs[2 + blocks : -1]
+    weights = refs[1 + blocks : 1 + blocks + pieces]
+    outs = refs[1 + blocks + pieces : -1]
     ordered = refs[-1]
     rows = parts[0].shape[0]
     share = outs[0].shape[0]
@@ -210,12 +275,16 @@
         ],
         axis=0,
     ).astype(BF16)
-    width = weight.shape[1]
-    step = column_step(width)
-    for c in range(0, width, step):
-        total = jnp.dot(left, weight[:, c : c + step], preferred_element_type=F32)
-        for j, out in enumerate(outs):
-            out[:, c : c + step] = total[j * share : (j + 1) * share].astype(BF16)
+    base = 0
+    for weight in weights:
+        width = weight.shape[1]
+        step = column_step(width)
+        for c in range(0, width, step):
+            total = jnp.dot(left, weight[:, c : c + step], preferred_element_type=F32)
+            for j, out in enumerate(outs):
+                at = base + c
+                out[:, at : at + step] = total[j * share : (j + 1) * share].astype(BF16)
+        base += width
 
 
 def finish(place, mid, *refs):
@@ -232,6 +301,22 @@
 
 def limit(mib):
     return pltpu.CompilerParams(vmem_limit_bytes=mib * MIB)
+
+
+def fetched(source, after, first=0, width=None):
+    width = width or source.shape[1]
+    return pl.pallas_call(
+        functools.partial(fetch, first),
+        out_shape=pltpu.VMEM((source.shape[0], width), source.dtype),
+        in_specs=[HBM, HBM],
+        out_specs=VMEM,
+        scratch_shapes=[pltpu.SemaphoreType.DMA((8,))],
+        compiler_params=limit(1),
+        cost_estimate=pl.CostEstimate(
+            flops=0, transcendentals=0, bytes_accessed=0
+        ),
+        name="fetch",
+    )(pltpu.with_memory_space_constraint(source, pltpu.HBM), after)
 
 
 def shards(
@@ -257,24 +342,37 @@
     hidden_here = gate_weight.shape[1]
     feat_width = out_weight.shape[1]
     place = jnp.stack([lax.axis_index("tok"), lax.axis_index(("ffn", "rep"))]).astype(jnp.int32)
-    in_vmem = functools.partial(pltpu.with_memory_space_constraint, memory_space=pltpu.VMEM)
-    out_weight, gate_weight, up_weight, down_weight = (
-        in_vmem(w) for w in (out_weight, gate_weight, up_weight, down_weight)
-    )
-
-    attended = pl.pallas_call(
+    in_hbm = functools.partial(pltpu.with_memory_space_constraint, memory_space=pltpu.HBM)
+
+    carried = [
+        out_weight,
+        slot_of.reshape(1, requests),
+        residual_in,
+        norm_gain.reshape(1, features),
+    ]
+    attended, out_weight, slot_of, residual_in, norm_gain = pl.pallas_call(
         functools.partial(attend, tok),
-        out_shape=like(tok * ffn, slots * kv_here, feat_width),
-        in_specs=[SMEM, VMEM, VMEM, VMEM, HBM, HBM],
-        out_specs=VMEM,
+        out_shape=[like(tok * ffn, slots * kv_here, feat_width)]
+        + [pltpu.VMEM(a.shape, a.dtype) for a in carried],
+        in_specs=[HBM] * (6 + len(carried)),
+        out_specs=[VMEM] * (1 + len(carried)),
         scratch_shapes=[
+            pltpu.SMEM(lengths.shape, jnp.int32),
+            pltpu.VMEM(queries.shape, BF16),
+            pltpu.VMEM(new_key.shape, BF16),
+            pltpu.VMEM(new_value.shape, BF16),
             pltpu.VMEM(key_cache.shape, BF16),
             pltpu.VMEM(value_cache.shape, BF16),
-            pltpu.SemaphoreType.DMA((2, slots)),
+            pltpu.SemaphoreType.DMA((4 + 2 * slots + len(carried),)),
         ],
         compiler_params=limit(8),
         name="attend",
-    )(lengths, queries, new_key, new_value, key_cache, value_cache)
+    )(
+        *(
+            in_hbm(a)
+            for a in [lengths, queries, new_key, new_value, key_cache, value_cache] + carried
+        )
+    )
     gathered = lax.all_to_all(attended, ("tok", "ffn"), 0, 0)
 
     partial = pl.pallas_call(
@@ -284,48 +382,82 @@
         out_specs=VMEM,
         compiler_params=limit(8),
         name="project",
-    )(slot_of.reshape(1, requests), gathered, out_weight)
+    )(slot_of, gathered, out_weight)
     here = partial
     for k in range(1, rep):
         here = here + lax.ppermute(partial, "rep", swap(rep, k))
     arrived = [lax.ppermute(here, "ffn", swap(ffn, k)) for k in range(1, ffn)]
+    gate_weight = fetched(gate_weight, here)
 
     rows = requests // tok
     share = requests // sums
-    mid, *parts = pl.pallas_call(
-        functools.partial(gate_and_up, len(arrived)),
-        out_shape=[like(sums, share, features)] + [like(rows, 2 * hidden_here + 128)] * tok,
-        in_specs=[SMEM] + [VMEM] * (5 + len(arrived)),
-        out_specs=[VMEM] * (1 + tok),
+    near = min(2, tok)
+    both_width = 2 * hidden_here + 128
+    mid, left, stat, *gates = pl.pallas_call(
+        functools.partial(gate, len(arrived)),
+        out_shape=[like(sums, share, features), like(requests, features), like(near, rows, 128)]
+        + [like(rows, hidden_here + (128 if k >= near else 0)) for k in range(tok)],
+        in_specs=[SMEM] + [VMEM] * (4 + len(arrived)),
+        out_specs=[VMEM] * (3 + tok),
         scratch_shapes=[
             pltpu.VMEM((tok, rows, features), F32),
             pltpu.VMEM((tok, rows, 128), F32),
         ],
         compiler_params=limit(8),
-        name="gate_and_up",
-    )(place, residual_in, norm_gain.reshape(1, features), here, *arrived, gate_weight, up_weight)
-    order = sorted(range(1, tok), reverse=True)
-    got = [parts[0]] + [lax.ppermute(parts[k], "tok", swap(tok, k)) for k in order]
+        name="gate",
+    )(place, residual_in, norm_gain, here, *arrived, gate_weight)
+    far = sorted(range(near, tok), reverse=True)
+    got_gates = [lax.ppermute(gates[k], "tok", swap(tok, k)) for k in far]
+    ups = pl.pallas_call(
+        up,
+        out_shape=[like(rows, hidden_here)] * tok,
+        in_specs=[VMEM, HBM],
+        out_specs=[VMEM] * tok,
+        scratch_shapes=[
+            pltpu.VMEM(up_weight.shape, BF16),
+            pltpu.SemaphoreType.DMA((hidden_here // column_step(hidden_here),)),
+        ],
+        compiler_params=limit(20),
+        cost_estimate=pl.CostEstimate(
+            flops=0, transcendentals=0, bytes_accessed=4 * up_weight.size
+        ),
+        name="up",
+    )(left, in_hbm(up_weight))
+    got_ups = [lax.ppermute(ups[k], "tok", swap(tok, k)) for k in far]
+    got_both = []
+    if near > 1:
+        both = pl.pallas_call(
+            join,
+            out_shape=like(rows, both_width),
+            in_specs=[VMEM] * 3 + [ANY] * len(far),
+            out_specs=VMEM,
+            compiler_params=limit(4),
+            name="join",
+        )(ups[1], gates[1], stat, *got_gates)
+        got_both.append(lax.ppermute(both, "tok", swap(tok, 1)))
+    half = features // 2
+    down_left = fetched(down_weight, ups[0], 0, half)
 
     hidden = pl.pallas_call(
-        functools.partial(activate, features * tok),
+        functools.partial(activate, features * tok, near),
         out_shape=like(rows, hidden_here),
-        in_specs=[VMEM] * tok,
+        in_specs=[VMEM] * (2 + near + 2 * len(far)) + [ANY],
         out_specs=VMEM,
         compiler_params=limit(8),
         name="activate",
-    )(*got)
-    pieces = {k: lax.ppermute(hidden, "tok", swap(tok, k)) for k in order}
+    )(ups[0], gates[0], stat, *got_both, *got_ups, *got_gates, down_left)
+    pieces = {k: lax.ppermute(hidden, "tok", swap(tok, k)) for k in sorted(range(1, tok), reverse=True)}
+    down_right = fetched(down_weight, hidden, half, half)
 
     downs = pl.pallas_call(
-        functools.partial(down, tok),
+        functools.partial(down, tok, 2),
         out_shape=[like(share, features)] * sums,
-        in_specs=[SMEM] + [VMEM] * (1 + tok),
+        in_specs=[SMEM] + [VMEM] * (2 + tok),
         out_specs=[VMEM] * sums,
         scratch_shapes=[pltpu.VMEM((requests, hidden_here), F32)],
         compiler_params=limit(8),
         name="down",
-    )(place, hidden, *[pieces[k] for k in range(1, tok)], down_weight)
+    )(place, hidden, *[pieces[k] for k in range(1, tok)], down_left, down_right)
     order = sorted(range(1, sums), reverse=True)
     got = [downs[0]] + [lax.ppermute(downs[j], ("ffn", "rep"), swap(sums, j)) for j in order]
 

time: 78.5 us -> 62.9 us (0.80)
  local copies, waits for them, and re-layouts: 20 us -> 0 us
  Pallas kernels: 13.5 us -> 29.3 us
  waiting for transfers between devices: 19.1 us -> 6.32 us
  starting transfers between devices: 11.3 us -> 12.9 us
    unnamed x32 -> x0, local copies, waits for them, and re-layouts: 20 us -> none
    pallas_call x4 -> x9, Pallas kernels: 11.3 us -> 27.2 us  [the longest x3 11.6 us: fetched(): pl.pallas_call(functools.partial(fetch, first), out_shape=pltpu.VMEM((sou...]
    ppermute x6 -> x8, waiting for transfers between devices: 10.3 us -> 2.82 us  [the longest x2 2.66 us: shards(): got_ups = [lax.ppermute(ups[k], 'tok', swap(tok, k)) for k in far]]
    ppermute x1, waiting for transfers between devices: 5.09 us -> 0.01 us  [shards(): arrived = [lax.ppermute(here, 'ffn', swap(ffn, k)) for k in range(1, ffn)]]
    ppermute x6 -> x8, starting transfers between devices: 8.91 us -> 10.5 us  [the longest x3 4.45 us: shards(): lax.ppermute(hidden, 'tok', swap(tok, k))]
  transfers between devices with their start and end apart: 11 -> 13, of which waited for: 8 -> 6; matrix products, arithmetic and copies ran while one was open for 0% -> 0% of each run, Pallas kernels for 0% -> 28%
where the time goes in v2:
time: 62.9 us; the launch traced here: 62.7 us
  Pallas kernels  29.3 us (47%)
  blocking collectives  14 us (22%)
  starting transfers between devices  12.9 us (21%)
  waiting for transfers between devices  6.32 us (10%)
    all_to_all x1, blocking collectives, shards(): gathered = lax.all_to_all(attended, ('tok', 'ffn'), 0, 0)  14 us
    pallas_call x3, Pallas kernels, fetched(): pl.pallas_call(functools.partial(fetch, first), out_shape=pltpu.VMEM((sou...  11.6 us
    pallas_call x1, Pallas kernels, shards(): pl.pallas_call(up, out_shape=[like(rows, hidden_here)] * tok, in_specs=[V...  6.08 us
    ppermute x3, starting transfers between devices, shards(): lax.ppermute(hidden, 'tok', swap(tok, k))  4.45 us
    pallas_call x1, Pallas kernels, shards(): pl.pallas_call(functools.partial(down, tok, 2), out_shape=[like(share, fe...  3.17 us
    pallas_call x1, Pallas kernels, shards(): pl.pallas_call(functools.partial(gate, len(arrived)), out_shape=[like(sum...  3.08 us
    pallas_call x1, Pallas kernels, shards(): pl.pallas_call(functools.partial(attend, tok), out_shape=[like(tok * ffn,...  3.03 us
    ppermute x2, waiting for transfers between devices, shards(): got_ups = [lax.ppermute(ups[k], 'tok', swap(tok, k)) for k in far]  2.66 us
  transfers between devices with their start and end apart: 13, of which 6 were waited for; matrix products, arithmetic and copies ran while one was open for 0% of the time, Pallas kernels for 28%

profile of v2, /device:TPU:0, one launch (start us, length us, event | category | flops | bytes accessed | tf_op | source)
XLA Modules:
  0.0 62.7 jit_solution(779282281965383225)
XLA Ops:
  0.0 3.0 %attend.1 = (bf16[8,8,512]{2,1,0:T(8,128)(2,1)S(1)}, bf16[2,512,2048]{2,1,0:T(8,128)(2,1)S(1)}, s32[1,32]{1,0:T(1,128)S(1)}, bf16[32,2048]{1,0:T(8,128)(2,1)S(1)}, f32[1,2048]{1,0:T(1,128)S(1)}) custom-call(s32[4]{0:T(128)} %lens_in.1, bf16[4,2048]{1,0:T(4,128)(2,1)} %queries_in.1, bf16[4,256]{1,0:T(4,128)(2,1)} %new_key_in.1, bf16[4,256]{1,0:T(4,128)(2,1)} %new_value_in.1, ...), custom_call_target="tpu_custom_call" | custom-call | tf_op jit(solution)/shard_map/attend/pallas_call | solution.py:353
  3.0 14.0 %all_to_all.5.heads = bf16[8,8,512]{2,1,0:T(8,128)(2,1)S(1)} all-to-all(bf16[8,8,512]{2,1,0:T(8,128)(2,1)S(1)} %get-tuple-element.28), channel_id=1, replica_groups=mesh['groups'=2,'tok'=4,'ffn'=2,'rep'=2] {'tok','ffn'}, dimensions={0} | all-to-all | bytes 131072 | tf_op jit(solution)/shard_map/all_to_all | solution.py:376
  17.0 1.0 %project.1 = bf16[32,2048]{1,0:T(8,128)(2,1)S(1)} custom-call(s32[1,32]{1,0:T(1,128)S(1)} %get-tuple-element.27.slot_of, bf16[8,8,512]{2,1,0:T(8,128)(2,1)S(1)} %all_to_all.5.heads, bf16[2,512,2048]{2,1,0:T(8,128)(2,1)S(1)} %get-tuple-element.29.weight), custom_call_target="tpu_custom_call" | custom-call | tf_op jit(solution)/shard_map/project/pallas_call | solution.py:378
  18.0 0.0 collective-permute-start
  18.0 1.3 %collective-permute-done = bf16[32,2048]{1,0:T(8,128)(2,1)S(1)} collective-permute-done((bf16[32,2048]{1,0:T(8,128)(2,1)S(1)}, bf16[32,2048]{1,0:T(8,128)(2,1)S(1)}, u32[]{:S(2)}, u32[]{:S(2)}) %collective-permute-start) | collective-permute-done | bytes 131104 | tf_op jit(solution)/shard_map/ppermute | solution.py:388
  19.4 0.5 collective-permute-start.1
  19.8 0.1 pad_add_fusion.refs_0_.place
  19.9 5.3 %fetch.3.refs_5_ = bf16[2048,3584]{1,0:T(8,128)(2,1)S(1)} custom-call(bf16[2048,3584]{1,0:T(8,128)(2,1)} %source.3, bf16[32,2048]{1,0:T(8,128)(2,1)S(1)} %add.7.refs_0_.refs_3_), custom_call_target="tpu_custom_call" | custom-call | tf_op jit(solution)/shard_map/fetch/pallas_call | solution.py:308
  25.2 0.0 collective-permute-done.1.refs_4_
  25.2 3.1 %gate.1 = (bf16[4,8,2048]{2,1,0:T(8,128)(2,1)S(1)}, bf16[32,2048]{1,0:T(8,128)(2,1)S(1)}, bf16[2,8,128]{2,1,0:T(8,128)(2,1)S(1)}, bf16[8,3584]{1,0:T(8,128)(2,1)...) custom-call(s32[2]{0:T(128)S(1)} %pad_add_fusion.refs_0_.place, ...), custom_call_target="tpu_custom_call" | custom-call | tf_op jit(solution)/shard_map/gate/pallas_call | solution.py:396
  28.3 1.1 %collective-permute-start.2 = (bf16[8,3712]{1,0:T(8,128)(2,1)S(1)}, bf16[8,3712]{1,0:T(8,128)(2,1)S(1)}, u32[]{:S(2)}, u32[]{:S(2)}) collective-permute-start(bf16[8,3712]{1,0:T(8,128)(2,1)S(1)} %get-tuple-element.37), channel_id=1, source_target_pairs={{0,12},{4,8},{8,4},{12,0},{1,13},{5,9},{9,5},{13,1},{2,14},{6,10},... | collective-permute-start | bytes 178184 | tf_op jit(solution)/shard_map/ppermute | solution.py:410
  29.4 1.3 %collective-permute-start.3 = (bf16[8,3712]{1,0:T(8,128)(2,1)S(1)}, bf16[8,3712]{1,0:T(8,128)(2,1)S(1)}, u32[]{:S(2)}, u32[]{:S(2)}) collective-permute-start(bf16[8,3712]{1,0:T(8,128)(2,1)S(1)} %get-tuple-element.38), channel_id=1, source_target_pairs={{0,8},{4,12},{8,0},{12,4},{1,9},{5,13},{9,1},{13,5},{2,10},{6,14},... | collective-permute-start | bytes 178184 | tf_op jit(solution)/shard_map/ppermute | solution.py:410
  30.7 6.1 %up.1 = (bf16[8,3584]{1,0:T(8,128)(2,1)S(1)}, bf16[8,3584]{1,0:T(8,128)(2,1)S(1)}, bf16[8,3584]{1,0:T(8,128)(2,1)S(1)}, bf16[8,3584]{1,0:T(8,128)(2,1)S(1)}) custom-call(bf16[32,2048]{1,0:T(8,128)(2,1)S(1)} %get-tuple-element.31.left, bf16[2048,3584]{1,0:T(8,128)(2,1)} %weight.1), custom_call_target="tpu_custom_call" | custom-call | bytes 29360128 | tf_op jit(solution)/shard_map/up/pallas_call | solution.py:411
  36.8 0.0 collective-permute-done.2.refs_0_.refs_6_
  36.8 0.0 collective-permute-done.3.refs_1_.refs_7_
  36.8 2.2 %collective-permute-start.4 = (bf16[8,7296]{1,0:T(8,128)(2,1)S(1)}, bf16[8,7296]{1,0:T(8,128)(2,1)S(1)}, u32[]{:S(2)}, u32[]{:S(2)}) collective-permute-start(bf16[8,7296]{1,0:T(8,128)(2,1)S(1)} %join.1), channel_id=1, source_target_pairs={{0,4},{4,0},{8,12},{12,8},{1,5},{5,1},{9,13},{13,9},{2,6},{6,2},{1... | collective-permute-start | bytes 350216 | tf_op jit(solution)/shard_map/ppermute | solution.py:437
  39.0 1.0 %collective-permute-start.5 = (bf16[8,3584]{1,0:T(8,128)(2,1)S(1)}, bf16[8,3584]{1,0:T(8,128)(2,1)S(1)}, u32[]{:S(2)}, u32[]{:S(2)}) collective-permute-start(bf16[8,3584]{1,0:T(8,128)(2,1)S(1)} %get-tuple-element.39), channel_id=1, source_target_pairs={{0,12},{4,8},{8,4},{12,0},{1,13},{5,9},{9,5},{13,1},{2,14},{6,10},... | collective-permute-start | bytes 172040 | tf_op jit(solution)/shard_map/ppermute | solution.py:426
  40.0 0.5 collective-permute-start.6
  40.5 3.2 %fetch.4.refs_8_.refs_5_ = bf16[3584,1024]{1,0:T(8,128)(2,1)S(1)} custom-call(bf16[3584,2048]{1,0:T(8,128)(2,1)} %source.5, bf16[8,3584]{1,0:T(8,128)(2,1)S(1)} %get-tuple-element.32.refs_0_), custom_call_target="tpu_custom_call" | custom-call | tf_op jit(solution)/shard_map/fetch/pallas_call | solution.py:308
  43.7 1.3 %collective-permute-done.5.refs_4_ = bf16[8,3584]{1,0:T(8,128)(2,1)S(1)} collective-permute-done((bf16[8,3584]{1,0:T(8,128)(2,1)S(1)}, bf16[8,3584]{1,0:T(8,128)(2,1)S(1)}, u32[]{:S(2)}, u32[]{:S(2)}) %collective-permute-start.5) | collective-permute-done | bytes 57376 | tf_op jit(solution)/shard_map/ppermute | solution.py:426
  44.9 1.4 %collective-permute-done.6.refs_5_ = bf16[8,3584]{1,0:T(8,128)(2,1)S(1)} collective-permute-done((bf16[8,3584]{1,0:T(8,128)(2,1)S(1)}, bf16[8,3584]{1,0:T(8,128)(2,1)S(1)}, u32[]{:S(2)}, u32[]{:S(2)}) %collective-permute-start.6) | collective-permute-done | bytes 57376 | tf_op jit(solution)/shard_map/ppermute | solution.py:426
  46.3 0.0 collective-permute-done.4.refs_3_
  46.3 0.2 activate.1.refs_0_.refs_1_
  46.5 2.0 %collective-permute-start.9 = (bf16[8,3584]{1,0:T(8,128)(2,1)S(1)}, bf16[8,3584]{1,0:T(8,128)(2,1)S(1)}, u32[]{:S(2)}, u32[]{:S(2)}) collective-permute-start(bf16[8,3584]{1,0:T(8,128)(2,1)S(1)} %activate.1.refs_0_.refs_1_), channel_id=1, source_target_pairs={{0,12},{4,8},{8,4},{12,0},{1,13},{5,9},{9,5},{13,1},{2,14},{6,10},... | collective-permute-start | bytes 172040 | tf_op jit(solution)/shard_map/ppermute | solution.py:449
  48.5 0.0 collective-permute-start.8
  48.5 2.5 %collective-permute-start.7 = (bf16[8,3584]{1,0:T(8,128)(2,1)S(1)}, bf16[8,3584]{1,0:T(8,128)(2,1)S(1)}, u32[]{:S(2)}, u32[]{:S(2)}) collective-permute-start(bf16[8,3584]{1,0:T(8,128)(2,1)S(1)} %activate.1.refs_0_.refs_1_), channel_id=1, source_target_pairs={{0,4},{4,0},{8,12},{12,8},{1,5},{5,1},{9,13},{13,9},{2,6},{6,2},{1... | collective-permute-start | bytes 172040 | tf_op jit(solution)/shard_map/ppermute | solution.py:449
  51.0 3.2 %fetch.5.refs_6_ = bf16[3584,1024]{1,0:T(8,128)(2,1)S(1)} custom-call(bf16[3584,2048]{1,0:T(8,128)(2,1)} %source.5, bf16[8,3584]{1,0:T(8,128)(2,1)S(1)} %activate.1.refs_0_.refs_1_), custom_call_target="tpu_custom_call" | custom-call | tf_op jit(solution)/shard_map/fetch/pallas_call | solution.py:308
  54.1 0.0 collective-permute-done.9.refs_4_
  54.2 0.1 collective-permute-done.8.refs_3_
  54.3 0.0 collective-permute-done.7.refs_2_
  54.3 3.2 %down.1 = (bf16[8,2048]{1,0:T(8,128)(2,1)S(1)}, bf16[8,2048]{1,0:T(8,128)(2,1)S(1)}, bf16[8,2048]{1,0:T(8,128)(2,1)S(1)}, bf16[8,2048]{1,0:T(8,128)(2,1)S(1)}) custom-call(s32[2]{0:T(128)S(1)} %pad_add_fusion.refs_0_.place, bf16[8,3584]{1,0:T(8,128)(2,1)S(1)} %activate.1.refs_0_.refs_1_, bf16[8,3584]{1,0:T(8,128)(2,1)S(1)} %collective-permute-done.7.refs_2_, ...), custom_call_target="tpu_custom_call" | custom-call | tf_op jit(solution)/shard_map/down/pallas_call | solution.py:452
  57.5 0.0 collective-permute-start.10
  57.5 1.3 %collective-permute-start.11 = (bf16[8,2048]{1,0:T(8,128)(2,1)S(1)}, bf16[8,2048]{1,0:T(8,128)(2,1)S(1)}, u32[]{:S(2)}, u32[]{:S(2)}) collective-permute-start(bf16[8,2048]{1,0:T(8,128)(2,1)S(1)} %get-tuple-element.43), channel_id=1, source_target_pairs={{0,2},{1,3},{2,0},{3,1},{4,6},{5,7},{6,4},{7,5},{8,10},{9,11},{10,... | collective-permute-start | bytes 98312 | tf_op jit(solution)/shard_map/ppermute | solution.py:462
  58.8 0.6 collective-permute-start.12
  59.4 1.6 %collective-permute-done.10.refs_1_ = bf16[8,2048]{1,0:T(8,128)(2,1)S(1)} collective-permute-done((bf16[8,2048]{1,0:T(8,128)(2,1)S(1)}, bf16[8,2048]{1,0:T(8,128)(2,1)S(1)}, u32[]{:S(2)}, u32[]{:S(2)}) %collective-permute-start.10) | collective-permute-done | bytes 32800 | tf_op jit(solution)/shard_map/ppermute | solution.py:462
  61.0 0.5 collective-permute-done.11.refs_2_
  61.5 0.0 collective-permute-done.12.refs_3_
  61.5 1.2 %finish.1 = bf16[8,2048]{1,0:T(8,128)(2,1)} custom-call(s32[2]{0:T(128)S(1)} %pad_add_fusion.refs_0_.place, bf16[4,8,2048]{2,1,0:T(8,128)(2,1)S(1)} %get-tuple-element.30.mid, bf16[8,2048]{1,0:T(8,128)(2,1)S(1)} %get-tuple-element.41.refs_0_, bf16[8,2048]{1,0:T(8,128)(2,1)S(1)} %collective-permute-done.10.refs_1_, ...), custom_call_target="tpu_custom_call" | custom-call | tf_op jit(solution)/shard_map/finish/pallas_call | solution.py:464
  (2 shorter events, 0.0 us)
Async XLA Ops:
  18.0 1.4 %collective-permute-start = (bf16[32,2048]{1,0:T(8,128)(2,1)S(1)}, bf16[32,2048]{1,0:T(8,128)(2,1)S(1)}, u32[]{:S(2)}, u32[]{:S(2)}) collective-permute-start(bf16[32,2048]{1,0:T(8,128)(2,1)S(1)} %project.1), channel_id=1, source_target_pairs={{0,1},{1,0},{2,3},{3,2},{4,5},{5,4},{6,7},{7,6},{8,9},{9,8},{10,11... | collective-permute-start | bytes 393224 | tf_op jit(solution)/shard_map/ppermute | solution.py:388
  19.4 5.8 %collective-permute-start.1 = (bf16[32,2048]{1,0:T(8,128)(2,1)S(1)}, bf16[32,2048]{1,0:T(8,128)(2,1)S(1)}, u32[]{:S(2)}, u32[]{:S(2)}) collective-permute-start(bf16[32,2048]{1,0:T(8,128)(2,1)S(1)} %add.7.refs_0_.refs_3_), channel_id=1, source_target_pairs={{0,2},{2,0},{1,3},{3,1},{4,6},{6,4},{5,7},{7,5},{8,10},{10,8},{9,1... | collective-permute-start | bytes 393224 | tf_op jit(solution)/shard_map/ppermute | solution.py:389
  28.3 8.4 %collective-permute-start.2 = (bf16[8,3712]{1,0:T(8,128)(2,1)S(1)}, bf16[8,3712]{1,0:T(8,128)(2,1)S(1)}, u32[]{:S(2)}, u32[]{:S(2)}) collective-permute-start(bf16[8,3712]{1,0:T(8,128)(2,1)S(1)} %get-tuple-element.37), channel_id=1, source_target_pairs={{0,12},{4,8},{8,4},{12,0},{1,13},{5,9},{9,5},{13,1},{2,14},{6,10},... | collective-permute-start | bytes 178184 | tf_op jit(solution)/shard_map/ppermute | solution.py:410
  29.4 7.4 %collective-permute-start.3 = (bf16[8,3712]{1,0:T(8,128)(2,1)S(1)}, bf16[8,3712]{1,0:T(8,128)(2,1)S(1)}, u32[]{:S(2)}, u32[]{:S(2)}) collective-permute-start(bf16[8,3712]{1,0:T(8,128)(2,1)S(1)} %get-tuple-element.38), channel_id=1, source_target_pairs={{0,8},{4,12},{8,0},{12,4},{1,9},{5,13},{9,1},{13,5},{2,10},{6,14},... | collective-permute-start | bytes 178184 | tf_op jit(solution)/shard_map/ppermute | solution.py:410
  36.8 9.5 %collective-permute-start.4 = (bf16[8,7296]{1,0:T(8,128)(2,1)S(1)}, bf16[8,7296]{1,0:T(8,128)(2,1)S(1)}, u32[]{:S(2)}, u32[]{:S(2)}) collective-permute-start(bf16[8,7296]{1,0:T(8,128)(2,1)S(1)} %join.1), channel_id=1, source_target_pairs={{0,4},{4,0},{8,12},{12,8},{1,5},{5,1},{9,13},{13,9},{2,6},{6,2},{1... | collective-permute-start | bytes 350216 | tf_op jit(solution)/shard_map/ppermute | solution.py:437
  39.0 6.0 %collective-permute-start.5 = (bf16[8,3584]{1,0:T(8,128)(2,1)S(1)}, bf16[8,3584]{1,0:T(8,128)(2,1)S(1)}, u32[]{:S(2)}, u32[]{:S(2)}) collective-permute-start(bf16[8,3584]{1,0:T(8,128)(2,1)S(1)} %get-tuple-element.39), channel_id=1, source_target_pairs={{0,12},{4,8},{8,4},{12,0},{1,13},{5,9},{9,5},{13,1},{2,14},{6,10},... | collective-permute-start | bytes 172040 | tf_op jit(solution)/shard_map/ppermute | solution.py:426
  40.0 6.4 %collective-permute-start.6 = (bf16[8,3584]{1,0:T(8,128)(2,1)S(1)}, bf16[8,3584]{1,0:T(8,128)(2,1)S(1)}, u32[]{:S(2)}, u32[]{:S(2)}) collective-permute-start(bf16[8,3584]{1,0:T(8,128)(2,1)S(1)} %get-tuple-element.40), channel_id=1, source_target_pairs={{0,8},{4,12},{8,0},{12,4},{1,9},{5,13},{9,1},{13,5},{2,10},{6,14},... | collective-permute-start | bytes 172040 | tf_op jit(solution)/shard_map/ppermute | solution.py:426
  46.5 7.6 %collective-permute-start.9 = (bf16[8,3584]{1,0:T(8,128)(2,1)S(1)}, bf16[8,3584]{1,0:T(8,128)(2,1)S(1)}, u32[]{:S(2)}, u32[]{:S(2)}) collective-permute-start(bf16[8,3584]{1,0:T(8,128)(2,1)S(1)} %activate.1.refs_0_.refs_1_), channel_id=1, source_target_pairs={{0,12},{4,8},{8,4},{12,0},{1,13},{5,9},{9,5},{13,1},{2,14},{6,10},... | collective-permute-start | bytes 172040 | tf_op jit(solution)/shard_map/ppermute | solution.py:449
  48.5 5.8 %collective-permute-start.8 = (bf16[8,3584]{1,0:T(8,128)(2,1)S(1)}, bf16[8,3584]{1,0:T(8,128)(2,1)S(1)}, u32[]{:S(2)}, u32[]{:S(2)}) collective-permute-start(bf16[8,3584]{1,0:T(8,128)(2,1)S(1)} %activate.1.refs_0_.refs_1_), channel_id=1, source_target_pairs={{0,8},{4,12},{8,0},{12,4},{1,9},{5,13},{9,1},{13,5},{2,10},{6,14},... | collective-permute-start | bytes 172040 | tf_op jit(solution)/shard_map/ppermute | solution.py:449
  48.5 5.8 %collective-permute-start.7 = (bf16[8,3584]{1,0:T(8,128)(2,1)S(1)}, bf16[8,3584]{1,0:T(8,128)(2,1)S(1)}, u32[]{:S(2)}, u32[]{:S(2)}) collective-permute-start(bf16[8,3584]{1,0:T(8,128)(2,1)S(1)} %activate.1.refs_0_.refs_1_), channel_id=1, source_target_pairs={{0,4},{4,0},{8,12},{12,8},{1,5},{5,1},{9,13},{13,9},{2,6},{6,2},{1... | collective-permute-start | bytes 172040 | tf_op jit(solution)/shard_map/ppermute | solution.py:449
  57.5 3.5 %collective-permute-start.10 = (bf16[8,2048]{1,0:T(8,128)(2,1)S(1)}, bf16[8,2048]{1,0:T(8,128)(2,1)S(1)}, u32[]{:S(2)}, u32[]{:S(2)}) collective-permute-start(bf16[8,2048]{1,0:T(8,128)(2,1)S(1)} %get-tuple-element.42), channel_id=1, source_target_pairs={{0,3},{1,2},{2,1},{3,0},{4,7},{5,6},{6,5},{7,4},{8,11},{9,10},{10,... | collective-permute-start | bytes 98312 | tf_op jit(solution)/shard_map/ppermute | solution.py:462
  57.5 4.0 %collective-permute-start.11 = (bf16[8,2048]{1,0:T(8,128)(2,1)S(1)}, bf16[8,2048]{1,0:T(8,128)(2,1)S(1)}, u32[]{:S(2)}, u32[]{:S(2)}) collective-permute-start(bf16[8,2048]{1,0:T(8,128)(2,1)S(1)} %get-tuple-element.43), channel_id=1, source_target_pairs={{0,2},{1,3},{2,0},{3,1},{4,6},{5,7},{6,4},{7,5},{8,10},{9,11},{10,... | collective-permute-start | bytes 98312 | tf_op jit(solution)/shard_map/ppermute | solution.py:462
  58.8 2.7 %collective-permute-start.12 = (bf16[8,2048]{1,0:T(8,128)(2,1)S(1)}, bf16[8,2048]{1,0:T(8,128)(2,1)S(1)}, u32[]{:S(2)}, u32[]{:S(2)}) collective-permute-start(bf16[8,2048]{1,0:T(8,128)(2,1)S(1)} %get-tuple-element.44), channel_id=1, source_target_pairs={{0,1},{1,0},{2,3},{3,2},{4,5},{5,4},{6,7},{7,6},{8,9},{9,8},{10,11... | collective-permute-start | bytes 98312 | tf_op jit(solution)/shard_map/ppermute | solution.py:462

commit v3 on v2

--- a/solution.py
+++ b/solution.py
@@ -28,12 +28,11 @@
     return width
 
 
-def attend(
-    copies, lens_in, queries_in, new_key_in, new_value_in, keys, values, *refs
-):
-    count = (len(refs) - 8) // 2
-    carried_in, out, carried_out = refs[:count], refs[count], refs[count + 1 : 2 * count + 1]
-    lens, queries, new_key, new_value, key_buf, value_buf, sems = refs[2 * count + 1 :]
+def attend(peers, lens_in, queries_in, new_key_in, new_value_in, keys, values, *refs):
+    count = (len(refs) - 8 - peers) // 2
+    carried_in, outs = refs[:count], refs[count : count + peers]
+    carried_out = refs[count + peers : 2 * count + peers]
+    lens, queries, new_key, new_value, key_buf, value_buf, shares, sems = refs[-8:]
     slots, span, width = key_buf.shape
     kv_here = width // HEAD_DIM
     group = queries.shape[1] // width
@@ -104,11 +103,9 @@
                 value_buf[s, :, g * HEAD_DIM : (g + 1) * HEAD_DIM],
                 preferred_element_type=F32,
             )
-    width_out = out.shape[2]
-    heads_out = width_out // HEAD_DIM
-    parts = group // heads_out
-    for f in range(parts):
-        block = jnp.concatenate(
+    heads_out = group // peers
+    for f in range(peers):
+        shares[f] = jnp.concatenate(
             [
                 jnp.concatenate(
                     [totals[g][h * slots : (h + 1) * slots] for g in range(kv_here)], axis=0
@@ -116,35 +113,38 @@
                 for h in range(f * heads_out, (f + 1) * heads_out)
             ],
             axis=1,
-        ).astype(BF16)
-        for t in range(copies):
-            out[t * parts + f] = block
+        )
+    mine = lax.axis_index("ffn")
+    for f in range(peers):
+        outs[f][...] = shares[mine ^ f].astype(BF16)
     for load in loads[2 * slots :]:
         load.wait()
 
 
-def fetch(first, source, *refs):
-    out, sems = refs[-2:]
-    rows = out.shape[0] // sems.shape[0]
-    loads = []
-    for i in range(sems.shape[0]):
-        at = pl.ds(i * rows, rows)
-        columns = pl.ds(first, out.shape[1])
-        loads.append(pltpu.make_async_copy(source.at[at, columns], out.at[at], sems.at[i]))
-    for load in loads:
-        load.start()
-    for load in loads:
-        load.wait()
-
-
-def project(slots, slot_of, heads, weight, out):
+def stack(count, *refs):
+    out = refs[-1]
+    for i, ref in enumerate(refs[:count]):
+        out[i] = ref[...]
+
+
+def add(count, *refs):
+    total = refs[0][...].astype(F32)
+    for ref in refs[1:count]:
+        total += ref[...].astype(F32)
+    refs[-1][...] = total.astype(BF16)
+
+
+def project(slots, slot_of, weight, *refs):
+    refs, out = refs[:-1], refs[-1]
     requests = slot_of.shape[1]
-    blocks, rows, width = heads.shape
+    _, rows, width = refs[0].shape
     kv_here = weight.shape[0]
-    table = heads[...].astype(F32).reshape(blocks * rows, width).astype(BF16)
+    table = [ref[...].astype(F32).reshape(ref.shape[0] * rows, width) for ref in refs]
+    table = jnp.concatenate(table, axis=0).astype(BF16)
     slot = slot_of[...]
-    where_from = (slot // slots) * rows + lax.rem(slot, slots)
-    row = lax.broadcasted_iota(jnp.int32, (blocks * rows, requests), 0)
+    mine = lax.axis_index(("tok", "ffn"))
+    where_from = ((slot // slots) ^ mine) * rows + lax.rem(slot, slots)
+    row = lax.broadcasted_iota(jnp.int32, (table.shape[0], requests), 0)
     ordered = []
     for g in range(kv_here):
         pick = (row == where_from + g * slots).astype(F32).astype(BF16)
@@ -164,10 +164,10 @@
 
 
 def gate(others, *refs):
-    place, residual, gain, here = refs[:4]
-    arrived = refs[4 : 4 + others]
-    weight, mid_out, left_out, stat_out = refs[4 + others : 8 + others]
-    parts = refs[8 + others : -2]
+    residual, gain, here = refs[:3]
+    arrived = refs[3 : 3 + others]
+    weight, mid_out, left_out, stat_out = refs[3 + others : 7 + others]
+    parts = refs[7 + others : -2]
     ordered, squares = refs[-2:]
     blocks, rows, _ = ordered.shape
     width = weight.shape[1]
@@ -183,7 +183,7 @@
     for k in range(blocks):
         ordered[k] = scaled[k * rows : (k + 1) * rows]
         squares[k] = square[k * rows : (k + 1) * rows]
-    mine = place[0]
+    mine = lax.axis_index("tok")
     left = jnp.concatenate([ordered[mine ^ k] for k in range(blocks)], axis=0).astype(BF16)
     left_out[...] = left
     lane = lax.broadcasted_iota(jnp.int32, (rows, 128), 1)
@@ -205,23 +205,20 @@
             parts[k][:, c : c + step] = total[k * rows : (k + 1) * rows].astype(BF16)
 
 
-def up(left, weight, *refs):
-    parts = refs[:-2]
-    buf, sems = refs[-2:]
-    rows, width = parts[0].shape
-    step = column_step(width)
-    loads = []
-    for i, c in enumerate(range(0, width, step)):
-        at = pl.ds(c, step)
-        loads.append(pltpu.make_async_copy(weight.at[:, at], buf.at[:, at], sems.at[i]))
-    for load in loads:
-        load.start()
+def up(pieces, left, *refs):
+    weights, parts = refs[:pieces], refs[pieces:]
+    rows = parts[0].shape[0]
     rhs = left[...]
-    for i, c in enumerate(range(0, width, step)):
-        loads[i].wait()
-        total = jnp.dot(rhs, buf[:, c : c + step], preferred_element_type=F32)
-        for k, part in enumerate(parts):
-            part[:, c : c + step] = total[k * rows : (k + 1) * rows].astype(BF16)
+    base = 0
+    for weight in weights:
+        width = weight.shape[1]
+        step = column_step(width)
+        for c in range(0, width, step):
+            total = jnp.dot(rhs, weight[:, c : c + step], preferred_element_type=F32)
+            at = base + c
+            for k, part in enumerate(parts):
+                part[:, at : at + step] = total[k * rows : (k + 1) * rows].astype(BF16)
+        base += width
 
 
 def join(up_part, gate_part, stat, *refs):
@@ -258,19 +255,19 @@
 
 
 def down(blocks, pieces, *refs):
-    place = refs[0]
-    parts = refs[1 : 1 + blocks]
-    weights = refs[1 + blocks : 1 + blocks + pieces]
-    outs = refs[1 + blocks + pieces : -1]
+    parts = refs[:blocks]
+    weights = refs[blocks : blocks + pieces]
+    outs = refs[blocks + pieces : -1]
     ordered = refs[-1]
+    mine, group = lax.axis_index("tok"), lax.axis_index(("ffn", "rep"))
     rows = parts[0].shape[0]
     share = outs[0].shape[0]
     for k in range(blocks):
-        at = pl.multiple_of((place[0] ^ k) * rows, 8)
+        at = pl.multiple_of((mine ^ k) * rows, 8)
         ordered[pl.ds(at, rows)] = parts[k][...].astype(F32)
     left = jnp.concatenate(
         [
-            ordered[pl.ds(pl.multiple_of((place[1] ^ j) * share, 8), share)]
+            ordered[pl.ds(pl.multiple_of((group ^ j) * share, 8), share)]
             for j in range(len(outs))
         ],
         axis=0,
@@ -287,9 +284,9 @@
         base += width
 
 
-def finish(place, mid, *refs):
+def finish(mid, *refs):
     out = refs[-1]
-    total = mid[place[1]].astype(F32)
+    total = mid[lax.axis_index(("ffn", "rep"))].astype(F32)
     for part in refs[:-1]:
         total += part[...].astype(F32)
     out[...] = total.astype(BF16)
@@ -301,22 +298,6 @@
 
 def limit(mib):
     return pltpu.CompilerParams(vmem_limit_bytes=mib * MIB)
-
-
-def fetched(source, after, first=0, width=None):
-    width = width or source.shape[1]
-    return pl.pallas_call(
-        functools.partial(fetch, first),
-        out_shape=pltpu.VMEM((source.shape[0], width), source.dtype),
-        in_specs=[HBM, HBM],
-        out_specs=VMEM,
-        scratch_shapes=[pltpu.SemaphoreType.DMA((8,))],
-        compiler_params=limit(1),
-        cost_estimate=pl.CostEstimate(
-            flops=0, transcendentals=0, bytes_accessed=0
-        ),
-        name="fetch",
-    )(pltpu.with_memory_space_constraint(source, pltpu.HBM), after)
 
 
 def shards(
@@ -341,7 +322,6 @@
     requests, features = residual_in.shape
     hidden_here = gate_weight.shape[1]
     feat_width = out_weight.shape[1]
-    place = jnp.stack([lax.axis_index("tok"), lax.axis_index(("ffn", "rep"))]).astype(jnp.int32)
     in_hbm = functools.partial(pltpu.with_memory_space_constraint, memory_space=pltpu.HBM)
 
     carried = [
@@ -350,12 +330,13 @@
         residual_in,
         norm_gain.reshape(1, features),
     ]
-    attended, out_weight, slot_of, residual_in, norm_gain = pl.pallas_call(
-        functools.partial(attend, tok),
-        out_shape=[like(tok * ffn, slots * kv_here, feat_width)]
+    table_rows = slots * kv_here
+    *attended, out_weight, slot_of, residual_in, norm_gain = pl.pallas_call(
+        functools.partial(attend, ffn),
+        out_shape=[like(table_rows, feat_width)] * ffn
         + [pltpu.VMEM(a.shape, a.dtype) for a in carried],
         in_specs=[HBM] * (6 + len(carried)),
-        out_specs=[VMEM] * (1 + len(carried)),
+        out_specs=[VMEM] * (ffn + len(carried)),
         scratch_shapes=[
             pltpu.SMEM(lengths.shape, jnp.int32),
             pltpu.VMEM(queries.shape, BF16),
@@ -363,9 +344,11 @@
             pltpu.VMEM(new_value.shape, BF16),
             pltpu.VMEM(key_cache.shape, BF16),
             pltpu.VMEM(value_cache.shape, BF16),
+            pltpu.VMEM((ffn, table_rows, feat_width), F32),
             pltpu.SemaphoreType.DMA((4 + 2 * slots + len(carried),)),
         ],
         compiler_params=limit(8),
+        cost_estimate=pl.CostEstimate(flops=20000000000, transcendentals=0, bytes_accessed=0),
         name="attend",
     )(
         *(
@@ -373,31 +356,53 @@
             for a in [lengths, queries, new_key, new_value, key_cache, value_cache] + carried
         )
     )
-    gathered = lax.all_to_all(attended, ("tok", "ffn"), 0, 0)
+    owners = tok * ffn
+    near = min(2, tok)
+    close = [attended[0]] + [None] * (near * ffn - 1)
+    for k in sorted(range(1, near * ffn), reverse=True):
+        close[k] = lax.ppermute(attended[k % ffn], ("tok", "ffn"), swap(owners, k))
+    in_vmem = functools.partial(pltpu.with_memory_space_constraint, memory_space=pltpu.VMEM)
+    up_pieces = [in_vmem(up_weight)]
+    close = pl.pallas_call(
+        functools.partial(stack, near * ffn),
+        out_shape=like(near * ffn, table_rows, feat_width),
+        in_specs=[VMEM] * (near * ffn),
+        out_specs=VMEM,
+        compiler_params=limit(4),
+        name="stack",
+    )(*close)
+    gathered = [close] + [
+        lax.ppermute(close, "tok", swap(tok, k)) for k in range(near, tok, near)
+    ]
 
     partial = pl.pallas_call(
         functools.partial(project, slots),
         out_shape=like(requests, features),
-        in_specs=[VMEM, VMEM, VMEM],
+        in_specs=[VMEM] * (2 + len(gathered)),
         out_specs=VMEM,
         compiler_params=limit(8),
         name="project",
-    )(slot_of, gathered, out_weight)
-    here = partial
-    for k in range(1, rep):
-        here = here + lax.ppermute(partial, "rep", swap(rep, k))
+    )(slot_of, out_weight, *gathered)
+    summed = [partial] + [lax.ppermute(partial, "rep", swap(rep, k)) for k in range(1, rep)]
+    here = pl.pallas_call(
+        functools.partial(add, len(summed)),
+        out_shape=like(requests, features),
+        in_specs=[VMEM] * len(summed),
+        out_specs=VMEM,
+        compiler_params=limit(4),
+        name="add",
+    )(*summed)
     arrived = [lax.ppermute(here, "ffn", swap(ffn, k)) for k in range(1, ffn)]
-    gate_weight = fetched(gate_weight, here)
+    gate_weight = in_vmem(gate_weight)
 
     rows = requests // tok
     share = requests // sums
-    near = min(2, tok)
     both_width = 2 * hidden_here + 128
     mid, left, stat, *gates = pl.pallas_call(
         functools.partial(gate, len(arrived)),
         out_shape=[like(sums, share, features), like(requests, features), like(near, rows, 128)]
         + [like(rows, hidden_here + (128 if k >= near else 0)) for k in range(tok)],
-        in_specs=[SMEM] + [VMEM] * (4 + len(arrived)),
+        in_specs=[VMEM] * (4 + len(arrived)),
         out_specs=[VMEM] * (3 + tok),
         scratch_shapes=[
             pltpu.VMEM((tok, rows, features), F32),
@@ -405,24 +410,20 @@
         ],
         compiler_params=limit(8),
         name="gate",
-    )(place, residual_in, norm_gain, here, *arrived, gate_weight)
+    )(residual_in, norm_gain, here, *arrived, gate_weight)
     far = sorted(range(near, tok), reverse=True)
     got_gates = [lax.ppermute(gates[k], "tok", swap(tok, k)) for k in far]
     ups = pl.pallas_call(
-        up,
+        functools.partial(up, len(up_pieces)),
         out_shape=[like(rows, hidden_here)] * tok,
-        in_specs=[VMEM, HBM],
+        in_specs=[VMEM] * (1 + len(up_pieces)),
         out_specs=[VMEM] * tok,
-        scratch_shapes=[
-            pltpu.VMEM(up_weight.shape, BF16),
-            pltpu.SemaphoreType.DMA((hidden_here // column_step(hidden_here),)),
-        ],
-        compiler_params=limit(20),
+        compiler_params=limit(8),
         cost_estimate=pl.CostEstimate(
             flops=0, transcendentals=0, bytes_accessed=4 * up_weight.size
         ),
         name="up",
-    )(left, in_hbm(up_weight))
+    )(left, *up_pieces)
     got_ups = [lax.ppermute(ups[k], "tok", swap(tok, k)) for k in far]
     got_both = []
     if near > 1:
@@ -435,40 +436,37 @@
             name="join",
         )(ups[1], gates[1], stat, *got_gates)
         got_both.append(lax.ppermute(both, "tok", swap(tok, 1)))
-    half = features // 2
-    down_left = fetched(down_weight, ups[0], 0, half)
 
     hidden = pl.pallas_call(
         functools.partial(activate, features * tok, near),
         out_shape=like(rows, hidden_here),
-        in_specs=[VMEM] * (2 + near + 2 * len(far)) + [ANY],
+        in_specs=[VMEM] * (2 + near + 2 * len(far)),
         out_specs=VMEM,
         compiler_params=limit(8),
         name="activate",
-    )(ups[0], gates[0], stat, *got_both, *got_ups, *got_gates, down_left)
+    )(ups[0], gates[0], stat, *got_both, *got_ups, *got_gates)
     pieces = {k: lax.ppermute(hidden, "tok", swap(tok, k)) for k in sorted(range(1, tok), reverse=True)}
-    down_right = fetched(down_weight, hidden, half, half)
 
     downs = pl.pallas_call(
-        functools.partial(down, tok, 2),
+        functools.partial(down, tok, 1),
         out_shape=[like(share, features)] * sums,
-        in_specs=[SMEM] + [VMEM] * (2 + tok),
+        in_specs=[VMEM] * (1 + tok),
         out_specs=[VMEM] * sums,
         scratch_shapes=[pltpu.VMEM((requests, hidden_here), F32)],
         compiler_params=limit(8),
         name="down",
-    )(place, hidden, *[pieces[k] for k in range(1, tok)], down_left, down_right)
+    )(hidden, *[pieces[k] for k in range(1, tok)], in_vmem(down_weight))
     order = sorted(range(1, sums), reverse=True)
     got = [downs[0]] + [lax.ppermute(downs[j], ("ffn", "rep"), swap(sums, j)) for j in order]
 
     return pl.pallas_call(
         finish,
         out_shape=like(share, features),
-        in_specs=[SMEM] + [VMEM] * (1 + sums),
+        in_specs=[VMEM] * (1 + sums),
         out_specs=VMEM,
         compiler_params=limit(8),
         name="finish",
-    )(place, mid, *got)
+    )(mid, *got)
 
 
 def solution(mesh):

time: 62.9 us -> 58.9 us (0.936)
  waiting for transfers between devices: 6.32 us -> 23.7 us
  Pallas kernels: 29.3 us -> 12.6 us
  blocking collectives: 14 us -> 0 us
  starting transfers between devices: 12.9 us -> 22.1 us
    pallas_call x7 -> x6, Pallas kernels: 25.1 us -> 8.89 us  [the longest x1 3.13 us: shards(): pl.pallas_call(functools.partial(attend, ffn), out_shape=[like(table_rows...]
    all_to_all x1 -> x0, blocking collectives: 14 us -> none  [shards(): gathered = lax.all_to_all(attended, ('tok', 'ffn'), 0, 0)]
    ppermute x1 -> x5, starting transfers between devices: 0.02 us -> 7.26 us  [the longest x3 4.65 us: shards(): close[k] = lax.ppermute(attended[k % ffn], ('tok', 'ffn'), swap(owners, k))]
    ppermute x1 -> x5, waiting for transfers between devices: 1.33 us -> 7.04 us  [the longest x3 3.49 us: shards(): close[k] = lax.ppermute(attended[k % ffn], ('tok', 'ffn'), swap(owners, k))]
    ppermute x1, waiting for transfers between devices: 0.01 us -> 4.53 us  [shards(): arrived = [lax.ppermute(here, 'ffn', swap(ffn, k)) for k in range(1, ffn)]]
    ppermute x3, waiting for transfers between devices: 0.15 us -> 2.82 us  [shards(): lax.ppermute(hidden, 'tok', swap(tok, k))]
    ppermute x2, waiting for transfers between devices: 0.01 us -> 2.58 us  [shards(): got_gates = [lax.ppermute(gates[k], 'tok', swap(tok, k)) for k in far]]
    ppermute x1, starting transfers between devices: 2.16 us -> 0.07 us  [shards(): got_both.append(lax.ppermute(both, 'tok', swap(tok, 1)))]
  transfers between devices with their start and end apart: 13 -> 17, of which waited for: 6 -> 14; matrix products, arithmetic and copies ran while one was open for 0% -> 0% of each run, Pallas kernels for 28% -> 4%
where the time goes in v3:
time: 58.9 us; the launch traced here: 58.7 us
  waiting for transfers between devices  23.7 us (40%)
  starting transfers between devices  22.1 us (38%)
  Pallas kernels  12.6 us (21%)
    ppermute x3, starting transfers between devices, shards(): close[k] = lax.ppermute(attended[k % ffn], ('tok', 'ffn'), swap(owners, k))  4.65 us
    ppermute x2, waiting for transfers between devices, shards(): got_ups = [lax.ppermute(ups[k], 'tok', swap(tok, k)) for k in far]  4.56 us
    ppermute x1, waiting for transfers between devices, shards(): arrived = [lax.ppermute(here, 'ffn', swap(ffn, k)) for k in range(1, ffn)]  4.53 us
    ppermute x3, starting transfers between devices, shards(): lax.ppermute(hidden, 'tok', swap(tok, k))  4.45 us
    ppermute x2, starting transfers between devices, shards(): got_gates = [lax.ppermute(gates[k], 'tok', swap(tok, k)) for k in far]  3.91 us
    ppermute x3, waiting for transfers between devices, shards(): close[k] = lax.ppermute(attended[k % ffn], ('tok', 'ffn'), swap(owners, k))  3.49 us
    ppermute x2, starting transfers between devices, shards(): got_ups = [lax.ppermute(ups[k], 'tok', swap(tok, k)) for k in far]  3.47 us
    pallas_call x1, Pallas kernels, shards(): pl.pallas_call(functools.partial(attend, ffn), out_shape=[like(table_rows...  3.13 us
  transfers between devices with their start and end apart: 17, of which 14 were waited for; matrix products, arithmetic and copies ran while one was open for 0% of the time, Pallas kernels for 4%

profile of v3, /device:TPU:0, one launch (start us, length us, event | category | flops | bytes accessed | tf_op | source)
XLA Modules:
  0.0 58.7 jit_solution(14455449572738561373)
XLA Ops:
  0.0 0.0 slice-start.8
  0.0 0.0 slice-start
  0.0 0.0 slice-start.9
  0.0 0.0 slice-start.10
  0.0 0.0 slice-start.1
  0.0 0.0 slice-start.2
  0.0 0.0 slice-start.3
  0.0 3.1 %attend.1 = (bf16[8,512]{1,0:T(8,128)(2,1)S(1)}, bf16[8,512]{1,0:T(8,128)(2,1)S(1)}, bf16[2,512,2048]{2,1,0:T(8,128)(2,1)S(1)}, s32[1,32]{1,0:T(1,128)S(1)}, bf1...) custom-call(s32[4]{0:T(128)} %lens_in.1, bf16[4,2048]{1,0:T(4,128)(2,1)} %queries_in.1, bf16[4,256]{1,0:T(4,128)(2,1)} %new_key_in.1, ...), custom_call_target="tpu_custom_call" | custom-call | flops 20000000000 | tf_op jit(solution)/shard_map/attend/pallas_call | solution.py:334
  3.2 3.1 %collective-permute-start.1 = (bf16[8,512]{1,0:T(8,128)(2,1)S(1)}, bf16[8,512]{1,0:T(8,128)(2,1)S(1)}, u32[]{:S(2)}, u32[]{:S(2)}) collective-permute-start(bf16[8,512]{1,0:T(8,128)(2,1)S(1)} %get-tuple-element.30.refs_0_), channel_id=1, source_target_pairs={{0,4},{2,6},{4,0},{6,2},{8,12},{10,14},{12,8},{14,10},{1,5},{3,7},... | collective-permute-start | bytes 24584 | tf_op jit(solution)/shard_map/ppermute | solution.py:363
  6.3 1.4 %collective-permute-start.2 = (bf16[8,512]{1,0:T(8,128)(2,1)S(1)}, bf16[8,512]{1,0:T(8,128)(2,1)S(1)}, u32[]{:S(2)}, u32[]{:S(2)}) collective-permute-start(bf16[8,512]{1,0:T(8,128)(2,1)S(1)} %get-tuple-element.31), channel_id=1, source_target_pairs={{0,6},{2,4},{4,2},{6,0},{8,14},{10,12},{12,10},{14,8},{1,7},{3,5},... | collective-permute-start | bytes 24584 | tf_op jit(solution)/shard_map/ppermute | solution.py:363
  7.7 0.2 collective-permute-start
  7.8 0.1 collective-permute-done.1.refs_2_
  7.9 2.9 %collective-permute-done.2.refs_3_ = bf16[8,512]{1,0:T(8,128)(2,1)S(1)} collective-permute-done((bf16[8,512]{1,0:T(8,128)(2,1)S(1)}, bf16[8,512]{1,0:T(8,128)(2,1)S(1)}, u32[]{:S(2)}, u32[]{:S(2)}) %collective-permute-start.2) | collective-permute-done | bytes 8224 | tf_op jit(solution)/shard_map/ppermute | solution.py:363
  10.8 0.5 collective-permute-done.refs_1_
  11.3 2.6 %collective-permute-start.3 = (bf16[4,8,512]{2,1,0:T(8,128)(2,1)S(1)}, bf16[4,8,512]{2,1,0:T(8,128)(2,1)S(1)}, u32[]{:S(2)}, u32[]{:S(2)}) collective-permute-start(bf16[4,8,512]{2,1,0:T(8,128)(2,1)S(1)} %stack.1.refs_0_), channel_id=1, source_target_pairs={{0,8},{4,12},{8,0},{12,4},{1,9},{5,13},{9,1},{13,5},{2,10},{6,14},... | collective-permute-start | bytes 98312 | tf_op jit(solution)/shard_map/ppermute | solution.py:375
  13.9 2.2 %collective-permute-done.3.refs_1_ = bf16[4,8,512]{2,1,0:T(8,128)(2,1)S(1)} collective-permute-done((bf16[4,8,512]{2,1,0:T(8,128)(2,1)S(1)}, bf16[4,8,512]{2,1,0:T(8,128)(2,1)S(1)}, u32[]{:S(2)}, u32[]{:S(2)}) %collective-permute-start.3) | collective-permute-done | bytes 32800 | tf_op jit(solution)/shard_map/ppermute | solution.py:375
  16.1 1.0 %project.1.refs_0_ = bf16[32,2048]{1,0:T(8,128)(2,1)S(1)} custom-call(s32[1,32]{1,0:T(1,128)S(1)} %get-tuple-element.28.slot_of, bf16[2,512,2048]{2,1,0:T(8,128)(2,1)S(1)} %get-tuple-element.29.weight, bf16[4,8,512]{2,1,0:T(8,128)(2,1)S(1)} %stack.1.refs_0_, bf16[4,8,512]{2,1,0:T(8,128)(2,1)S(1)} %collective-permute-done.3.refs_1_), custom_call_target="tpu_custom_call" | custom-call | tf_op jit(solution)/shard_map/project/pallas_call | solution.py:378
  17.1 0.0 collective-permute-start.4
  17.2 1.3 %collective-permute-done.4.refs_1_ = bf16[32,2048]{1,0:T(8,128)(2,1)S(1)} collective-permute-done((bf16[32,2048]{1,0:T(8,128)(2,1)S(1)}, bf16[32,2048]{1,0:T(8,128)(2,1)S(1)}, u32[]{:S(2)}, u32[]{:S(2)}) %collective-permute-start.4) | collective-permute-done | bytes 131104 | tf_op jit(solution)/shard_map/ppermute | solution.py:386
  18.5 1.1 %collective-permute-start.5 = (bf16[32,2048]{1,0:T(8,128)(2,1)S(1)}, bf16[32,2048]{1,0:T(8,128)(2,1)S(1)}, u32[]{:S(2)}, u32[]{:S(2)}) collective-permute-start(bf16[32,2048]{1,0:T(8,128)(2,1)S(1)} %add.1.refs_2_), channel_id=1, source_target_pairs={{0,2},{2,0},{1,3},{3,1},{4,6},{6,4},{5,7},{7,5},{8,10},{10,8},{9,1... | collective-permute-start | bytes 393224 | tf_op jit(solution)/shard_map/ppermute | solution.py:395
  19.6 4.5 %collective-permute-done.5.refs_3_ = bf16[32,2048]{1,0:T(8,128)(2,1)S(1)} collective-permute-done((bf16[32,2048]{1,0:T(8,128)(2,1)S(1)}, bf16[32,2048]{1,0:T(8,128)(2,1)S(1)}, u32[]{:S(2)}, u32[]{:S(2)}) %collective-permute-start.5) | collective-permute-done | bytes 131104 | tf_op jit(solution)/shard_map/ppermute | solution.py:395
  24.1 0.0 slice-done.8
  24.1 0.0 slice-done.9
  24.1 0.0 slice-done.10
  24.2 0.0 slice-done.11
  24.2 0.0 slice-start.4
  24.2 0.0 slice-start.5
  24.2 2.5 %gate.1 = (bf16[4,8,2048]{2,1,0:T(8,128)(2,1)S(1)}, bf16[32,2048]{1,0:T(8,128)(2,1)S(1)}, bf16[2,8,128]{2,1,0:T(8,128)(2,1)S(1)}, bf16[8,3584]{1,0:T(8,128)(2,1)...) custom-call(bf16[32,2048]{1,0:T(8,128)(2,1)S(1)} %get-tuple-element.26.refs_0_, ...), custom_call_target="tpu_custom_call" | custom-call | tf_op jit(solution)/shard_map/gate/pallas_call | solution.py:401
  26.7 3.9 %collective-permute-start.6 = (bf16[8,3712]{1,0:T(8,128)(2,1)S(1)}, bf16[8,3712]{1,0:T(8,128)(2,1)S(1)}, u32[]{:S(2)}, u32[]{:S(2)}) collective-permute-start(bf16[8,3712]{1,0:T(8,128)(2,1)S(1)} %get-tuple-element.39), channel_id=1, source_target_pairs={{0,12},{4,8},{8,4},{12,0},{1,13},{5,9},{9,5},{13,1},{2,14},{6,10},... | collective-permute-start | bytes 178184 | tf_op jit(solution)/shard_map/ppermute | solution.py:415
  30.6 0.0 collective-permute-start.7
  30.6 0.0 slice-done
  30.7 0.0 slice-done.1
  30.7 0.0 slice-done.2
  30.7 0.0 slice-done.3
  30.7 0.0 slice-start.6
  30.7 0.0 slice-start.7
  30.7 2.5 %up.1 = (bf16[8,3584]{1,0:T(8,128)(2,1)S(1)}, bf16[8,3584]{1,0:T(8,128)(2,1)S(1)}, bf16[8,3584]{1,0:T(8,128)(2,1)S(1)}, bf16[8,3584]{1,0:T(8,128)(2,1)S(1)}) custom-call(bf16[32,2048]{1,0:T(8,128)(2,1)S(1)} %get-tuple-element.33.left, bf16[2048,3584]{1,0:T(8,128)(2,1)S(1)} %bitcast.3), custom_call_target="tpu_custom_call" | custom-call | bytes 29360128 | tf_op jit(solution)/shard_map/up/pallas_call | solution.py:416
  33.2 0.2 collective-permute-done.6.refs_0_.refs_6_
  33.3 2.4 %collective-permute-done.7.refs_1_.refs_7_ = bf16[8,3712]{1,0:T(8,128)(2,1)S(1)} collective-permute-done((bf16[8,3712]{1,0:T(8,128)(2,1)S(1)}, bf16[8,3712]{1,0:T(8,128)(2,1)S(1)}, u32[]{:S(2)}, u32[]{:S(2)}) %collective-permute-start.7) | collective-permute-done | bytes 59424 | tf_op jit(solution)/shard_map/ppermute | solution.py:415
  35.8 0.1 collective-permute-start.8
  35.8 2.3 %collective-permute-start.9 = (bf16[8,3584]{1,0:T(8,128)(2,1)S(1)}, bf16[8,3584]{1,0:T(8,128)(2,1)S(1)}, u32[]{:S(2)}, u32[]{:S(2)}) collective-permute-start(bf16[8,3584]{1,0:T(8,128)(2,1)S(1)} %get-tuple-element.41), channel_id=1, source_target_pairs={{0,12},{4,8},{8,4},{12,0},{1,13},{5,9},{9,5},{13,1},{2,14},{6,10},... | collective-permute-start | bytes 172040 | tf_op jit(solution)/shard_map/ppermute | solution.py:427
  38.1 1.2 %collective-permute-start.10 = (bf16[8,3584]{1,0:T(8,128)(2,1)S(1)}, bf16[8,3584]{1,0:T(8,128)(2,1)S(1)}, u32[]{:S(2)}, u32[]{:S(2)}) collective-permute-start(bf16[8,3584]{1,0:T(8,128)(2,1)S(1)} %get-tuple-element.42), channel_id=1, source_target_pairs={{0,8},{4,12},{8,0},{12,4},{1,9},{5,13},{9,1},{13,5},{2,10},{6,14},... | collective-permute-start | bytes 172040 | tf_op jit(solution)/shard_map/ppermute | solution.py:427
  39.3 2.8 %collective-permute-done.9.refs_4_ = bf16[8,3584]{1,0:T(8,128)(2,1)S(1)} collective-permute-done((bf16[8,3584]{1,0:T(8,128)(2,1)S(1)}, bf16[8,3584]{1,0:T(8,128)(2,1)S(1)}, u32[]{:S(2)}, u32[]{:S(2)}) %collective-permute-start.9) | collective-permute-done | bytes 57376 | tf_op jit(solution)/shard_map/ppermute | solution.py:427
  42.1 1.8 %collective-permute-done.10.refs_5_ = bf16[8,3584]{1,0:T(8,128)(2,1)S(1)} collective-permute-done((bf16[8,3584]{1,0:T(8,128)(2,1)S(1)}, bf16[8,3584]{1,0:T(8,128)(2,1)S(1)}, u32[]{:S(2)}, u32[]{:S(2)}) %collective-permute-start.10) | collective-permute-done | bytes 57376 | tf_op jit(solution)/shard_map/ppermute | solution.py:427
  43.9 0.0 collective-permute-done.8.refs_3_
  43.9 0.2 activate.1.refs_0_
  44.0 1.7 %collective-permute-start.13 = (bf16[8,3584]{1,0:T(8,128)(2,1)S(1)}, bf16[8,3584]{1,0:T(8,128)(2,1)S(1)}, u32[]{:S(2)}, u32[]{:S(2)}) collective-permute-start(bf16[8,3584]{1,0:T(8,128)(2,1)S(1)} %activate.1.refs_0_), channel_id=1, source_target_pairs={{0,12},{4,8},{8,4},{12,0},{1,13},{5,9},{9,5},{13,1},{2,14},{6,10},... | collective-permute-start | bytes 172040 | tf_op jit(solution)/shard_map/ppermute | solution.py:448
  45.8 0.3 collective-permute-start.12
  46.1 2.4 %collective-permute-start.11 = (bf16[8,3584]{1,0:T(8,128)(2,1)S(1)}, bf16[8,3584]{1,0:T(8,128)(2,1)S(1)}, u32[]{:S(2)}, u32[]{:S(2)}) collective-permute-start(bf16[8,3584]{1,0:T(8,128)(2,1)S(1)} %activate.1.refs_0_), channel_id=1, source_target_pairs={{0,4},{4,0},{8,12},{12,8},{1,5},{5,1},{9,13},{13,9},{2,6},{6,2},{1... | collective-permute-start | bytes 172040 | tf_op jit(solution)/shard_map/ppermute | solution.py:448
  48.5 1.6 %collective-permute-done.13.refs_3_ = bf16[8,3584]{1,0:T(8,128)(2,1)S(1)} collective-permute-done((bf16[8,3584]{1,0:T(8,128)(2,1)S(1)}, bf16[8,3584]{1,0:T(8,128)(2,1)S(1)}, u32[]{:S(2)}, u32[]{:S(2)}) %collective-permute-start.13) | collective-permute-done | bytes 57376 | tf_op jit(solution)/shard_map/ppermute | solution.py:448
  50.1 1.2 %collective-permute-done.12.refs_2_ = bf16[8,3584]{1,0:T(8,128)(2,1)S(1)} collective-permute-done((bf16[8,3584]{1,0:T(8,128)(2,1)S(1)}, bf16[8,3584]{1,0:T(8,128)(2,1)S(1)}, u32[]{:S(2)}, u32[]{:S(2)}) %collective-permute-start.12) | collective-permute-done | bytes 57376 | tf_op jit(solution)/shard_map/ppermute | solution.py:448
  51.3 0.0 collective-permute-done.11.refs_1_
  51.3 0.0 slice-done.4
  51.3 0.0 slice-done.5
  51.3 0.0 slice-done.6
  51.3 0.0 slice-done.7
  51.4 2.6 %down.1 = (bf16[8,2048]{1,0:T(8,128)(2,1)S(1)}, bf16[8,2048]{1,0:T(8,128)(2,1)S(1)}, bf16[8,2048]{1,0:T(8,128)(2,1)S(1)}, bf16[8,2048]{1,0:T(8,128)(2,1)S(1)}) custom-call(bf16[8,3584]{1,0:T(8,128)(2,1)S(1)} %activate.1.refs_0_, bf16[8,3584]{1,0:T(8,128)(2,1)S(1)} %collective-permute-done.11.refs_1_, bf16[8,3584]{1,0:T(8,128)(2,1)S(1)} %collective-permute-done.12.refs_2_, ...), custom_call_target="tpu_custom_call" | custom-call | tf_op jit(solution)/shard_map/down/pallas_call | solution.py:450
  54.0 0.0 collective-permute-start.14
  54.0 1.3 %collective-permute-start.15 = (bf16[8,2048]{1,0:T(8,128)(2,1)S(1)}, bf16[8,2048]{1,0:T(8,128)(2,1)S(1)}, u32[]{:S(2)}, u32[]{:S(2)}) collective-permute-start(bf16[8,2048]{1,0:T(8,128)(2,1)S(1)} %get-tuple-element.45), channel_id=1, source_target_pairs={{0,2},{1,3},{2,0},{3,1},{4,6},{5,7},{6,4},{7,5},{8,10},{9,11},{10,... | collective-permute-start | bytes 98312 | tf_op jit(solution)/shard_map/ppermute | solution.py:460
  55.3 0.6 %collective-permute-start.16 = (bf16[8,2048]{1,0:T(8,128)(2,1)S(1)}, bf16[8,2048]{1,0:T(8,128)(2,1)S(1)}, u32[]{:S(2)}, u32[]{:S(2)}) collective-permute-start(bf16[8,2048]{1,0:T(8,128)(2,1)S(1)} %get-tuple-element.46), channel_id=1, source_target_pairs={{0,1},{1,0},{2,3},{3,2},{4,5},{5,4},{6,7},{7,6},{8,9},{9,8},{10,11... | collective-permute-start | bytes 98312 | tf_op jit(solution)/shard_map/ppermute | solution.py:460
  55.9 1.6 %collective-permute-done.14.refs_1_ = bf16[8,2048]{1,0:T(8,128)(2,1)S(1)} collective-permute-done((bf16[8,2048]{1,0:T(8,128)(2,1)S(1)}, bf16[8,2048]{1,0:T(8,128)(2,1)S(1)}, u32[]{:S(2)}, u32[]{:S(2)}) %collective-permute-start.14) | collective-permute-done | bytes 32800 | tf_op jit(solution)/shard_map/ppermute | solution.py:460
  57.4 0.6 %collective-permute-done.15.refs_2_ = bf16[8,2048]{1,0:T(8,128)(2,1)S(1)} collective-permute-done((bf16[8,2048]{1,0:T(8,128)(2,1)S(1)}, bf16[8,2048]{1,0:T(8,128)(2,1)S(1)}, u32[]{:S(2)}, u32[]{:S(2)}) %collective-permute-start.15) | collective-permute-done | bytes 32800 | tf_op jit(solution)/shard_map/ppermute | solution.py:460
  58.1 0.0 collective-permute-done.16.refs_3_
  58.1 0.6 %finish.1 = bf16[8,2048]{1,0:T(8,128)(2,1)} custom-call(bf16[4,8,2048]{2,1,0:T(8,128)(2,1)S(1)} %get-tuple-element.32.mid, bf16[8,2048]{1,0:T(8,128)(2,1)S(1)} %get-tuple-element.43.refs_0_, bf16[8,2048]{1,0:T(8,128)(2,1)S(1)} %collective-permute-done.14.refs_1_, bf16[8,2048]{1,0:T(8,128)(2,1)S(1)} %collective-permute-done.15.refs_2_, ...), custom_call_target="tpu_custom_call" | custom-call | tf_op jit(solution)/shard_map/finish/pallas_call | solution.py:462
  (7 shorter events, 0.0 us)
Async XLA Ops:
  0.0 24.1 %slice-start.8 = ((s8[14680064]{0:T(1024)(128)(4,1)}), s8[4194304]{0:T(1024)(128)(4,1)S(1)}, s32[]{:S(2)}) async-start(s8[14680064]{0:T(1024)(128)(4,1)} %bitcast.6), calls=%async_computation.8 | async-start | bytes 8388608
  0.0 30.6 %slice-start = ((s8[14680064]{0:T(1024)(128)(4,1)}), s8[4194304]{0:T(1024)(128)(4,1)S(1)}, s32[]{:S(2)}) async-start(s8[14680064]{0:T(1024)(128)(4,1)} %bitcast.2), calls=%async_computation | async-start | bytes 8388608
  0.0 24.1 %slice-start.9 = ((s8[14680064]{0:T(1024)(128)(4,1)}), s8[4194304]{0:T(1024)(128)(4,1)S(1)}, s32[]{:S(2)}) async-start(s8[14680064]{0:T(1024)(128)(4,1)} %bitcast.6), calls=%async_computation.9 | async-start | bytes 8388608
  0.0 24.1 %slice-start.10 = ((s8[14680064]{0:T(1024)(128)(4,1)}), s8[4194304]{0:T(1024)(128)(4,1)S(1)}, s32[]{:S(2)}) async-start(s8[14680064]{0:T(1024)(128)(4,1)} %bitcast.6), calls=%async_computation.10 | async-start | bytes 8388608
  0.0 24.1 %slice-start.11 = ((s8[14680064]{0:T(1024)(128)(4,1)}), s8[2097152]{0:T(1024)(128)(4,1)S(1)}, s32[]{:S(2)}) async-start(s8[14680064]{0:T(1024)(128)(4,1)} %bitcast.6), calls=%async_computation.11 | async-start | bytes 4194304
  0.0 30.6 %slice-start.1 = ((s8[14680064]{0:T(1024)(128)(4,1)}), s8[4194304]{0:T(1024)(128)(4,1)S(1)}, s32[]{:S(2)}) async-start(s8[14680064]{0:T(1024)(128)(4,1)} %bitcast.2), calls=%async_computation.1 | async-start | bytes 8388608
  0.0 30.6 %slice-start.2 = ((s8[14680064]{0:T(1024)(128)(4,1)}), s8[4194304]{0:T(1024)(128)(4,1)S(1)}, s32[]{:S(2)}) async-start(s8[14680064]{0:T(1024)(128)(4,1)} %bitcast.2), calls=%async_computation.2 | async-start | bytes 8388608
  0.0 30.6 %slice-start.3 = ((s8[14680064]{0:T(1024)(128)(4,1)}), s8[2097152]{0:T(1024)(128)(4,1)S(1)}, s32[]{:S(2)}) async-start(s8[14680064]{0:T(1024)(128)(4,1)} %bitcast.2), calls=%async_computation.3 | async-start | bytes 4194304
  3.2 4.7 %collective-permute-start.1 = (bf16[8,512]{1,0:T(8,128)(2,1)S(1)}, bf16[8,512]{1,0:T(8,128)(2,1)S(1)}, u32[]{:S(2)}, u32[]{:S(2)}) collective-permute-start(bf16[8,512]{1,0:T(8,128)(2,1)S(1)} %get-tuple-element.30.refs_0_), channel_id=1, source_target_pairs={{0,4},{2,6},{4,0},{6,2},{8,12},{10,14},{12,8},{14,10},{1,5},{3,7},... | collective-permute-start | bytes 24584 | tf_op jit(solution)/shard_map/ppermute | solution.py:363
  6.3 4.5 %collective-permute-start.2 = (bf16[8,512]{1,0:T(8,128)(2,1)S(1)}, bf16[8,512]{1,0:T(8,128)(2,1)S(1)}, u32[]{:S(2)}, u32[]{:S(2)}) collective-permute-start(bf16[8,512]{1,0:T(8,128)(2,1)S(1)} %get-tuple-element.31), channel_id=1, source_target_pairs={{0,6},{2,4},{4,2},{6,0},{8,14},{10,12},{12,10},{14,8},{1,7},{3,5},... | collective-permute-start | bytes 24584 | tf_op jit(solution)/shard_map/ppermute | solution.py:363
  7.7 3.7 %collective-permute-start = (bf16[8,512]{1,0:T(8,128)(2,1)S(1)}, bf16[8,512]{1,0:T(8,128)(2,1)S(1)}, u32[]{:S(2)}, u32[]{:S(2)}) collective-permute-start(bf16[8,512]{1,0:T(8,128)(2,1)S(1)} %get-tuple-element.31), channel_id=1, source_target_pairs={{0,2},{2,0},{4,6},{6,4},{8,10},{10,8},{12,14},{14,12},{1,3},{3,1},... | collective-permute-start | bytes 24584 | tf_op jit(solution)/shard_map/ppermute | solution.py:363
  11.3 4.8 %collective-permute-start.3 = (bf16[4,8,512]{2,1,0:T(8,128)(2,1)S(1)}, bf16[4,8,512]{2,1,0:T(8,128)(2,1)S(1)}, u32[]{:S(2)}, u32[]{:S(2)}) collective-permute-start(bf16[4,8,512]{2,1,0:T(8,128)(2,1)S(1)} %stack.1.refs_0_), channel_id=1, source_target_pairs={{0,8},{4,12},{8,0},{12,4},{1,9},{5,13},{9,1},{13,5},{2,10},{6,14},... | collective-permute-start | bytes 98312 | tf_op jit(solution)/shard_map/ppermute | solution.py:375
  17.1 1.4 %collective-permute-start.4 = (bf16[32,2048]{1,0:T(8,128)(2,1)S(1)}, bf16[32,2048]{1,0:T(8,128)(2,1)S(1)}, u32[]{:S(2)}, u32[]{:S(2)}) collective-permute-start(bf16[32,2048]{1,0:T(8,128)(2,1)S(1)} %project.1.refs_0_), channel_id=1, source_target_pairs={{0,1},{1,0},{2,3},{3,2},{4,5},{5,4},{6,7},{7,6},{8,9},{9,8},{10,11... | collective-permute-start | bytes 393224 | tf_op jit(solution)/shard_map/ppermute | solution.py:386
  18.5 5.6 %collective-permute-start.5 = (bf16[32,2048]{1,0:T(8,128)(2,1)S(1)}, bf16[32,2048]{1,0:T(8,128)(2,1)S(1)}, u32[]{:S(2)}, u32[]{:S(2)}) collective-permute-start(bf16[32,2048]{1,0:T(8,128)(2,1)S(1)} %add.1.refs_2_), channel_id=1, source_target_pairs={{0,2},{2,0},{1,3},{3,1},{4,6},{6,4},{5,7},{7,5},{8,10},{10,8},{9,1... | collective-permute-start | bytes 393224 | tf_op jit(solution)/shard_map/ppermute | solution.py:395
  24.2 27.2 %slice-start.4 = ((s8[14680064]{0:T(1024)(128)(4,1)}), s8[4194304]{0:T(1024)(128)(4,1)S(1)}, s32[]{:S(2)}) async-start(s8[14680064]{0:T(1024)(128)(4,1)} %bitcast.4), calls=%async_computation.4 | async-start | bytes 8388608
  24.2 27.1 %slice-start.5 = ((s8[14680064]{0:T(1024)(128)(4,1)}), s8[4194304]{0:T(1024)(128)(4,1)S(1)}, s32[]{:S(2)}) async-start(s8[14680064]{0:T(1024)(128)(4,1)} %bitcast.4), calls=%async_computation.5 | async-start | bytes 8388608
  26.7 6.6 %collective-permute-start.6 = (bf16[8,3712]{1,0:T(8,128)(2,1)S(1)}, bf16[8,3712]{1,0:T(8,128)(2,1)S(1)}, u32[]{:S(2)}, u32[]{:S(2)}) collective-permute-start(bf16[8,3712]{1,0:T(8,128)(2,1)S(1)} %get-tuple-element.39), channel_id=1, source_target_pairs={{0,12},{4,8},{8,4},{12,0},{1,13},{5,9},{9,5},{13,1},{2,14},{6,10},... | collective-permute-start | bytes 178184 | tf_op jit(solution)/shard_map/ppermute | solution.py:415
  30.6 5.1 %collective-permute-start.7 = (bf16[8,3712]{1,0:T(8,128)(2,1)S(1)}, bf16[8,3712]{1,0:T(8,128)(2,1)S(1)}, u32[]{:S(2)}, u32[]{:S(2)}) collective-permute-start(bf16[8,3712]{1,0:T(8,128)(2,1)S(1)} %get-tuple-element.40), channel_id=1, source_target_pairs={{0,8},{4,12},{8,0},{12,4},{1,9},{5,13},{9,1},{13,5},{2,10},{6,14},... | collective-permute-start | bytes 178184 | tf_op jit(solution)/shard_map/ppermute | solution.py:415
  30.7 20.6 %slice-start.6 = ((s8[14680064]{0:T(1024)(128)(4,1)}), s8[4194304]{0:T(1024)(128)(4,1)S(1)}, s32[]{:S(2)}) async-start(s8[14680064]{0:T(1024)(128)(4,1)} %bitcast.4), calls=%async_computation.6 | async-start | bytes 8388608
  30.7 20.6 %slice-start.7 = ((s8[14680064]{0:T(1024)(128)(4,1)}), s8[2097152]{0:T(1024)(128)(4,1)S(1)}, s32[]{:S(2)}) async-start(s8[14680064]{0:T(1024)(128)(4,1)} %bitcast.4), calls=%async_computation.7 | async-start | bytes 4194304
  35.8 8.1 %collective-permute-start.8 = (bf16[8,7296]{1,0:T(8,128)(2,1)S(1)}, bf16[8,7296]{1,0:T(8,128)(2,1)S(1)}, u32[]{:S(2)}, u32[]{:S(2)}) collective-permute-start(bf16[8,7296]{1,0:T(8,128)(2,1)S(1)} %join.1), channel_id=1, source_target_pairs={{0,4},{4,0},{8,12},{12,8},{1,5},{5,1},{9,13},{13,9},{2,6},{6,2},{1... | collective-permute-start | bytes 350216 | tf_op jit(solution)/shard_map/ppermute | solution.py:438
  35.8 6.3 %collective-permute-start.9 = (bf16[8,3584]{1,0:T(8,128)(2,1)S(1)}, bf16[8,3584]{1,0:T(8,128)(2,1)S(1)}, u32[]{:S(2)}, u32[]{:S(2)}) collective-permute-start(bf16[8,3584]{1,0:T(8,128)(2,1)S(1)} %get-tuple-element.41), channel_id=1, source_target_pairs={{0,12},{4,8},{8,4},{12,0},{1,13},{5,9},{9,5},{13,1},{2,14},{6,10},... | collective-permute-start | bytes 172040 | tf_op jit(solution)/shard_map/ppermute | solution.py:427
  38.1 5.7 %collective-permute-start.10 = (bf16[8,3584]{1,0:T(8,128)(2,1)S(1)}, bf16[8,3584]{1,0:T(8,128)(2,1)S(1)}, u32[]{:S(2)}, u32[]{:S(2)}) collective-permute-start(bf16[8,3584]{1,0:T(8,128)(2,1)S(1)} %get-tuple-element.42), channel_id=1, source_target_pairs={{0,8},{4,12},{8,0},{12,4},{1,9},{5,13},{9,1},{13,5},{2,10},{6,14},... | collective-permute-start | bytes 172040 | tf_op jit(solution)/shard_map/ppermute | solution.py:427
  44.0 6.0 %collective-permute-start.13 = (bf16[8,3584]{1,0:T(8,128)(2,1)S(1)}, bf16[8,3584]{1,0:T(8,128)(2,1)S(1)}, u32[]{:S(2)}, u32[]{:S(2)}) collective-permute-start(bf16[8,3584]{1,0:T(8,128)(2,1)S(1)} %activate.1.refs_0_), channel_id=1, source_target_pairs={{0,12},{4,8},{8,4},{12,0},{1,13},{5,9},{9,5},{13,1},{2,14},{6,10},... | collective-permute-start | bytes 172040 | tf_op jit(solution)/shard_map/ppermute | solution.py:448
  45.8 5.5 %collective-permute-start.12 = (bf16[8,3584]{1,0:T(8,128)(2,1)S(1)}, bf16[8,3584]{1,0:T(8,128)(2,1)S(1)}, u32[]{:S(2)}, u32[]{:S(2)}) collective-permute-start(bf16[8,3584]{1,0:T(8,128)(2,1)S(1)} %activate.1.refs_0_), channel_id=1, source_target_pairs={{0,8},{4,12},{8,0},{12,4},{1,9},{5,13},{9,1},{13,5},{2,10},{6,14},... | collective-permute-start | bytes 172040 | tf_op jit(solution)/shard_map/ppermute | solution.py:448
  46.1 5.2 %collective-permute-start.11 = (bf16[8,3584]{1,0:T(8,128)(2,1)S(1)}, bf16[8,3584]{1,0:T(8,128)(2,1)S(1)}, u32[]{:S(2)}, u32[]{:S(2)}) collective-permute-start(bf16[8,3584]{1,0:T(8,128)(2,1)S(1)} %activate.1.refs_0_), channel_id=1, source_target_pairs={{0,4},{4,0},{8,12},{12,8},{1,5},{5,1},{9,13},{13,9},{2,6},{6,2},{1... | collective-permute-start | bytes 172040 | tf_op jit(solution)/shard_map/ppermute | solution.py:448
  54.0 3.4 %collective-permute-start.14 = (bf16[8,2048]{1,0:T(8,128)(2,1)S(1)}, bf16[8,2048]{1,0:T(8,128)(2,1)S(1)}, u32[]{:S(2)}, u32[]{:S(2)}) collective-permute-start(bf16[8,2048]{1,0:T(8,128)(2,1)S(1)} %get-tuple-element.44), channel_id=1, source_target_pairs={{0,3},{1,2},{2,1},{3,0},{4,7},{5,6},{6,5},{7,4},{8,11},{9,10},{10,... | collective-permute-start | bytes 98312 | tf_op jit(solution)/shard_map/ppermute | solution.py:460
  54.0 4.1 %collective-permute-start.15 = (bf16[8,2048]{1,0:T(8,128)(2,1)S(1)}, bf16[8,2048]{1,0:T(8,128)(2,1)S(1)}, u32[]{:S(2)}, u32[]{:S(2)}) collective-permute-start(bf16[8,2048]{1,0:T(8,128)(2,1)S(1)} %get-tuple-element.45), channel_id=1, source_target_pairs={{0,2},{1,3},{2,0},{3,1},{4,6},{5,7},{6,4},{7,5},{8,10},{9,11},{10,... | collective-permute-start | bytes 98312 | tf_op jit(solution)/shard_map/ppermute | solution.py:460
  55.3 2.8 %collective-permute-start.16 = (bf16[8,2048]{1,0:T(8,128)(2,1)S(1)}, bf16[8,2048]{1,0:T(8,128)(2,1)S(1)}, u32[]{:S(2)}, u32[]{:S(2)}) collective-permute-start(bf16[8,2048]{1,0:T(8,128)(2,1)S(1)} %get-tuple-element.46), channel_id=1, source_target_pairs={{0,1},{1,0},{2,3},{3,2},{4,5},{5,4},{6,7},{7,6},{8,9},{9,8},{10,11... | collective-permute-start | bytes 98312 | tf_op jit(solution)/shard_map/ppermute | solution.py:460

commit v4 on v3

--- a/solution.py
+++ b/solution.py
@@ -166,8 +166,7 @@
 def gate(others, *refs):
     residual, gain, here = refs[:3]
     arrived = refs[3 : 3 + others]
-    weight, mid_out, left_out, stat_out = refs[3 + others : 7 + others]
-    parts = refs[7 + others : -2]
+    weight, mid_out, left_out, stat_out, out = refs[3 + others : 8 + others]
     ordered, squares = refs[-2:]
     blocks, rows, _ = ordered.shape
     width = weight.shape[1]
@@ -193,65 +192,39 @@
         middle = (value - high).astype(BF16).astype(F32)
         low = value - high - middle
         stat = jnp.where(lane == 0, high, jnp.where(lane == 1, middle, low))
-        stat = jnp.where(lane < 3, stat, 0.0).astype(BF16)
-        if k < 2:
-            stat_out[k] = stat
-        else:
-            parts[k][:, width:] = stat
+        stat_out[k] = jnp.where(lane < 3, stat, 0.0).astype(BF16)
     step = column_step(width)
     for c in range(0, width, step):
         total = jnp.dot(left, weight[:, c : c + step], preferred_element_type=F32)
         for k in range(blocks):
-            parts[k][:, c : c + step] = total[k * rows : (k + 1) * rows].astype(BF16)
-
-
-def up(pieces, left, *refs):
-    weights, parts = refs[:pieces], refs[pieces:]
+            out[k, :, c : c + step] = total[k * rows : (k + 1) * rows].astype(BF16)
+
+
+def up(left, stat, gates, weight, *parts):
     rows = parts[0].shape[0]
+    width = weight.shape[1]
+    for k, part in enumerate(parts):
+        part[:, :width] = gates[k]
+        part[:, 2 * width :] = stat[k]
     rhs = left[...]
-    base = 0
-    for weight in weights:
-        width = weight.shape[1]
-        step = column_step(width)
-        for c in range(0, width, step):
-            total = jnp.dot(rhs, weight[:, c : c + step], preferred_element_type=F32)
-            at = base + c
-            for k, part in enumerate(parts):
-                part[:, at : at + step] = total[k * rows : (k + 1) * rows].astype(BF16)
-        base += width
-
-
-def join(up_part, gate_part, stat, *refs):
-    out = refs[-1]
-    width = up_part.shape[1]
-    out[:, :width] = up_part[...]
-    out[:, width : 2 * width] = gate_part[...]
-    out[:, 2 * width :] = stat[1]
-
-
-def activate(features, near, *refs):
+    step = column_step(width)
+    for c in range(0, width, step):
+        total = jnp.dot(rhs, weight[:, c : c + step], preferred_element_type=F32)
+        for k, part in enumerate(parts):
+            part[:, width + c : width + c + step] = total[k * rows : (k + 1) * rows].astype(BF16)
+
+
+def activate(features, *refs):
     out = refs[-1]
     width = out.shape[1]
-    own_up, own_gate, own_stat = refs[:3]
-    both, refs = refs[3 : 2 + near], refs[2 + near : -1]
-    far = len(refs) // 2
-    ups, gates = refs[:far], refs[far : 2 * far]
-    up_sum = own_up[...].astype(F32)
-    gate_sum = own_gate[...].astype(F32)
-    stat = own_stat[0].astype(F32)
-    for part in both:
-        up_sum += part[:, :width].astype(F32)
-        gate_sum += part[:, width : 2 * width].astype(F32)
-        stat += part[:, 2 * width :].astype(F32)
-    for part in ups:
-        up_sum += part[...].astype(F32)
-    for part in gates:
-        gate_sum += part[:, :width].astype(F32)
-        stat += part[:, width:].astype(F32)
-    square = jnp.sum(stat, axis=1, keepdims=True)
+    total = refs[0][...].astype(F32)
+    for part in refs[1:-1]:
+        total += part[...].astype(F32)
+    square = jnp.sum(total[:, 2 * width :], axis=1, keepdims=True)
     inv_rms = lax.rsqrt(square / features + 1e-05)
-    gated = gate_sum * inv_rms
-    out[...] = (gated / (1.0 + jnp.exp(-gated)) * (up_sum * inv_rms)).astype(BF16)
+    gate = total[:, :width] * inv_rms
+    up = total[:, width : 2 * width] * inv_rms
+    out[...] = (gate / (1.0 + jnp.exp(-gate)) * up).astype(BF16)
 
 
 def down(blocks, pieces, *refs):
@@ -325,13 +298,12 @@
     in_hbm = functools.partial(pltpu.with_memory_space_constraint, memory_space=pltpu.HBM)
 
     carried = [
-        out_weight,
         slot_of.reshape(1, requests),
         residual_in,
         norm_gain.reshape(1, features),
     ]
     table_rows = slots * kv_here
-    *attended, out_weight, slot_of, residual_in, norm_gain = pl.pallas_call(
+    *attended, slot_of, residual_in, norm_gain = pl.pallas_call(
         functools.partial(attend, ffn),
         out_shape=[like(table_rows, feat_width)] * ffn
         + [pltpu.VMEM(a.shape, a.dtype) for a in carried],
@@ -347,7 +319,7 @@
             pltpu.VMEM((ffn, table_rows, feat_width), F32),
             pltpu.SemaphoreType.DMA((4 + 2 * slots + len(carried),)),
         ],
-        compiler_params=limit(8),
+        compiler_params=limit(3),
         cost_estimate=pl.CostEstimate(flops=20000000000, transcendentals=0, bytes_accessed=0),
         name="attend",
     )(
@@ -358,21 +330,24 @@
     )
     owners = tok * ffn
     near = min(2, tok)
-    close = [attended[0]] + [None] * (near * ffn - 1)
-    for k in sorted(range(1, near * ffn), reverse=True):
-        close[k] = lax.ppermute(attended[k % ffn], ("tok", "ffn"), swap(owners, k))
+    out_weight = pltpu.with_memory_space_constraint(out_weight, pltpu.VMEM)
     in_vmem = functools.partial(pltpu.with_memory_space_constraint, memory_space=pltpu.VMEM)
-    up_pieces = [in_vmem(up_weight)]
+    close = [None] * (near * ffn)
+    for k in reversed(range(near * ffn)):
+        close[k] = lax.ppermute(
+            attended[k % ffn], ("tok", "ffn", "rep"), swap(owners * rep, k * rep + rep - 1)
+        )
     close = pl.pallas_call(
         functools.partial(stack, near * ffn),
         out_shape=like(near * ffn, table_rows, feat_width),
         in_specs=[VMEM] * (near * ffn),
         out_specs=VMEM,
-        compiler_params=limit(4),
+        compiler_params=limit(3),
         name="stack",
     )(*close)
-    gathered = [close] + [
-        lax.ppermute(close, "tok", swap(tok, k)) for k in range(near, tok, near)
+    gathered = [
+        lax.ppermute(close, ("tok", "rep"), swap(tok * rep, k * rep + rep - 1))
+        for k in range(0, tok, near)
     ]
 
     partial = pl.pallas_call(
@@ -380,7 +355,7 @@
         out_shape=like(requests, features),
         in_specs=[VMEM] * (2 + len(gathered)),
         out_specs=VMEM,
-        compiler_params=limit(8),
+        compiler_params=limit(3),
         name="project",
     )(slot_of, out_weight, *gathered)
     summed = [partial] + [lax.ppermute(partial, "rep", swap(rep, k)) for k in range(1, rep)]
@@ -389,7 +364,7 @@
         out_shape=like(requests, features),
         in_specs=[VMEM] * len(summed),
         out_specs=VMEM,
-        compiler_params=limit(4),
+        compiler_params=limit(3),
         name="add",
     )(*summed)
     arrived = [lax.ppermute(here, "ffn", swap(ffn, k)) for k in range(1, ffn)]
@@ -397,54 +372,42 @@
 
     rows = requests // tok
     share = requests // sums
-    both_width = 2 * hidden_here + 128
-    mid, left, stat, *gates = pl.pallas_call(
+    mid, left, stat, gates = pl.pallas_call(
         functools.partial(gate, len(arrived)),
-        out_shape=[like(sums, share, features), like(requests, features), like(near, rows, 128)]
-        + [like(rows, hidden_here + (128 if k >= near else 0)) for k in range(tok)],
+        out_shape=[
+            like(sums, share, features),
+            like(requests, features),
+            like(tok, rows, 128),
+            like(tok, rows, hidden_here),
+        ],
         in_specs=[VMEM] * (4 + len(arrived)),
-        out_specs=[VMEM] * (3 + tok),
+        out_specs=[VMEM] * 4,
         scratch_shapes=[
             pltpu.VMEM((tok, rows, features), F32),
             pltpu.VMEM((tok, rows, 128), F32),
         ],
-        compiler_params=limit(8),
+        compiler_params=limit(3),
         name="gate",
     )(residual_in, norm_gain, here, *arrived, gate_weight)
-    far = sorted(range(near, tok), reverse=True)
-    got_gates = [lax.ppermute(gates[k], "tok", swap(tok, k)) for k in far]
-    ups = pl.pallas_call(
-        functools.partial(up, len(up_pieces)),
-        out_shape=[like(rows, hidden_here)] * tok,
-        in_specs=[VMEM] * (1 + len(up_pieces)),
+    parts = pl.pallas_call(
+        up,
+        out_shape=[like(rows, 2 * hidden_here + 128)] * tok,
+        in_specs=[VMEM] * 4,
         out_specs=[VMEM] * tok,
-        compiler_params=limit(8),
-        cost_estimate=pl.CostEstimate(
-            flops=0, transcendentals=0, bytes_accessed=4 * up_weight.size
-        ),
+        compiler_params=limit(3),
         name="up",
-    )(left, *up_pieces)
-    got_ups = [lax.ppermute(ups[k], "tok", swap(tok, k)) for k in far]
-    got_both = []
-    if near > 1:
-        both = pl.pallas_call(
-            join,
-            out_shape=like(rows, both_width),
-            in_specs=[VMEM] * 3 + [ANY] * len(far),
-            out_specs=VMEM,
-            compiler_params=limit(4),
-            name="join",
-        )(ups[1], gates[1], stat, *got_gates)
-        got_both.append(lax.ppermute(both, "tok", swap(tok, 1)))
+    )(left, stat, gates, in_vmem(up_weight))
+    order = sorted(range(1, tok), reverse=True)
+    got = [parts[0]] + [lax.ppermute(parts[k], "tok", swap(tok, k)) for k in order]
 
     hidden = pl.pallas_call(
-        functools.partial(activate, features * tok, near),
+        functools.partial(activate, features * tok),
         out_shape=like(rows, hidden_here),
-        in_specs=[VMEM] * (2 + near + 2 * len(far)),
+        in_specs=[VMEM] * tok,
         out_specs=VMEM,
-        compiler_params=limit(8),
+        compiler_params=limit(3),
         name="activate",
-    )(ups[0], gates[0], stat, *got_both, *got_ups, *got_gates)
+    )(*got)
     pieces = {k: lax.ppermute(hidden, "tok", swap(tok, k)) for k in sorted(range(1, tok), reverse=True)}
 
     downs = pl.pallas_call(
@@ -453,7 +416,7 @@
         in_specs=[VMEM] * (1 + tok),
         out_specs=[VMEM] * sums,
         scratch_shapes=[pltpu.VMEM((requests, hidden_here), F32)],
-        compiler_params=limit(8),
+        compiler_params=limit(3),
         name="down",
     )(hidden, *[pieces[k] for k in range(1, tok)], in_vmem(down_weight))
     order = sorted(range(1, sums), reverse=True)
@@ -464,7 +427,7 @@
         out_shape=like(share, features),
         in_specs=[VMEM] * (1 + sums),
         out_specs=VMEM,
-        compiler_params=limit(8),
+        compiler_params=limit(3),
         name="finish",
     )(mid, *got)
 

time: 58.9 us -> 56.7 us (0.963)
  starting transfers between devices: 22.1 us -> 20.4 us
    ppermute x9, starting transfers between devices: 14.7 us -> 11.7 us  [the longest x3 4.58 us: shards(): lax.ppermute(parts[k], 'tok', swap(tok, k))]
    ppermute x1, starting transfers between devices: 1.08 us -> 1.86 us  [shards(): arrived = [lax.ppermute(here, 'ffn', swap(ffn, k)) for k in range(1, ffn)]]
    pallas_call x3 -> x2, Pallas kernels: 2.62 us -> 2.65 us  [the longest x1 2.45 us: shards(): pl.pallas_call(up, out_shape=[like(rows, 2 * hidden_here + 128)] * tok, i...]
  transfers between devices with their start and end apart: 17 -> 17, of which waited for: 14 -> 11; matrix products, arithmetic and copies ran while one was open for 0% -> 0% of each run, Pallas kernels for 4% -> 0%
where the time goes in v4:
time: 56.7 us; the launch traced here: 56.6 us
  waiting for transfers between devices  23.5 us (41%)
  starting transfers between devices  20.4 us (36%)
  Pallas kernels  12.4 us (22%)
    ppermute x3, waiting for transfers between devices, shards(): lax.ppermute(parts[k], 'tok', swap(tok, k))  8.56 us
    ppermute x3, starting transfers between devices, shards(): lax.ppermute(parts[k], 'tok', swap(tok, k))  4.58 us
    ppermute x3, starting transfers between devices, shards(): lax.ppermute(hidden, 'tok', swap(tok, k))  4.45 us
    ppermute x4, starting transfers between devices, shards(): lax.ppermute(attended[k % ffn], ('tok', 'ffn', 'rep'), swap(owners * rep,...  4.45 us
    ppermute x1, waiting for transfers between devices, shards(): arrived = [lax.ppermute(here, 'ffn', swap(ffn, k)) for k in range(1, ffn)]  4.01 us
    ppermute x3, waiting for transfers between devices, shards(): lax.ppermute(hidden, 'tok', swap(tok, k))  3.4 us
    pallas_call x1, Pallas kernels, shards(): pl.pallas_call(functools.partial(attend, ffn), out_shape=[like(table_rows...  2.95 us
    ppermute x4, waiting for transfers between devices, shards(): lax.ppermute(attended[k % ffn], ('tok', 'ffn', 'rep'), swap(owners * rep,...  2.87 us
  transfers between devices with their start and end apart: 17, of which 11 were waited for; matrix products, arithmetic and copies ran while one was open for 0% of the time, Pallas kernels for 0%

profile of v4, /device:TPU:0, one launch (start us, length us, event | category | flops | bytes accessed | tf_op | source)
XLA Modules:
  0.0 56.6 jit_solution(7272358152759522607)
XLA Ops:
  0.0 0.0 slice-start.4
  0.0 0.0 slice-start.8
  0.0 0.0 slice-start.7
  0.0 0.0 slice-start.9
  0.0 0.0 slice-start.10
  0.0 0.0 slice-start.11
  0.1 3.0 %attend.1 = (bf16[8,512]{1,0:T(8,128)(2,1)S(1)}, bf16[8,512]{1,0:T(8,128)(2,1)S(1)}, s32[1,32]{1,0:T(1,128)S(1)}, bf16[32,2048]{1,0:T(8,128)(2,1)S(1)}, f32[1,2048]{1,0:T(1,128)S(1)}) custom-call(s32[4]{0:T(128)} %lens_in.1, bf16[4,2048]{1,0:T(4,128)(2,1)} %queries_in.1, bf16[4,256]{1,0:T(4,128)(2,1)} %new_key_in.1, bf16[4,256]{1,0:T(4,128)(2,1)} %new_value_in.1, ...), custom_call_target="tpu_custom_call" | custom-call | flops 20000000000 | tf_op jit(solution)/shard_map/attend/pallas_call | solution.py:306
  3.0 2.5 %collective-permute-start.2 = (bf16[8,512]{1,0:T(8,128)(2,1)S(1)}, bf16[8,512]{1,0:T(8,128)(2,1)S(1)}, u32[]{:S(2)}, u32[]{:S(2)}) collective-permute-start(bf16[8,512]{1,0:T(8,128)(2,1)S(1)} %get-tuple-element.25), channel_id=1, source_target_pairs={{0,5},{1,4},{2,7},{3,6},{4,1},{5,0},{6,3},{7,2},{8,13},{9,12},{10,... | collective-permute-start | bytes 24584 | tf_op jit(solution)/shard_map/ppermute | solution.py:337
  5.6 0.7 %collective-permute-start = (bf16[8,512]{1,0:T(8,128)(2,1)S(1)}, bf16[8,512]{1,0:T(8,128)(2,1)S(1)}, u32[]{:S(2)}, u32[]{:S(2)}) collective-permute-start(bf16[8,512]{1,0:T(8,128)(2,1)S(1)} %get-tuple-element.25), channel_id=1, source_target_pairs={{0,1},{1,0},{2,3},{3,2},{4,5},{5,4},{6,7},{7,6},{8,9},{9,8},{10,11... | collective-permute-start | bytes 24584 | tf_op jit(solution)/shard_map/ppermute | solution.py:337
  6.2 1.0 %collective-permute-start.3 = (bf16[8,512]{1,0:T(8,128)(2,1)S(1)}, bf16[8,512]{1,0:T(8,128)(2,1)S(1)}, u32[]{:S(2)}, u32[]{:S(2)}) collective-permute-start(bf16[8,512]{1,0:T(8,128)(2,1)S(1)} %get-tuple-element.26), channel_id=1, source_target_pairs={{0,7},{1,6},{2,5},{3,4},{4,3},{5,2},{6,1},{7,0},{8,15},{9,14},{10,... | collective-permute-start | bytes 24584 | tf_op jit(solution)/shard_map/ppermute | solution.py:337
  7.2 0.2 collective-permute-start.1
  7.5 0.0 collective-permute-done.2.refs_2_
  7.5 0.0 collective-permute-done.refs_0_
  7.5 2.7 %collective-permute-done.3.refs_3_ = bf16[8,512]{1,0:T(8,128)(2,1)S(1)} collective-permute-done((bf16[8,512]{1,0:T(8,128)(2,1)S(1)}, bf16[8,512]{1,0:T(8,128)(2,1)S(1)}, u32[]{:S(2)}, u32[]{:S(2)}) %collective-permute-start.3) | collective-permute-done | bytes 8224 | tf_op jit(solution)/shard_map/ppermute | solution.py:337
  10.2 0.1 collective-permute-done.1.refs_1_
  10.3 2.7 %collective-permute-start.5 = (bf16[4,8,512]{2,1,0:T(8,128)(2,1)S(1)}, bf16[4,8,512]{2,1,0:T(8,128)(2,1)S(1)}, u32[]{:S(2)}, u32[]{:S(2)}) collective-permute-start(bf16[4,8,512]{2,1,0:T(8,128)(2,1)S(1)} %stack.1), channel_id=1, source_target_pairs={{0,9},{1,8},{4,13},{5,12},{8,1},{9,0},{12,5},{13,4},{2,11},{3,10},... | collective-permute-start | bytes 98312 | tf_op jit(solution)/shard_map/ppermute | solution.py:349
  13.0 0.0 collective-permute-start.4
  13.0 1.6 %collective-permute-done.5.refs_1_ = bf16[4,8,512]{2,1,0:T(8,128)(2,1)S(1)} collective-permute-done((bf16[4,8,512]{2,1,0:T(8,128)(2,1)S(1)}, bf16[4,8,512]{2,1,0:T(8,128)(2,1)S(1)}, u32[]{:S(2)}, u32[]{:S(2)}) %collective-permute-start.5) | collective-permute-done | bytes 32800 | tf_op jit(solution)/shard_map/ppermute | solution.py:349
  14.6 0.0 collective-permute-done.4.refs_0_
  14.6 0.0 copy-done
  14.6 1.0 %project.1.refs_0_ = bf16[32,2048]{1,0:T(8,128)(2,1)S(1)} custom-call(s32[1,32]{1,0:T(1,128)S(1)} %get-tuple-element.24.slot_of, bf16[2,512,2048]{2,1,0:T(8,128)(2,1)S(1)} %copy-done, bf16[4,8,512]{2,1,0:T(8,128)(2,1)S(1)} %collective-permute-done.4.refs_0_, bf16[4,8,512]{2,1,0:T(8,128)(2,1)S(1)} %collective-permute-done.5.refs_1_), custom_call_target="tpu_custom_call" | custom-call | tf_op jit(solution)/shard_map/project/pallas_call | solution.py:353
  15.6 0.5 collective-permute-start.6
  16.1 1.0 %collective-permute-done.6.refs_1_ = bf16[32,2048]{1,0:T(8,128)(2,1)S(1)} collective-permute-done((bf16[32,2048]{1,0:T(8,128)(2,1)S(1)}, bf16[32,2048]{1,0:T(8,128)(2,1)S(1)}, u32[]{:S(2)}, u32[]{:S(2)}) %collective-permute-start.6) | collective-permute-done | bytes 131104 | tf_op jit(solution)/shard_map/ppermute | solution.py:361
  17.1 1.9 %collective-permute-start.7 = (bf16[32,2048]{1,0:T(8,128)(2,1)S(1)}, bf16[32,2048]{1,0:T(8,128)(2,1)S(1)}, u32[]{:S(2)}, u32[]{:S(2)}) collective-permute-start(bf16[32,2048]{1,0:T(8,128)(2,1)S(1)} %add.1.refs_2_), channel_id=1, source_target_pairs={{0,2},{2,0},{1,3},{3,1},{4,6},{6,4},{5,7},{7,5},{8,10},{10,8},{9,1... | collective-permute-start | bytes 393224 | tf_op jit(solution)/shard_map/ppermute | solution.py:370
  18.9 4.0 %collective-permute-done.7.refs_3_ = bf16[32,2048]{1,0:T(8,128)(2,1)S(1)} collective-permute-done((bf16[32,2048]{1,0:T(8,128)(2,1)S(1)}, bf16[32,2048]{1,0:T(8,128)(2,1)S(1)}, u32[]{:S(2)}, u32[]{:S(2)}) %collective-permute-start.7) | collective-permute-done | bytes 131104 | tf_op jit(solution)/shard_map/ppermute | solution.py:370
  23.0 0.0 slice-done.4
  23.0 0.0 slice-done.5
  23.0 0.0 slice-done.6
  23.0 0.0 slice-done.7
  23.0 0.0 slice-start
  23.0 0.0 slice-start.1
  23.0 2.5 %gate.1 = (bf16[4,8,2048]{2,1,0:T(8,128)(2,1)S(1)}, bf16[32,2048]{1,0:T(8,128)(2,1)S(1)}, bf16[4,8,128]{2,1,0:T(8,128)(2,1)S(1)}, bf16[4,8,3584]{2,1,0:T(8,128)(2,1)S(1)}) custom-call(bf16[32,2048]{1,0:T(8,128)(2,1)S(1)} %get-tuple-element.22.refs_0_, f32[1,2048]{1,0:T(1,128)S(1)} %get-tuple-element.23.refs_1_, bf16[32,2048]{1,0:T(8,128)(2,1)S(1)} %add.1.refs_2_, ...), custom_call_target="tpu_custom_call" | custom-call | tf_op jit(solution)/shard_map/gate/pallas_call | solution.py:375
  25.5 0.0 slice-done.8
  25.6 0.0 slice-done.9
  25.6 0.0 slice-done.10
  25.6 0.0 slice-done.11
  25.6 0.0 slice-start.2
  25.6 0.0 slice-start.3
  25.6 2.4 %up.1 = (bf16[8,7296]{1,0:T(8,128)(2,1)S(1)}, bf16[8,7296]{1,0:T(8,128)(2,1)S(1)}, bf16[8,7296]{1,0:T(8,128)(2,1)S(1)}, bf16[8,7296]{1,0:T(8,128)(2,1)S(1)}) custom-call(bf16[32,2048]{1,0:T(8,128)(2,1)S(1)} %get-tuple-element.28.left, bf16[4,8,128]{2,1,0:T(8,128)(2,1)S(1)} %get-tuple-element.29.stat, bf16[4,8,3584]{2,1,0:T(8,128)(2,1)S(1)} %get-tuple-element.30.gates, ...), custom_call_target="tpu_custom_call" | custom-call | tf_op jit(solution)/shard_map/up/pallas_call | solution.py:392
  28.1 3.9 %collective-permute-start.8 = (bf16[8,7296]{1,0:T(8,128)(2,1)S(1)}, bf16[8,7296]{1,0:T(8,128)(2,1)S(1)}, u32[]{:S(2)}, u32[]{:S(2)}) collective-permute-start(bf16[8,7296]{1,0:T(8,128)(2,1)S(1)} %get-tuple-element.32), channel_id=1, source_target_pairs={{0,12},{4,8},{8,4},{12,0},{1,13},{5,9},{9,5},{13,1},{2,14},{6,10},... | collective-permute-start | bytes 350216 | tf_op jit(solution)/shard_map/ppermute | solution.py:401
  32.0 0.0 collective-permute-start.9
  32.0 0.6 %collective-permute-start.10 = (bf16[8,7296]{1,0:T(8,128)(2,1)S(1)}, bf16[8,7296]{1,0:T(8,128)(2,1)S(1)}, u32[]{:S(2)}, u32[]{:S(2)}) collective-permute-start(bf16[8,7296]{1,0:T(8,128)(2,1)S(1)} %get-tuple-element.34), channel_id=1, source_target_pairs={{0,4},{4,0},{8,12},{12,8},{1,5},{5,1},{9,13},{13,9},{2,6},{6,2},{1... | collective-permute-start | bytes 350216 | tf_op jit(solution)/shard_map/ppermute | solution.py:401
  32.7 3.5 %collective-permute-done.8.refs_1_ = bf16[8,7296]{1,0:T(8,128)(2,1)S(1)} collective-permute-done((bf16[8,7296]{1,0:T(8,128)(2,1)S(1)}, bf16[8,7296]{1,0:T(8,128)(2,1)S(1)}, u32[]{:S(2)}, u32[]{:S(2)}) %collective-permute-start.8) | collective-permute-done | bytes 116768 | tf_op jit(solution)/shard_map/ppermute | solution.py:401
  36.2 5.1 %collective-permute-done.9.refs_2_ = bf16[8,7296]{1,0:T(8,128)(2,1)S(1)} collective-permute-done((bf16[8,7296]{1,0:T(8,128)(2,1)S(1)}, bf16[8,7296]{1,0:T(8,128)(2,1)S(1)}, u32[]{:S(2)}, u32[]{:S(2)}) %collective-permute-start.9) | collective-permute-done | bytes 116768 | tf_op jit(solution)/shard_map/ppermute | solution.py:401
  41.2 0.0 collective-permute-done.10.refs_3_
  41.2 0.2 activate.1.refs_0_
  41.4 2.8 %collective-permute-start.13 = (bf16[8,3584]{1,0:T(8,128)(2,1)S(1)}, bf16[8,3584]{1,0:T(8,128)(2,1)S(1)}, u32[]{:S(2)}, u32[]{:S(2)}) collective-permute-start(bf16[8,3584]{1,0:T(8,128)(2,1)S(1)} %activate.1.refs_0_), channel_id=1, source_target_pairs={{0,12},{4,8},{8,4},{12,0},{1,13},{5,9},{9,5},{13,1},{2,14},{6,10},... | collective-permute-start | bytes 172040 | tf_op jit(solution)/shard_map/ppermute | solution.py:411
  44.2 0.0 collective-permute-start.12
  44.2 1.7 %collective-permute-start.11 = (bf16[8,3584]{1,0:T(8,128)(2,1)S(1)}, bf16[8,3584]{1,0:T(8,128)(2,1)S(1)}, u32[]{:S(2)}, u32[]{:S(2)}) collective-permute-start(bf16[8,3584]{1,0:T(8,128)(2,1)S(1)} %activate.1.refs_0_), channel_id=1, source_target_pairs={{0,4},{4,0},{8,12},{12,8},{1,5},{5,1},{9,13},{13,9},{2,6},{6,2},{1... | collective-permute-start | bytes 172040 | tf_op jit(solution)/shard_map/ppermute | solution.py:411
  45.9 2.2 %collective-permute-done.13.refs_3_ = bf16[8,3584]{1,0:T(8,128)(2,1)S(1)} collective-permute-done((bf16[8,3584]{1,0:T(8,128)(2,1)S(1)}, bf16[8,3584]{1,0:T(8,128)(2,1)S(1)}, u32[]{:S(2)}, u32[]{:S(2)}) %collective-permute-start.13) | collective-permute-done | bytes 57376 | tf_op jit(solution)/shard_map/ppermute | solution.py:411
  48.1 1.2 %collective-permute-done.12.refs_2_ = bf16[8,3584]{1,0:T(8,128)(2,1)S(1)} collective-permute-done((bf16[8,3584]{1,0:T(8,128)(2,1)S(1)}, bf16[8,3584]{1,0:T(8,128)(2,1)S(1)}, u32[]{:S(2)}, u32[]{:S(2)}) %collective-permute-start.12) | collective-permute-done | bytes 57376 | tf_op jit(solution)/shard_map/ppermute | solution.py:411
  49.3 0.0 collective-permute-done.11.refs_1_
  49.3 0.0 slice-done
  49.3 0.0 slice-done.1
  49.3 0.0 slice-done.2
  49.3 0.0 slice-done.3
  49.3 2.6 %down.1 = (bf16[8,2048]{1,0:T(8,128)(2,1)S(1)}, bf16[8,2048]{1,0:T(8,128)(2,1)S(1)}, bf16[8,2048]{1,0:T(8,128)(2,1)S(1)}, bf16[8,2048]{1,0:T(8,128)(2,1)S(1)}) custom-call(bf16[8,3584]{1,0:T(8,128)(2,1)S(1)} %activate.1.refs_0_, bf16[8,3584]{1,0:T(8,128)(2,1)S(1)} %collective-permute-done.11.refs_1_, bf16[8,3584]{1,0:T(8,128)(2,1)S(1)} %collective-permute-done.12.refs_2_, ...), custom_call_target="tpu_custom_call" | custom-call | tf_op jit(solution)/shard_map/down/pallas_call | solution.py:413
  52.0 0.0 collective-permute-start.14
  52.0 1.5 %collective-permute-start.15 = (bf16[8,2048]{1,0:T(8,128)(2,1)S(1)}, bf16[8,2048]{1,0:T(8,128)(2,1)S(1)}, u32[]{:S(2)}, u32[]{:S(2)}) collective-permute-start(bf16[8,2048]{1,0:T(8,128)(2,1)S(1)} %get-tuple-element.37), channel_id=1, source_target_pairs={{0,2},{1,3},{2,0},{3,1},{4,6},{5,7},{6,4},{7,5},{8,10},{9,11},{10,... | collective-permute-start | bytes 98312 | tf_op jit(solution)/shard_map/ppermute | solution.py:423
  53.4 0.4 collective-permute-start.16
  53.8 1.8 %collective-permute-done.14.refs_1_ = bf16[8,2048]{1,0:T(8,128)(2,1)S(1)} collective-permute-done((bf16[8,2048]{1,0:T(8,128)(2,1)S(1)}, bf16[8,2048]{1,0:T(8,128)(2,1)S(1)}, u32[]{:S(2)}, u32[]{:S(2)}) %collective-permute-start.14) | collective-permute-done | bytes 32800 | tf_op jit(solution)/shard_map/ppermute | solution.py:423
  55.6 0.3 collective-permute-done.15.refs_2_
  56.0 0.0 collective-permute-done.16.refs_3_
  56.0 0.6 %finish.1 = bf16[8,2048]{1,0:T(8,128)(2,1)} custom-call(bf16[4,8,2048]{2,1,0:T(8,128)(2,1)S(1)} %get-tuple-element.27.mid, bf16[8,2048]{1,0:T(8,128)(2,1)S(1)} %get-tuple-element.35.refs_0_, bf16[8,2048]{1,0:T(8,128)(2,1)S(1)} %collective-permute-done.14.refs_1_, bf16[8,2048]{1,0:T(8,128)(2,1)S(1)} %collective-permute-done.15.refs_2_, ...), custom_call_target="tpu_custom_call" | custom-call | tf_op jit(solution)/shard_map/finish/pallas_call | solution.py:425
  (8 shorter events, 0.0 us)
Async XLA Ops:
  0.0 23.0 %slice-start.4 = ((s8[14680064]{0:T(1024)(128)(4,1)}), s8[4194304]{0:T(1024)(128)(4,1)S(1)}, s32[]{:S(2)}) async-start(s8[14680064]{0:T(1024)(128)(4,1)} %bitcast.4), calls=%async_computation.4 | async-start | bytes 8388608
  0.0 25.6 %slice-start.8 = ((s8[14680064]{0:T(1024)(128)(4,1)}), s8[4194304]{0:T(1024)(128)(4,1)S(1)}, s32[]{:S(2)}) async-start(s8[14680064]{0:T(1024)(128)(4,1)} %bitcast.6), calls=%async_computation.8 | async-start | bytes 8388608
  0.0 14.6 %copy-start = (bf16[2,512,2048]{2,1,0:T(8,128)(2,1)S(1)}, bf16[2,512,2048]{2,1,0:T(8,128)(2,1)}, u32[]{:S(2)}) copy-start(bf16[2,512,2048]{2,1,0:T(8,128)(2,1)} %weight.2) | copy-start | bytes 12582916
  0.0 23.0 %slice-start.5 = ((s8[14680064]{0:T(1024)(128)(4,1)}), s8[4194304]{0:T(1024)(128)(4,1)S(1)}, s32[]{:S(2)}) async-start(s8[14680064]{0:T(1024)(128)(4,1)} %bitcast.4), calls=%async_computation.5 | async-start | bytes 8388608
  0.0 23.0 %slice-start.6 = ((s8[14680064]{0:T(1024)(128)(4,1)}), s8[4194304]{0:T(1024)(128)(4,1)S(1)}, s32[]{:S(2)}) async-start(s8[14680064]{0:T(1024)(128)(4,1)} %bitcast.4), calls=%async_computation.6 | async-start | bytes 8388608
  0.0 23.0 %slice-start.7 = ((s8[14680064]{0:T(1024)(128)(4,1)}), s8[2097152]{0:T(1024)(128)(4,1)S(1)}, s32[]{:S(2)}) async-start(s8[14680064]{0:T(1024)(128)(4,1)} %bitcast.4), calls=%async_computation.7 | async-start | bytes 4194304
  0.0 25.5 %slice-start.9 = ((s8[14680064]{0:T(1024)(128)(4,1)}), s8[4194304]{0:T(1024)(128)(4,1)S(1)}, s32[]{:S(2)}) async-start(s8[14680064]{0:T(1024)(128)(4,1)} %bitcast.6), calls=%async_computation.9 | async-start | bytes 8388608
  0.0 25.5 %slice-start.10 = ((s8[14680064]{0:T(1024)(128)(4,1)}), s8[4194304]{0:T(1024)(128)(4,1)S(1)}, s32[]{:S(2)}) async-start(s8[14680064]{0:T(1024)(128)(4,1)} %bitcast.6), calls=%async_computation.10 | async-start | bytes 8388608
  0.0 25.5 %slice-start.11 = ((s8[14680064]{0:T(1024)(128)(4,1)}), s8[2097152]{0:T(1024)(128)(4,1)S(1)}, s32[]{:S(2)}) async-start(s8[14680064]{0:T(1024)(128)(4,1)} %bitcast.6), calls=%async_computation.11 | async-start | bytes 4194304
  3.0 4.5 %collective-permute-start.2 = (bf16[8,512]{1,0:T(8,128)(2,1)S(1)}, bf16[8,512]{1,0:T(8,128)(2,1)S(1)}, u32[]{:S(2)}, u32[]{:S(2)}) collective-permute-start(bf16[8,512]{1,0:T(8,128)(2,1)S(1)} %get-tuple-element.25), channel_id=1, source_target_pairs={{0,5},{1,4},{2,7},{3,6},{4,1},{5,0},{6,3},{7,2},{8,13},{9,12},{10,... | collective-permute-start | bytes 24584 | tf_op jit(solution)/shard_map/ppermute | solution.py:337
  5.6 1.9 %collective-permute-start = (bf16[8,512]{1,0:T(8,128)(2,1)S(1)}, bf16[8,512]{1,0:T(8,128)(2,1)S(1)}, u32[]{:S(2)}, u32[]{:S(2)}) collective-permute-start(bf16[8,512]{1,0:T(8,128)(2,1)S(1)} %get-tuple-element.25), channel_id=1, source_target_pairs={{0,1},{1,0},{2,3},{3,2},{4,5},{5,4},{6,7},{7,6},{8,9},{9,8},{10,11... | collective-permute-start | bytes 24584 | tf_op jit(solution)/shard_map/ppermute | solution.py:337
  6.2 4.0 %collective-permute-start.3 = (bf16[8,512]{1,0:T(8,128)(2,1)S(1)}, bf16[8,512]{1,0:T(8,128)(2,1)S(1)}, u32[]{:S(2)}, u32[]{:S(2)}) collective-permute-start(bf16[8,512]{1,0:T(8,128)(2,1)S(1)} %get-tuple-element.26), channel_id=1, source_target_pairs={{0,7},{1,6},{2,5},{3,4},{4,3},{5,2},{6,1},{7,0},{8,15},{9,14},{10,... | collective-permute-start | bytes 24584 | tf_op jit(solution)/shard_map/ppermute | solution.py:337
  7.2 3.1 %collective-permute-start.1 = (bf16[8,512]{1,0:T(8,128)(2,1)S(1)}, bf16[8,512]{1,0:T(8,128)(2,1)S(1)}, u32[]{:S(2)}, u32[]{:S(2)}) collective-permute-start(bf16[8,512]{1,0:T(8,128)(2,1)S(1)} %get-tuple-element.26), channel_id=1, source_target_pairs={{0,3},{1,2},{2,1},{3,0},{4,7},{5,6},{6,5},{7,4},{8,11},{9,10},{10,... | collective-permute-start | bytes 24584 | tf_op jit(solution)/shard_map/ppermute | solution.py:337
  10.3 4.3 %collective-permute-start.5 = (bf16[4,8,512]{2,1,0:T(8,128)(2,1)S(1)}, bf16[4,8,512]{2,1,0:T(8,128)(2,1)S(1)}, u32[]{:S(2)}, u32[]{:S(2)}) collective-permute-start(bf16[4,8,512]{2,1,0:T(8,128)(2,1)S(1)} %stack.1), channel_id=1, source_target_pairs={{0,9},{1,8},{4,13},{5,12},{8,1},{9,0},{12,5},{13,4},{2,11},{3,10},... | collective-permute-start | bytes 98312 | tf_op jit(solution)/shard_map/ppermute | solution.py:349
  13.0 1.6 %collective-permute-start.4 = (bf16[4,8,512]{2,1,0:T(8,128)(2,1)S(1)}, bf16[4,8,512]{2,1,0:T(8,128)(2,1)S(1)}, u32[]{:S(2)}, u32[]{:S(2)}) collective-permute-start(bf16[4,8,512]{2,1,0:T(8,128)(2,1)S(1)} %stack.1), channel_id=1, source_target_pairs={{0,1},{1,0},{4,5},{5,4},{8,9},{9,8},{12,13},{13,12},{2,3},{3,2},{6... | collective-permute-start | bytes 98312 | tf_op jit(solution)/shard_map/ppermute | solution.py:349
  15.6 1.5 %collective-permute-start.6 = (bf16[32,2048]{1,0:T(8,128)(2,1)S(1)}, bf16[32,2048]{1,0:T(8,128)(2,1)S(1)}, u32[]{:S(2)}, u32[]{:S(2)}) collective-permute-start(bf16[32,2048]{1,0:T(8,128)(2,1)S(1)} %project.1.refs_0_), channel_id=1, source_target_pairs={{0,1},{1,0},{2,3},{3,2},{4,5},{5,4},{6,7},{7,6},{8,9},{9,8},{10,11... | collective-permute-start | bytes 393224 | tf_op jit(solution)/shard_map/ppermute | solution.py:361
  17.1 5.9 %collective-permute-start.7 = (bf16[32,2048]{1,0:T(8,128)(2,1)S(1)}, bf16[32,2048]{1,0:T(8,128)(2,1)S(1)}, u32[]{:S(2)}, u32[]{:S(2)}) collective-permute-start(bf16[32,2048]{1,0:T(8,128)(2,1)S(1)} %add.1.refs_2_), channel_id=1, source_target_pairs={{0,2},{2,0},{1,3},{3,1},{4,6},{6,4},{5,7},{7,5},{8,10},{10,8},{9,1... | collective-permute-start | bytes 393224 | tf_op jit(solution)/shard_map/ppermute | solution.py:370
  23.0 26.3 %slice-start = ((s8[14680064]{0:T(1024)(128)(4,1)}), s8[2097152]{0:T(1024)(128)(4,1)S(1)}, s32[]{:S(2)}) async-start(s8[14680064]{0:T(1024)(128)(4,1)} %bitcast.2), calls=%async_computation | async-start | bytes 4194304
  23.0 26.3 %slice-start.1 = ((s8[14680064]{0:T(1024)(128)(4,1)}), s8[4194304]{0:T(1024)(128)(4,1)S(1)}, s32[]{:S(2)}) async-start(s8[14680064]{0:T(1024)(128)(4,1)} %bitcast.2), calls=%async_computation.1 | async-start | bytes 8388608
  25.6 23.7 %slice-start.2 = ((s8[14680064]{0:T(1024)(128)(4,1)}), s8[4194304]{0:T(1024)(128)(4,1)S(1)}, s32[]{:S(2)}) async-start(s8[14680064]{0:T(1024)(128)(4,1)} %bitcast.2), calls=%async_computation.2 | async-start | bytes 8388608
  25.6 23.7 %slice-start.3 = ((s8[14680064]{0:T(1024)(128)(4,1)}), s8[4194304]{0:T(1024)(128)(4,1)S(1)}, s32[]{:S(2)}) async-start(s8[14680064]{0:T(1024)(128)(4,1)} %bitcast.2), calls=%async_computation.3 | async-start | bytes 8388608
  28.1 8.1 %collective-permute-start.8 = (bf16[8,7296]{1,0:T(8,128)(2,1)S(1)}, bf16[8,7296]{1,0:T(8,128)(2,1)S(1)}, u32[]{:S(2)}, u32[]{:S(2)}) collective-permute-start(bf16[8,7296]{1,0:T(8,128)(2,1)S(1)} %get-tuple-element.32), channel_id=1, source_target_pairs={{0,12},{4,8},{8,4},{12,0},{1,13},{5,9},{9,5},{13,1},{2,14},{6,10},... | collective-permute-start | bytes 350216 | tf_op jit(solution)/shard_map/ppermute | solution.py:401
  32.0 9.2 %collective-permute-start.9 = (bf16[8,7296]{1,0:T(8,128)(2,1)S(1)}, bf16[8,7296]{1,0:T(8,128)(2,1)S(1)}, u32[]{:S(2)}, u32[]{:S(2)}) collective-permute-start(bf16[8,7296]{1,0:T(8,128)(2,1)S(1)} %get-tuple-element.33), channel_id=1, source_target_pairs={{0,8},{4,12},{8,0},{12,4},{1,9},{5,13},{9,1},{13,5},{2,10},{6,14},... | collective-permute-start | bytes 350216 | tf_op jit(solution)/shard_map/ppermute | solution.py:401
  32.0 9.2 %collective-permute-start.10 = (bf16[8,7296]{1,0:T(8,128)(2,1)S(1)}, bf16[8,7296]{1,0:T(8,128)(2,1)S(1)}, u32[]{:S(2)}, u32[]{:S(2)}) collective-permute-start(bf16[8,7296]{1,0:T(8,128)(2,1)S(1)} %get-tuple-element.34), channel_id=1, source_target_pairs={{0,4},{4,0},{8,12},{12,8},{1,5},{5,1},{9,13},{13,9},{2,6},{6,2},{1... | collective-permute-start | bytes 350216 | tf_op jit(solution)/shard_map/ppermute | solution.py:401
  41.4 6.7 %collective-permute-start.13 = (bf16[8,3584]{1,0:T(8,128)(2,1)S(1)}, bf16[8,3584]{1,0:T(8,128)(2,1)S(1)}, u32[]{:S(2)}, u32[]{:S(2)}) collective-permute-start(bf16[8,3584]{1,0:T(8,128)(2,1)S(1)} %activate.1.refs_0_), channel_id=1, source_target_pairs={{0,12},{4,8},{8,4},{12,0},{1,13},{5,9},{9,5},{13,1},{2,14},{6,10},... | collective-permute-start | bytes 172040 | tf_op jit(solution)/shard_map/ppermute | solution.py:411
  44.2 5.1 %collective-permute-start.12 = (bf16[8,3584]{1,0:T(8,128)(2,1)S(1)}, bf16[8,3584]{1,0:T(8,128)(2,1)S(1)}, u32[]{:S(2)}, u32[]{:S(2)}) collective-permute-start(bf16[8,3584]{1,0:T(8,128)(2,1)S(1)} %activate.1.refs_0_), channel_id=1, source_target_pairs={{0,8},{4,12},{8,0},{12,4},{1,9},{5,13},{9,1},{13,5},{2,10},{6,14},... | collective-permute-start | bytes 172040 | tf_op jit(solution)/shard_map/ppermute | solution.py:411
  44.2 5.1 %collective-permute-start.11 = (bf16[8,3584]{1,0:T(8,128)(2,1)S(1)}, bf16[8,3584]{1,0:T(8,128)(2,1)S(1)}, u32[]{:S(2)}, u32[]{:S(2)}) collective-permute-start(bf16[8,3584]{1,0:T(8,128)(2,1)S(1)} %activate.1.refs_0_), channel_id=1, source_target_pairs={{0,4},{4,0},{8,12},{12,8},{1,5},{5,1},{9,13},{13,9},{2,6},{6,2},{1... | collective-permute-start | bytes 172040 | tf_op jit(solution)/shard_map/ppermute | solution.py:411
  52.0 3.7 %collective-permute-start.14 = (bf16[8,2048]{1,0:T(8,128)(2,1)S(1)}, bf16[8,2048]{1,0:T(8,128)(2,1)S(1)}, u32[]{:S(2)}, u32[]{:S(2)}) collective-permute-start(bf16[8,2048]{1,0:T(8,128)(2,1)S(1)} %get-tuple-element.36), channel_id=1, source_target_pairs={{0,3},{1,2},{2,1},{3,0},{4,7},{5,6},{6,5},{7,4},{8,11},{9,10},{10,... | collective-permute-start | bytes 98312 | tf_op jit(solution)/shard_map/ppermute | solution.py:423
  52.0 4.0 %collective-permute-start.15 = (bf16[8,2048]{1,0:T(8,128)(2,1)S(1)}, bf16[8,2048]{1,0:T(8,128)(2,1)S(1)}, u32[]{:S(2)}, u32[]{:S(2)}) collective-permute-start(bf16[8,2048]{1,0:T(8,128)(2,1)S(1)} %get-tuple-element.37), channel_id=1, source_target_pairs={{0,2},{1,3},{2,0},{3,1},{4,6},{5,7},{6,4},{7,5},{8,10},{9,11},{10,... | collective-permute-start | bytes 98312 | tf_op jit(solution)/shard_map/ppermute | solution.py:423
  53.4 2.5 %collective-permute-start.16 = (bf16[8,2048]{1,0:T(8,128)(2,1)S(1)}, bf16[8,2048]{1,0:T(8,128)(2,1)S(1)}, u32[]{:S(2)}, u32[]{:S(2)}) collective-permute-start(bf16[8,2048]{1,0:T(8,128)(2,1)S(1)} %get-tuple-element.38), channel_id=1, source_target_pairs={{0,1},{1,0},{2,3},{3,2},{4,5},{5,4},{6,7},{7,6},{8,9},{9,8},{10,11... | collective-permute-start | bytes 98312 | tf_op jit(solution)/shard_map/ppermute | solution.py:423

commit v5 on v4

--- a/solution.py
+++ b/solution.py
@@ -41,7 +41,12 @@
     small.append((new_value_in, new_value))
     pairs = small + [(keys.at[s], key_buf.at[s]) for s in range(slots)]
     pairs += [(values.at[s], value_buf.at[s]) for s in range(slots)]
-    pairs += list(zip(carried_in, carried_out))
+    for a, b in zip(carried_in, carried_out):
+        if a.shape == b.shape:
+            pairs.append((a, b))
+        else:
+            part = b.shape[2]
+            pairs += [(a.at[:, pl.ds(p * part, part)], b.at[p]) for p in range(b.shape[0])]
     loads = [pltpu.make_async_copy(a, b, sems.at[i]) for i, (a, b) in enumerate(pairs)]
     for load in loads:
         load.start()
@@ -134,8 +139,8 @@
     refs[-1][...] = total.astype(BF16)
 
 
-def project(slots, slot_of, weight, *refs):
-    refs, out = refs[:-1], refs[-1]
+def project(slots, peers, slot_of, weight, *refs):
+    refs, outs, parts = refs[: -1 - peers], refs[-1 - peers : -1], refs[-1]
     requests = slot_of.shape[1]
     _, rows, width = refs[0].shape
     kv_here = weight.shape[0]
@@ -153,63 +158,127 @@
                 pick, table, (((0,), (0,)), ((), ())), preferred_element_type=F32
             ).astype(BF16)
         )
-    step = column_step(out.shape[1])
-    for c in range(0, out.shape[1], step):
-        total = jnp.zeros((requests, step), F32)
-        for g in range(kv_here):
-            total += jnp.dot(
-                ordered[g], weight[g, :, c : c + step], preferred_element_type=F32
+    width = parts.shape[2]
+    step = column_step(width)
+    for p in range(peers):
+        for c in range(0, width, step):
+            at = p * width + c
+            total = jnp.zeros((requests, step), F32)
+            for g in range(kv_here):
+                total += jnp.dot(
+                    ordered[g], weight[g, :, at : at + step], preferred_element_type=F32
+                )
+            parts[p, :, c : c + step] = total
+    core = lax.axis_index("rep")
+    for p, out in enumerate(outs):
+        out[...] = parts[core ^ p].astype(BF16)
+
+
+def by_owner(value, ordered):
+    blocks, rows, _ = ordered.shape
+    mine = lax.axis_index("tok")
+    for k in range(blocks):
+        ordered[k] = value[k * rows : (k + 1) * rows]
+    return jnp.concatenate([ordered[mine ^ k] for k in range(blocks)], axis=0)
+
+
+def part_rows(peer, height):
+    return pl.ds(pl.multiple_of((lax.axis_index("rep") ^ peer) * height, height), height)
+
+
+def own_part(core, mid, gain, weight, left, sums, ordered):
+    @pl.when(lax.axis_index("rep") == core)
+    def _():
+        scaled = mid[...].astype(F32) * gain[core]
+        rhs = by_owner(scaled, ordered).astype(BF16)
+        left[...] = rhs
+        height = mid.shape[1]
+        step = column_step(weight.shape[1])
+        for c in range(0, weight.shape[1], step):
+            sums[:, c : c + step] = jnp.dot(
+                rhs,
+                weight[core * height : (core + 1) * height, c : c + step],
+                preferred_element_type=F32,
             )
-        out[:, c : c + step] = total.astype(BF16)
-
-
-def gate(others, *refs):
-    residual, gain, here = refs[:3]
-    arrived = refs[3 : 3 + others]
-    weight, mid_out, left_out, stat_out, out = refs[3 + others : 8 + others]
-    ordered, squares = refs[-2:]
-    blocks, rows, _ = ordered.shape
+
+
+def gate_first(core, residual, gain, weight, *refs):
+    mid, left, sums, ordered = refs[-4:]
+    total = residual[lax.axis_index("rep")].astype(F32)
+    for ref in refs[:-4]:
+        total += ref[...].astype(F32)
+    mid[...] = total.astype(BF16)
+    own_part(core, mid, gain, weight, left, sums, ordered)
+
+
+def gate_next(core, mid, gain, weight, left_in, sums_in, left, sums, ordered):
+    own_part(core, mid, gain, weight, left, sums, ordered)
+
+
+def up_own(left, weight, sums):
+    rhs = left[...]
+    at = part_rows(0, left.shape[1])
+    step = column_step(weight.shape[1])
+    for c in range(0, weight.shape[1], step):
+        sums[:, c : c + step] = jnp.dot(
+            rhs, weight[at, c : c + step], preferred_element_type=F32
+        )
+
+
+def gate_rest(peers, *refs):
+    mids = refs[:peers]
+    gain, weight, sums, mid_out, left, stat_out, out, ordered, squares = refs[peers:]
+    blocks, rows, height = ordered.shape
+    core = lax.axis_index("rep")
+    share = mid_out.shape[2]
+    square = jnp.zeros((blocks * rows, 1), F32)
+    lefts = []
+    for p in range(peers):
+        mid = mids[p][...].astype(F32)
+        for j in range(mid_out.shape[1]):
+            mid_out[core ^ p, j] = mid[j * share : (j + 1) * share].astype(BF16)
+        square += jnp.sum(mid * mid, axis=1, keepdims=True)
+        if p > 0:
+            scaled = by_owner(mid * gain[core ^ p], ordered).astype(BF16)
+            left[p - 1] = scaled
+            lefts.append(scaled)
+    square = by_owner(jnp.broadcast_to(square, (blocks * rows, 128)), squares)
+    high = square.astype(BF16).astype(F32)
+    medium = (square - high).astype(BF16).astype(F32)
+    low = square - high - medium
+    lane = lax.broadcasted_iota(jnp.int32, square.shape, 1)
+    stat = jnp.where(lane == 0, high, jnp.where(lane == 1, medium, low))
+    stat = jnp.where(lane < 3, stat, 0.0).astype(BF16)
+    for k in range(blocks):
+        stat_out[k] = stat[k * rows : (k + 1) * rows]
     width = weight.shape[1]
-    mid = residual[...].astype(F32) + here[...].astype(F32)
-    for other in arrived:
-        mid += other[...].astype(F32)
-    mid = mid.astype(BF16).astype(F32)
-    share = mid_out.shape[1]
-    for j in range(mid_out.shape[0]):
-        mid_out[j] = mid[j * share : (j + 1) * share].astype(BF16)
-    square = jnp.broadcast_to(jnp.sum(mid * mid, axis=1, keepdims=True), (mid.shape[0], 128))
-    scaled = mid * gain[...]
-    for k in range(blocks):
-        ordered[k] = scaled[k * rows : (k + 1) * rows]
-        squares[k] = square[k * rows : (k + 1) * rows]
-    mine = lax.axis_index("tok")
-    left = jnp.concatenate([ordered[mine ^ k] for k in range(blocks)], axis=0).astype(BF16)
-    left_out[...] = left
-    lane = lax.broadcasted_iota(jnp.int32, (rows, 128), 1)
-    for k in range(blocks):
-        value = squares[mine ^ k]
-        high = value.astype(BF16).astype(F32)
-        middle = (value - high).astype(BF16).astype(F32)
-        low = value - high - middle
-        stat = jnp.where(lane == 0, high, jnp.where(lane == 1, middle, low))
-        stat_out[k] = jnp.where(lane < 3, stat, 0.0).astype(BF16)
     step = column_step(width)
     for c in range(0, width, step):
-        total = jnp.dot(left, weight[:, c : c + step], preferred_element_type=F32)
+        total = sums[:, c : c + step]
+        for p in range(1, peers):
+            total += jnp.dot(
+                lefts[p - 1],
+                weight[part_rows(p, height), c : c + step],
+                preferred_element_type=F32,
+            )
         for k in range(blocks):
             out[k, :, c : c + step] = total[k * rows : (k + 1) * rows].astype(BF16)
 
 
-def up(left, stat, gates, weight, *parts):
+def up_rest(sums, rest, stat, gates, weight, *parts):
     rows = parts[0].shape[0]
-    width = weight.shape[1]
+    height, width = rest.shape[2], weight.shape[1]
     for k, part in enumerate(parts):
         part[:, :width] = gates[k]
         part[:, 2 * width :] = stat[k]
-    rhs = left[...]
+    lefts = [rest[p] for p in range(rest.shape[0])]
     step = column_step(width)
     for c in range(0, width, step):
-        total = jnp.dot(rhs, weight[:, c : c + step], preferred_element_type=F32)
+        total = sums[:, c : c + step]
+        for p, left in enumerate(lefts):
+            total += jnp.dot(
+                left, weight[part_rows(p + 1, height), c : c + step], preferred_element_type=F32
+            )
         for k, part in enumerate(parts):
             part[:, width + c : width + c + step] = total[k * rows : (k + 1) * rows].astype(BF16)
 
@@ -258,8 +327,9 @@
 
 
 def finish(mid, *refs):
+    mine = lax.axis_index(("ffn", "rep"))
     out = refs[-1]
-    total = mid[lax.axis_index(("ffn", "rep"))].astype(F32)
+    total = jnp.concatenate([mid[p, mine] for p in range(mid.shape[0])], axis=1).astype(F32)
     for part in refs[:-1]:
         total += part[...].astype(F32)
     out[...] = total.astype(BF16)
@@ -297,8 +367,10 @@
     feat_width = out_weight.shape[1]
     in_hbm = functools.partial(pltpu.with_memory_space_constraint, memory_space=pltpu.HBM)
 
+    height = features // rep
+    slot_of = slot_of.reshape(1, requests)
     carried = [
-        slot_of.reshape(1, requests),
+        slot_of,
         residual_in,
         norm_gain.reshape(1, features),
     ]
@@ -306,7 +378,11 @@
     *attended, slot_of, residual_in, norm_gain = pl.pallas_call(
         functools.partial(attend, ffn),
         out_shape=[like(table_rows, feat_width)] * ffn
-        + [pltpu.VMEM(a.shape, a.dtype) for a in carried],
+        + [
+            pltpu.VMEM(slot_of.shape, slot_of.dtype),
+            pltpu.VMEM((rep, requests, height), BF16),
+            pltpu.VMEM((rep, 1, height), F32),
+        ],
         in_specs=[HBM] * (6 + len(carried)),
         out_specs=[VMEM] * (ffn + len(carried)),
         scratch_shapes=[
@@ -317,7 +393,7 @@
             pltpu.VMEM(key_cache.shape, BF16),
             pltpu.VMEM(value_cache.shape, BF16),
             pltpu.VMEM((ffn, table_rows, feat_width), F32),
-            pltpu.SemaphoreType.DMA((4 + 2 * slots + len(carried),)),
+            pltpu.SemaphoreType.DMA((5 + 2 * slots + 2 * rep,)),
         ],
         compiler_params=limit(3),
         cost_estimate=pl.CostEstimate(flops=20000000000, transcendentals=0, bytes_accessed=0),
@@ -350,53 +426,87 @@
         for k in range(0, tok, near)
     ]
 
-    partial = pl.pallas_call(
-        functools.partial(project, slots),
-        out_shape=like(requests, features),
+    partials = pl.pallas_call(
+        functools.partial(project, slots, rep),
+        out_shape=[like(requests, height)] * rep,
         in_specs=[VMEM] * (2 + len(gathered)),
-        out_specs=VMEM,
-        compiler_params=limit(3),
+        out_specs=[VMEM] * rep,
+        scratch_shapes=[pltpu.VMEM((rep, requests, height), F32)],
+        compiler_params=limit(3),
+        cost_estimate=pl.CostEstimate(flops=10000000000, transcendentals=0, bytes_accessed=0),
         name="project",
     )(slot_of, out_weight, *gathered)
-    summed = [partial] + [lax.ppermute(partial, "rep", swap(rep, k)) for k in range(1, rep)]
+    summed = [partials[0]] + [
+        lax.ppermute(partials[k], "rep", swap(rep, k)) for k in range(1, rep)
+    ]
+    up_weight = in_vmem(up_weight)
     here = pl.pallas_call(
         functools.partial(add, len(summed)),
-        out_shape=like(requests, features),
-        in_specs=[VMEM] * len(summed),
+        out_shape=like(requests, height),
+        in_specs=[VMEM] * (len(summed) + 1),
         out_specs=VMEM,
         compiler_params=limit(3),
         name="add",
-    )(*summed)
+    )(*summed, up_weight)
     arrived = [lax.ppermute(here, "ffn", swap(ffn, k)) for k in range(1, ffn)]
     gate_weight = in_vmem(gate_weight)
-
     rows = requests // tok
     share = requests // sums
-    mid, left, stat, gates = pl.pallas_call(
-        functools.partial(gate, len(arrived)),
+    own_shapes = [like(requests, height), jax.ShapeDtypeStruct((requests, hidden_here), F32)]
+    mid_own, own, own_sums = pl.pallas_call(
+        functools.partial(gate_first, rep - 1),
+        out_shape=[like(requests, height)] + own_shapes,
+        in_specs=[VMEM] * (3 + ffn),
+        out_specs=[VMEM] * 3,
+        scratch_shapes=[pltpu.VMEM((tok, rows, height), F32)],
+        compiler_params=limit(3),
+        name="gate_first",
+    )(residual_in, norm_gain, gate_weight, here, *arrived)
+    mids = [mid_own] + [lax.ppermute(mid_own, "rep", swap(rep, k)) for k in range(1, rep)]
+    for core in reversed(range(rep - 1)):
+        own, own_sums = pl.pallas_call(
+            functools.partial(gate_next, core),
+            out_shape=own_shapes,
+            in_specs=[VMEM] * 5,
+            out_specs=[VMEM] * 2,
+            input_output_aliases={3: 0, 4: 1},
+            scratch_shapes=[pltpu.VMEM((tok, rows, height), F32)],
+            compiler_params=limit(3),
+            name="gate_next",
+        )(mid_own, norm_gain, gate_weight, own, own_sums)
+    up_sums = pl.pallas_call(
+        up_own,
+        out_shape=own_shapes[1],
+        in_specs=[VMEM] * 2,
+        out_specs=VMEM,
+        compiler_params=limit(3),
+        name="up_own",
+    )(own, up_weight)
+    mid, rest, stat, gates = pl.pallas_call(
+        functools.partial(gate_rest, rep),
         out_shape=[
-            like(sums, share, features),
-            like(requests, features),
+            like(rep, sums, share, height),
+            like(rep - 1, requests, height),
             like(tok, rows, 128),
             like(tok, rows, hidden_here),
         ],
-        in_specs=[VMEM] * (4 + len(arrived)),
+        in_specs=[VMEM] * (3 + rep),
         out_specs=[VMEM] * 4,
         scratch_shapes=[
-            pltpu.VMEM((tok, rows, features), F32),
+            pltpu.VMEM((tok, rows, height), F32),
             pltpu.VMEM((tok, rows, 128), F32),
         ],
         compiler_params=limit(3),
-        name="gate",
-    )(residual_in, norm_gain, here, *arrived, gate_weight)
+        name="gate_rest",
+    )(*mids, norm_gain, gate_weight, own_sums)
     parts = pl.pallas_call(
-        up,
+        up_rest,
         out_shape=[like(rows, 2 * hidden_here + 128)] * tok,
-        in_specs=[VMEM] * 4,
+        in_specs=[VMEM] * 5,
         out_specs=[VMEM] * tok,
         compiler_params=limit(3),
-        name="up",
-    )(left, stat, gates, in_vmem(up_weight))
+        name="up_rest",
+    )(up_sums, rest, stat, gates, up_weight)
     order = sorted(range(1, tok), reverse=True)
     got = [parts[0]] + [lax.ppermute(parts[k], "tok", swap(tok, k)) for k in order]
 

time: 56.7 us -> 56 us (0.988)
  waiting for transfers between devices: 23.5 us -> 21.6 us
  starting transfers between devices: 20.4 us -> 21.2 us
    ppermute x1, waiting for transfers between devices: 4.01 us -> 2.6 us  [shards(): arrived = [lax.ppermute(here, 'ffn', swap(ffn, k)) for k in range(1, ffn)]]
    ppermute x1 -> x2, starting transfers between devices: 0.47 us -> 1.43 us  [the longest x1 0.92 us: shards(): lax.ppermute(mid_own, 'rep', swap(rep, k))]
    ppermute x3, waiting for transfers between devices: 8.56 us -> 7.84 us  [shards(): lax.ppermute(parts[k], 'tok', swap(tok, k))]
    pallas_call x3 -> x6, Pallas kernels: 5.97 us -> 6.22 us  [the longest x1 1.3 us: shards(): pl.pallas_call(functools.partial(gate_rest, rep), out_shape=[like(rep, su...]
  transfers between devices with their start and end apart: 17 -> 18, of which waited for: 11 -> 11; matrix products, arithmetic and copies ran while one was open for 0% -> 0% of each run, Pallas kernels for 0% -> 5%
where the time goes in v5:
time: 56 us; the launch traced here: 55.8 us
  waiting for transfers between devices  21.6 us (39%)
  starting transfers between devices  21.2 us (38%)
  Pallas kernels  12.7 us (23%)
    ppermute x3, waiting for transfers between devices, shards(): lax.ppermute(parts[k], 'tok', swap(tok, k))  7.84 us
    ppermute x3, starting transfers between devices, shards(): lax.ppermute(parts[k], 'tok', swap(tok, k))  4.49 us
    ppermute x3, starting transfers between devices, shards(): lax.ppermute(hidden, 'tok', swap(tok, k))  4.45 us
    ppermute x4, starting transfers between devices, shards(): lax.ppermute(attended[k % ffn], ('tok', 'ffn', 'rep'), swap(owners * rep,...  4.44 us
    ppermute x3, waiting for transfers between devices, shards(): lax.ppermute(hidden, 'tok', swap(tok, k))  3.69 us
    pallas_call x1, Pallas kernels, shards(): pl.pallas_call(functools.partial(attend, ffn), out_shape=[like(table_rows...  2.97 us
    ppermute x4, waiting for transfers between devices, shards(): lax.ppermute(attended[k % ffn], ('tok', 'ffn', 'rep'), swap(owners * rep,...  2.87 us
    ppermute x2, starting transfers between devices, shards(): lax.ppermute(close, ('tok', 'rep'), swap(tok * rep, k * rep + rep - 1))  2.7 us
  transfers between devices with their start and end apart: 18, of which 11 were waited for; matrix products, arithmetic and copies ran while one was open for 0% of the time, Pallas kernels for 5%

profile of v5, /device:TPU:0, one launch (start us, length us, event | category | flops | bytes accessed | tf_op | source)
XLA Modules:
  0.0 55.8 jit_solution(18160005902247829201)
XLA Ops:
  0.0 3.0 %attend.1 = (bf16[8,512]{1,0:T(8,128)(2,1)S(1)}, bf16[8,512]{1,0:T(8,128)(2,1)S(1)}, s32[1,32]{1,0:T(1,128)S(1)}, bf16[2,32,1024]{2,1,0:T(8,128)(2,1)S(1)}, f32[2,1,1024]{2,1,0:T(1,128)S(1)}) custom-call(s32[4]{0:T(128)} %lens_in.1, bf16[4,2048]{1,0:T(4,128)(2,1)} %queries_in.1, bf16[4,256]{1,0:T(4,128)(2,1)} %new_key_in.1, bf16[4,256]{1,0:T(4,128)(2,1)} %new_value_in.1, ...), custom_call_target="tpu_custom_call" | custom-call | flops 20000000000 | tf_op jit(solution)/shard_map/attend/pallas_call | solution.py:378
  3.0 2.5 %collective-permute-start.2 = (bf16[8,512]{1,0:T(8,128)(2,1)S(1)}, bf16[8,512]{1,0:T(8,128)(2,1)S(1)}, u32[]{:S(2)}, u32[]{:S(2)}) collective-permute-start(bf16[8,512]{1,0:T(8,128)(2,1)S(1)} %get-tuple-element.32), channel_id=1, source_target_pairs={{0,5},{1,4},{2,7},{3,6},{4,1},{5,0},{6,3},{7,2},{8,13},{9,12},{10,... | collective-permute-start | bytes 24584 | tf_op jit(solution)/shard_map/ppermute | solution.py:413
  5.5 0.7 %collective-permute-start = (bf16[8,512]{1,0:T(8,128)(2,1)S(1)}, bf16[8,512]{1,0:T(8,128)(2,1)S(1)}, u32[]{:S(2)}, u32[]{:S(2)}) collective-permute-start(bf16[8,512]{1,0:T(8,128)(2,1)S(1)} %get-tuple-element.32), channel_id=1, source_target_pairs={{0,1},{1,0},{2,3},{3,2},{4,5},{5,4},{6,7},{7,6},{8,9},{9,8},{10,11... | collective-permute-start | bytes 24584 | tf_op jit(solution)/shard_map/ppermute | solution.py:413
  6.2 1.0 %collective-permute-start.3 = (bf16[8,512]{1,0:T(8,128)(2,1)S(1)}, bf16[8,512]{1,0:T(8,128)(2,1)S(1)}, u32[]{:S(2)}, u32[]{:S(2)}) collective-permute-start(bf16[8,512]{1,0:T(8,128)(2,1)S(1)} %get-tuple-element.33), channel_id=1, source_target_pairs={{0,7},{1,6},{2,5},{3,4},{4,3},{5,2},{6,1},{7,0},{8,15},{9,14},{10,... | collective-permute-start | bytes 24584 | tf_op jit(solution)/shard_map/ppermute | solution.py:413
  7.2 0.2 collective-permute-start.1
  7.4 0.0 collective-permute-done.2.refs_2_
  7.4 0.0 collective-permute-done.refs_0_
  7.4 2.7 %collective-permute-done.3.refs_3_ = bf16[8,512]{1,0:T(8,128)(2,1)S(1)} collective-permute-done((bf16[8,512]{1,0:T(8,128)(2,1)S(1)}, bf16[8,512]{1,0:T(8,128)(2,1)S(1)}, u32[]{:S(2)}, u32[]{:S(2)}) %collective-permute-start.3) | collective-permute-done | bytes 8224 | tf_op jit(solution)/shard_map/ppermute | solution.py:413
  10.2 0.1 collective-permute-done.1.refs_1_
  10.3 2.7 %collective-permute-start.5 = (bf16[4,8,512]{2,1,0:T(8,128)(2,1)S(1)}, bf16[4,8,512]{2,1,0:T(8,128)(2,1)S(1)}, u32[]{:S(2)}, u32[]{:S(2)}) collective-permute-start(bf16[4,8,512]{2,1,0:T(8,128)(2,1)S(1)} %stack.1), channel_id=1, source_target_pairs={{0,9},{1,8},{4,13},{5,12},{8,1},{9,0},{12,5},{13,4},{2,11},{3,10},... | collective-permute-start | bytes 98312 | tf_op jit(solution)/shard_map/ppermute | solution.py:425
  13.0 0.0 collective-permute-start.4
  13.0 1.6 %collective-permute-done.5.refs_1_ = bf16[4,8,512]{2,1,0:T(8,128)(2,1)S(1)} collective-permute-done((bf16[4,8,512]{2,1,0:T(8,128)(2,1)S(1)}, bf16[4,8,512]{2,1,0:T(8,128)(2,1)S(1)}, u32[]{:S(2)}, u32[]{:S(2)}) %collective-permute-start.5) | collective-permute-done | bytes 32800 | tf_op jit(solution)/shard_map/ppermute | solution.py:425
  14.6 0.0 collective-permute-done.4.refs_0_
  14.6 0.0 copy-done
  14.6 0.0 slice-start
  14.6 0.0 slice-start.1
  14.6 0.0 slice-start.2
  14.6 1.0 %project.1 = (bf16[32,1024]{1,0:T(8,128)(2,1)S(1)}, bf16[32,1024]{1,0:T(8,128)(2,1)S(1)}) custom-call(s32[1,32]{1,0:T(1,128)S(1)} %get-tuple-element.31.slot_of, bf16[2,512,2048]{2,1,0:T(8,128)(2,1)S(1)} %copy-done, bf16[4,8,512]{2,1,0:T(8,128)(2,1)S(1)} %collective-permute-done.4.refs_0_, bf16[4,8,512]{2,1,0:T(8,128)(2,1)S(1)} %collective-permute-done.5.refs_1_), custom_call_target="tpu_custom_call" | custom-call | flops 10000000000 | tf_op jit(solution)/shard_map/project/pallas_call | solution.py:429
  15.6 0.5 collective-permute-start.6
  16.2 0.9 %collective-permute-done.6.refs_1_ = bf16[32,1024]{1,0:T(8,128)(2,1)S(1)} collective-permute-done((bf16[32,1024]{1,0:T(8,128)(2,1)S(1)}, bf16[32,1024]{1,0:T(8,128)(2,1)S(1)}, u32[]{:S(2)}, u32[]{:S(2)}) %collective-permute-start.6) | collective-permute-done | bytes 65568 | tf_op jit(solution)/shard_map/ppermute | solution.py:440
  17.1 0.0 slice-done.4
  17.1 0.0 slice-done.5
  17.1 0.0 slice-done.6
  17.1 0.0 slice-done.7
  17.1 0.0 slice-start.3
  17.1 1.9 %collective-permute-start.7 = (bf16[32,1024]{1,0:T(8,128)(2,1)S(1)}, bf16[32,1024]{1,0:T(8,128)(2,1)S(1)}, u32[]{:S(2)}, u32[]{:S(2)}) collective-permute-start(bf16[32,1024]{1,0:T(8,128)(2,1)S(1)} %add.1.refs_0_), channel_id=1, source_target_pairs={{0,2},{2,0},{1,3},{3,1},{4,6},{6,4},{5,7},{7,5},{8,10},{10,8},{9,1... | collective-permute-start | bytes 196616 | tf_op jit(solution)/shard_map/ppermute | solution.py:451
  19.0 2.6 %collective-permute-done.7.refs_1_ = bf16[32,1024]{1,0:T(8,128)(2,1)S(1)} collective-permute-done((bf16[32,1024]{1,0:T(8,128)(2,1)S(1)}, bf16[32,1024]{1,0:T(8,128)(2,1)S(1)}, u32[]{:S(2)}, u32[]{:S(2)}) %collective-permute-start.7) | collective-permute-done | bytes 65568 | tf_op jit(solution)/shard_map/ppermute | solution.py:451
  21.6 0.0 slice-done
  21.6 0.0 slice-done.1
  21.6 0.0 slice-done.2
  21.6 0.0 slice-done.3
  21.6 0.9 %collective-permute-start.8 = (bf16[32,1024]{1,0:T(8,128)(2,1)S(1)}, bf16[32,1024]{1,0:T(8,128)(2,1)S(1)}, u32[]{:S(2)}, u32[]{:S(2)}) collective-permute-start(bf16[32,1024]{1,0:T(8,128)(2,1)S(1)} %get-tuple-element.36.mid.refs_0_), channel_id=1, source_target_pairs={{0,1},{1,0},{2,3},{3,2},{4,5},{5,4},{6,7},{7,6},{8,9},{9,8},{10,11... | collective-permute-start | bytes 196616 | tf_op jit(solution)/shard_map/ppermute | solution.py:465
  22.6 1.3 %gate_next.1 = (bf16[32,1024]{1,0:T(8,128)(2,1)S(1)}, f32[32,3584]{1,0:T(8,128)S(1)}) custom-call(bf16[32,1024]{1,0:T(8,128)(2,1)S(1)} %get-tuple-element.36.mid.refs_0_, f32[2,1,1024]{2,1,0:T(1,128)S(1)} %get-tuple-element.30.gain.refs_2_, bf16[2048,3584]{1,0:T(8,128)(2,1)S(1)} %bitcast.3, ...), custom_call_target="tpu_custom_call", output_to_operand_aliasing={{0}: (3, {}), {1}: (4, {})} | custom-call | tf_op jit(solution)/shard_map/gate_next/pallas_call | solution.py:467
  23.9 1.3 %up_own.1.sums = f32[32,3584]{1,0:T(8,128)S(1)} custom-call(bf16[32,1024]{1,0:T(8,128)(2,1)S(1)} %get-tuple-element.41.left, bf16[2048,3584]{1,0:T(8,128)(2,1)S(1)} %bitcast.5), custom_call_target="tpu_custom_call" | custom-call | tf_op jit(solution)/shard_map/up_own/pallas_call | solution.py:477
  25.1 0.0 collective-permute-done.8.refs_1_
  25.2 0.0 slice-start.8
  25.2 0.0 slice-start.9
  25.2 1.3 %gate_rest.1 = (bf16[2,4,8,1024]{3,2,1,0:T(8,128)(2,1)S(1)}, bf16[1,32,1024]{2,1,0:T(8,128)(2,1)S(1)}, bf16[4,8,128]{2,1,0:T(8,128)(2,1)S(1)}, bf16[4,8,3584]{2,1,0:T(8,128)(2,1)S(1)}) custom-call(bf16[32,1024]{1,0:T(8,128)(2,1)S(1)} %get-tuple-element.36.mid.refs_0_, bf16[32,1024]{1,0:T(8,128)(2,1)S(1)} %collective-permute-done.8.refs_1_, ...), custom_call_target="tpu_custom_call" | custom-call | tf_op jit(solution)/shard_map/gate_rest/pallas_call | solution.py:485
  26.5 0.0 slice-start.10
  26.5 0.0 slice-start.11
  26.5 1.3 %up_rest.1 = (bf16[8,7296]{1,0:T(8,128)(2,1)S(1)}, bf16[8,7296]{1,0:T(8,128)(2,1)S(1)}, bf16[8,7296]{1,0:T(8,128)(2,1)S(1)}, bf16[8,7296]{1,0:T(8,128)(2,1)S(1)}) custom-call(f32[32,3584]{1,0:T(8,128)S(1)} %up_own.1.sums, bf16[1,32,1024]{2,1,0:T(8,128)(2,1)S(1)} %get-tuple-element.42.rest, bf16[4,8,128]{2,1,0:T(8,128)(2,1)S(1)} %get-tuple-element.43.stat, ...), custom_call_target="tpu_custom_call" | custom-call | tf_op jit(solution)/shard_map/up_rest/pallas_call | solution.py:502
  27.8 3.8 %collective-permute-start.9 = (bf16[8,7296]{1,0:T(8,128)(2,1)S(1)}, bf16[8,7296]{1,0:T(8,128)(2,1)S(1)}, u32[]{:S(2)}, u32[]{:S(2)}) collective-permute-start(bf16[8,7296]{1,0:T(8,128)(2,1)S(1)} %get-tuple-element.46), channel_id=1, source_target_pairs={{0,12},{4,8},{8,4},{12,0},{1,13},{5,9},{9,5},{13,1},{2,14},{6,10},... | collective-permute-start | bytes 350216 | tf_op jit(solution)/shard_map/ppermute | solution.py:511
  31.7 0.0 collective-permute-start.10
  31.7 0.6 %collective-permute-start.11 = (bf16[8,7296]{1,0:T(8,128)(2,1)S(1)}, bf16[8,7296]{1,0:T(8,128)(2,1)S(1)}, u32[]{:S(2)}, u32[]{:S(2)}) collective-permute-start(bf16[8,7296]{1,0:T(8,128)(2,1)S(1)} %get-tuple-element.48), channel_id=1, source_target_pairs={{0,4},{4,0},{8,12},{12,8},{1,5},{5,1},{9,13},{13,9},{2,6},{6,2},{1... | collective-permute-start | bytes 350216 | tf_op jit(solution)/shard_map/ppermute | solution.py:511
  32.3 3.0 %collective-permute-done.9.refs_1_ = bf16[8,7296]{1,0:T(8,128)(2,1)S(1)} collective-permute-done((bf16[8,7296]{1,0:T(8,128)(2,1)S(1)}, bf16[8,7296]{1,0:T(8,128)(2,1)S(1)}, u32[]{:S(2)}, u32[]{:S(2)}) %collective-permute-start.9) | collective-permute-done | bytes 116768 | tf_op jit(solution)/shard_map/ppermute | solution.py:511
  35.3 4.8 %collective-permute-done.10.refs_2_ = bf16[8,7296]{1,0:T(8,128)(2,1)S(1)} collective-permute-done((bf16[8,7296]{1,0:T(8,128)(2,1)S(1)}, bf16[8,7296]{1,0:T(8,128)(2,1)S(1)}, u32[]{:S(2)}, u32[]{:S(2)}) %collective-permute-start.10) | collective-permute-done | bytes 116768 | tf_op jit(solution)/shard_map/ppermute | solution.py:511
  40.2 0.0 collective-permute-done.11.refs_3_
  40.2 0.2 activate.1.refs_0_
  40.4 3.1 %collective-permute-start.14 = (bf16[8,3584]{1,0:T(8,128)(2,1)S(1)}, bf16[8,3584]{1,0:T(8,128)(2,1)S(1)}, u32[]{:S(2)}, u32[]{:S(2)}) collective-permute-start(bf16[8,3584]{1,0:T(8,128)(2,1)S(1)} %activate.1.refs_0_), channel_id=1, source_target_pairs={{0,12},{4,8},{8,4},{12,0},{1,13},{5,9},{9,5},{13,1},{2,14},{6,10},... | collective-permute-start | bytes 172040 | tf_op jit(solution)/shard_map/ppermute | solution.py:521
  43.4 0.0 collective-permute-start.13
  43.4 1.4 %collective-permute-start.12 = (bf16[8,3584]{1,0:T(8,128)(2,1)S(1)}, bf16[8,3584]{1,0:T(8,128)(2,1)S(1)}, u32[]{:S(2)}, u32[]{:S(2)}) collective-permute-start(bf16[8,3584]{1,0:T(8,128)(2,1)S(1)} %activate.1.refs_0_), channel_id=1, source_target_pairs={{0,4},{4,0},{8,12},{12,8},{1,5},{5,1},{9,13},{13,9},{2,6},{6,2},{1... | collective-permute-start | bytes 172040 | tf_op jit(solution)/shard_map/ppermute | solution.py:521
  44.8 1.6 %collective-permute-done.14.refs_3_ = bf16[8,3584]{1,0:T(8,128)(2,1)S(1)} collective-permute-done((bf16[8,3584]{1,0:T(8,128)(2,1)S(1)}, bf16[8,3584]{1,0:T(8,128)(2,1)S(1)}, u32[]{:S(2)}, u32[]{:S(2)}) %collective-permute-start.14) | collective-permute-done | bytes 57376 | tf_op jit(solution)/shard_map/ppermute | solution.py:521
  46.4 2.1 %collective-permute-done.13.refs_2_ = bf16[8,3584]{1,0:T(8,128)(2,1)S(1)} collective-permute-done((bf16[8,3584]{1,0:T(8,128)(2,1)S(1)}, bf16[8,3584]{1,0:T(8,128)(2,1)S(1)}, u32[]{:S(2)}, u32[]{:S(2)}) %collective-permute-start.13) | collective-permute-done | bytes 57376 | tf_op jit(solution)/shard_map/ppermute | solution.py:521
  48.5 0.0 collective-permute-done.12.refs_1_
  48.5 0.0 slice-done.10
  48.5 0.0 slice-done.11
  48.5 2.6 %down.1 = (bf16[8,2048]{1,0:T(8,128)(2,1)S(1)}, bf16[8,2048]{1,0:T(8,128)(2,1)S(1)}, bf16[8,2048]{1,0:T(8,128)(2,1)S(1)}, bf16[8,2048]{1,0:T(8,128)(2,1)S(1)}) custom-call(bf16[8,3584]{1,0:T(8,128)(2,1)S(1)} %activate.1.refs_0_, bf16[8,3584]{1,0:T(8,128)(2,1)S(1)} %collective-permute-done.12.refs_1_, bf16[8,3584]{1,0:T(8,128)(2,1)S(1)} %collective-permute-done.13.refs_2_, ...), custom_call_target="tpu_custom_call" | custom-call | tf_op jit(solution)/shard_map/down/pallas_call | solution.py:523
  51.2 0.0 collective-permute-start.15
  51.2 1.4 %collective-permute-start.16 = (bf16[8,2048]{1,0:T(8,128)(2,1)S(1)}, bf16[8,2048]{1,0:T(8,128)(2,1)S(1)}, u32[]{:S(2)}, u32[]{:S(2)}) collective-permute-start(bf16[8,2048]{1,0:T(8,128)(2,1)S(1)} %get-tuple-element.51), channel_id=1, source_target_pairs={{0,2},{1,3},{2,0},{3,1},{4,6},{5,7},{6,4},{7,5},{8,10},{9,11},{10,... | collective-permute-start | bytes 98312 | tf_op jit(solution)/shard_map/ppermute | solution.py:533
  52.5 0.5 collective-permute-start.17
  53.1 1.7 %collective-permute-done.15.refs_1_ = bf16[8,2048]{1,0:T(8,128)(2,1)S(1)} collective-permute-done((bf16[8,2048]{1,0:T(8,128)(2,1)S(1)}, bf16[8,2048]{1,0:T(8,128)(2,1)S(1)}, u32[]{:S(2)}, u32[]{:S(2)}) %collective-permute-start.15) | collective-permute-done | bytes 32800 | tf_op jit(solution)/shard_map/ppermute | solution.py:533
  54.7 0.4 collective-permute-done.16.refs_2_
  55.2 0.0 collective-permute-done.17.refs_3_
  55.2 0.6 %finish.1 = bf16[8,2048]{1,0:T(8,128)(2,1)} custom-call(bf16[2,4,8,1024]{3,2,1,0:T(8,128)(2,1)S(1)} %get-tuple-element.40.mid, bf16[8,2048]{1,0:T(8,128)(2,1)S(1)} %get-tuple-element.49.refs_0_, bf16[8,2048]{1,0:T(8,128)(2,1)S(1)} %collective-permute-done.15.refs_1_, bf16[8,2048]{1,0:T(8,128)(2,1)S(1)} %collective-permute-done.16.refs_2_, ...), custom_call_target="tpu_custom_call" | custom-call | tf_op jit(solution)/shard_map/finish/pallas_call | solution.py:535
  (13 shorter events, 0.1 us)
Async XLA Ops:
  0.0 14.6 %copy-start = (bf16[2,512,2048]{2,1,0:T(8,128)(2,1)S(1)}, bf16[2,512,2048]{2,1,0:T(8,128)(2,1)}, u32[]{:S(2)}) copy-start(bf16[2,512,2048]{2,1,0:T(8,128)(2,1)} %weight.5) | copy-start | bytes 12582916
  0.0 17.1 %slice-start.4 = ((s8[14680064]{0:T(1024)(128)(4,1)}), s8[4194304]{0:T(1024)(128)(4,1)S(1)}, s32[]{:S(2)}) async-start(s8[14680064]{0:T(1024)(128)(4,1)} %bitcast.4), calls=%async_computation.4 | async-start | bytes 8388608
  0.0 17.1 %slice-start.5 = ((s8[14680064]{0:T(1024)(128)(4,1)}), s8[4194304]{0:T(1024)(128)(4,1)S(1)}, s32[]{:S(2)}) async-start(s8[14680064]{0:T(1024)(128)(4,1)} %bitcast.4), calls=%async_computation.5 | async-start | bytes 8388608
  0.0 17.1 %slice-start.6 = ((s8[14680064]{0:T(1024)(128)(4,1)}), s8[4194304]{0:T(1024)(128)(4,1)S(1)}, s32[]{:S(2)}) async-start(s8[14680064]{0:T(1024)(128)(4,1)} %bitcast.4), calls=%async_computation.6 | async-start | bytes 8388608
  3.0 4.4 %collective-permute-start.2 = (bf16[8,512]{1,0:T(8,128)(2,1)S(1)}, bf16[8,512]{1,0:T(8,128)(2,1)S(1)}, u32[]{:S(2)}, u32[]{:S(2)}) collective-permute-start(bf16[8,512]{1,0:T(8,128)(2,1)S(1)} %get-tuple-element.32), channel_id=1, source_target_pairs={{0,5},{1,4},{2,7},{3,6},{4,1},{5,0},{6,3},{7,2},{8,13},{9,12},{10,... | collective-permute-start | bytes 24584 | tf_op jit(solution)/shard_map/ppermute | solution.py:413
  5.5 1.9 %collective-permute-start = (bf16[8,512]{1,0:T(8,128)(2,1)S(1)}, bf16[8,512]{1,0:T(8,128)(2,1)S(1)}, u32[]{:S(2)}, u32[]{:S(2)}) collective-permute-start(bf16[8,512]{1,0:T(8,128)(2,1)S(1)} %get-tuple-element.32), channel_id=1, source_target_pairs={{0,1},{1,0},{2,3},{3,2},{4,5},{5,4},{6,7},{7,6},{8,9},{9,8},{10,11... | collective-permute-start | bytes 24584 | tf_op jit(solution)/shard_map/ppermute | solution.py:413
  6.2 4.0 %collective-permute-start.3 = (bf16[8,512]{1,0:T(8,128)(2,1)S(1)}, bf16[8,512]{1,0:T(8,128)(2,1)S(1)}, u32[]{:S(2)}, u32[]{:S(2)}) collective-permute-start(bf16[8,512]{1,0:T(8,128)(2,1)S(1)} %get-tuple-element.33), channel_id=1, source_target_pairs={{0,7},{1,6},{2,5},{3,4},{4,3},{5,2},{6,1},{7,0},{8,15},{9,14},{10,... | collective-permute-start | bytes 24584 | tf_op jit(solution)/shard_map/ppermute | solution.py:413
  7.2 3.1 %collective-permute-start.1 = (bf16[8,512]{1,0:T(8,128)(2,1)S(1)}, bf16[8,512]{1,0:T(8,128)(2,1)S(1)}, u32[]{:S(2)}, u32[]{:S(2)}) collective-permute-start(bf16[8,512]{1,0:T(8,128)(2,1)S(1)} %get-tuple-element.33), channel_id=1, source_target_pairs={{0,3},{1,2},{2,1},{3,0},{4,7},{5,6},{6,5},{7,4},{8,11},{9,10},{10,... | collective-permute-start | bytes 24584 | tf_op jit(solution)/shard_map/ppermute | solution.py:413
  10.3 4.3 %collective-permute-start.5 = (bf16[4,8,512]{2,1,0:T(8,128)(2,1)S(1)}, bf16[4,8,512]{2,1,0:T(8,128)(2,1)S(1)}, u32[]{:S(2)}, u32[]{:S(2)}) collective-permute-start(bf16[4,8,512]{2,1,0:T(8,128)(2,1)S(1)} %stack.1), channel_id=1, source_target_pairs={{0,9},{1,8},{4,13},{5,12},{8,1},{9,0},{12,5},{13,4},{2,11},{3,10},... | collective-permute-start | bytes 98312 | tf_op jit(solution)/shard_map/ppermute | solution.py:425
  13.0 1.6 %collective-permute-start.4 = (bf16[4,8,512]{2,1,0:T(8,128)(2,1)S(1)}, bf16[4,8,512]{2,1,0:T(8,128)(2,1)S(1)}, u32[]{:S(2)}, u32[]{:S(2)}) collective-permute-start(bf16[4,8,512]{2,1,0:T(8,128)(2,1)S(1)} %stack.1), channel_id=1, source_target_pairs={{0,1},{1,0},{4,5},{5,4},{8,9},{9,8},{12,13},{13,12},{2,3},{3,2},{6... | collective-permute-start | bytes 98312 | tf_op jit(solution)/shard_map/ppermute | solution.py:425
  14.6 2.5 %slice-start.7 = ((s8[14680064]{0:T(1024)(128)(4,1)}), s8[2097152]{0:T(1024)(128)(4,1)S(1)}, s32[]{:S(2)}) async-start(s8[14680064]{0:T(1024)(128)(4,1)} %bitcast.4), calls=%async_computation.7 | async-start | bytes 4194304
  14.6 7.0 %slice-start = ((s8[14680064]{0:T(1024)(128)(4,1)}), s8[4194304]{0:T(1024)(128)(4,1)S(1)}, s32[]{:S(2)}) async-start(s8[14680064]{0:T(1024)(128)(4,1)} %bitcast.2), calls=%async_computation | async-start | bytes 8388608
  14.6 7.0 %slice-start.1 = ((s8[14680064]{0:T(1024)(128)(4,1)}), s8[4194304]{0:T(1024)(128)(4,1)S(1)}, s32[]{:S(2)}) async-start(s8[14680064]{0:T(1024)(128)(4,1)} %bitcast.2), calls=%async_computation.1 | async-start | bytes 8388608
  14.6 7.0 %slice-start.2 = ((s8[14680064]{0:T(1024)(128)(4,1)}), s8[4194304]{0:T(1024)(128)(4,1)S(1)}, s32[]{:S(2)}) async-start(s8[14680064]{0:T(1024)(128)(4,1)} %bitcast.2), calls=%async_computation.2 | async-start | bytes 8388608
  15.6 1.4 %collective-permute-start.6 = (bf16[32,1024]{1,0:T(8,128)(2,1)S(1)}, bf16[32,1024]{1,0:T(8,128)(2,1)S(1)}, u32[]{:S(2)}, u32[]{:S(2)}) collective-permute-start(bf16[32,1024]{1,0:T(8,128)(2,1)S(1)} %get-tuple-element.35), channel_id=1, source_target_pairs={{0,1},{1,0},{2,3},{3,2},{4,5},{5,4},{6,7},{7,6},{8,9},{9,8},{10,11... | collective-permute-start | bytes 196616 | tf_op jit(solution)/shard_map/ppermute | solution.py:440
  17.1 4.5 %slice-start.3 = ((s8[14680064]{0:T(1024)(128)(4,1)}), s8[2097152]{0:T(1024)(128)(4,1)S(1)}, s32[]{:S(2)}) async-start(s8[14680064]{0:T(1024)(128)(4,1)} %bitcast.2), calls=%async_computation.3 | async-start | bytes 4194304
  17.1 4.5 %collective-permute-start.7 = (bf16[32,1024]{1,0:T(8,128)(2,1)S(1)}, bf16[32,1024]{1,0:T(8,128)(2,1)S(1)}, u32[]{:S(2)}, u32[]{:S(2)}) collective-permute-start(bf16[32,1024]{1,0:T(8,128)(2,1)S(1)} %add.1.refs_0_), channel_id=1, source_target_pairs={{0,2},{2,0},{1,3},{3,1},{4,6},{6,4},{5,7},{7,5},{8,10},{10,8},{9,1... | collective-permute-start | bytes 196616 | tf_op jit(solution)/shard_map/ppermute | solution.py:451
  21.6 3.5 %collective-permute-start.8 = (bf16[32,1024]{1,0:T(8,128)(2,1)S(1)}, bf16[32,1024]{1,0:T(8,128)(2,1)S(1)}, u32[]{:S(2)}, u32[]{:S(2)}) collective-permute-start(bf16[32,1024]{1,0:T(8,128)(2,1)S(1)} %get-tuple-element.36.mid.refs_0_), channel_id=1, source_target_pairs={{0,1},{1,0},{2,3},{3,2},{4,5},{5,4},{6,7},{7,6},{8,9},{9,8},{10,11... | collective-permute-start | bytes 196616 | tf_op jit(solution)/shard_map/ppermute | solution.py:465
  25.2 23.4 %slice-start.8 = ((s8[14680064]{0:T(1024)(128)(4,1)}), s8[4194304]{0:T(1024)(128)(4,1)S(1)}, s32[]{:S(2)}) async-start(s8[14680064]{0:T(1024)(128)(4,1)} %bitcast.6), calls=%async_computation.8 | async-start | bytes 8388608
  25.2 23.3 %slice-start.9 = ((s8[14680064]{0:T(1024)(128)(4,1)}), s8[4194304]{0:T(1024)(128)(4,1)S(1)}, s32[]{:S(2)}) async-start(s8[14680064]{0:T(1024)(128)(4,1)} %bitcast.6), calls=%async_computation.9 | async-start | bytes 8388608
  26.5 22.0 %slice-start.10 = ((s8[14680064]{0:T(1024)(128)(4,1)}), s8[4194304]{0:T(1024)(128)(4,1)S(1)}, s32[]{:S(2)}) async-start(s8[14680064]{0:T(1024)(128)(4,1)} %bitcast.6), calls=%async_computation.10 | async-start | bytes 8388608
  26.5 22.0 %slice-start.11 = ((s8[14680064]{0:T(1024)(128)(4,1)}), s8[2097152]{0:T(1024)(128)(4,1)S(1)}, s32[]{:S(2)}) async-start(s8[14680064]{0:T(1024)(128)(4,1)} %bitcast.6), calls=%async_computation.11 | async-start | bytes 4194304
  27.8 7.5 %collective-permute-start.9 = (bf16[8,7296]{1,0:T(8,128)(2,1)S(1)}, bf16[8,7296]{1,0:T(8,128)(2,1)S(1)}, u32[]{:S(2)}, u32[]{:S(2)}) collective-permute-start(bf16[8,7296]{1,0:T(8,128)(2,1)S(1)} %get-tuple-element.46), channel_id=1, source_target_pairs={{0,12},{4,8},{8,4},{12,0},{1,13},{5,9},{9,5},{13,1},{2,14},{6,10},... | collective-permute-start | bytes 350216 | tf_op jit(solution)/shard_map/ppermute | solution.py:511
  31.7 8.5 %collective-permute-start.10 = (bf16[8,7296]{1,0:T(8,128)(2,1)S(1)}, bf16[8,7296]{1,0:T(8,128)(2,1)S(1)}, u32[]{:S(2)}, u32[]{:S(2)}) collective-permute-start(bf16[8,7296]{1,0:T(8,128)(2,1)S(1)} %get-tuple-element.47), channel_id=1, source_target_pairs={{0,8},{4,12},{8,0},{12,4},{1,9},{5,13},{9,1},{13,5},{2,10},{6,14},... | collective-permute-start | bytes 350216 | tf_op jit(solution)/shard_map/ppermute | solution.py:511
  31.7 8.5 %collective-permute-start.11 = (bf16[8,7296]{1,0:T(8,128)(2,1)S(1)}, bf16[8,7296]{1,0:T(8,128)(2,1)S(1)}, u32[]{:S(2)}, u32[]{:S(2)}) collective-permute-start(bf16[8,7296]{1,0:T(8,128)(2,1)S(1)} %get-tuple-element.48), channel_id=1, source_target_pairs={{0,4},{4,0},{8,12},{12,8},{1,5},{5,1},{9,13},{13,9},{2,6},{6,2},{1... | collective-permute-start | bytes 350216 | tf_op jit(solution)/shard_map/ppermute | solution.py:511
  40.4 6.0 %collective-permute-start.14 = (bf16[8,3584]{1,0:T(8,128)(2,1)S(1)}, bf16[8,3584]{1,0:T(8,128)(2,1)S(1)}, u32[]{:S(2)}, u32[]{:S(2)}) collective-permute-start(bf16[8,3584]{1,0:T(8,128)(2,1)S(1)} %activate.1.refs_0_), channel_id=1, source_target_pairs={{0,12},{4,8},{8,4},{12,0},{1,13},{5,9},{9,5},{13,1},{2,14},{6,10},... | collective-permute-start | bytes 172040 | tf_op jit(solution)/shard_map/ppermute | solution.py:521
  43.4 5.1 %collective-permute-start.13 = (bf16[8,3584]{1,0:T(8,128)(2,1)S(1)}, bf16[8,3584]{1,0:T(8,128)(2,1)S(1)}, u32[]{:S(2)}, u32[]{:S(2)}) collective-permute-start(bf16[8,3584]{1,0:T(8,128)(2,1)S(1)} %activate.1.refs_0_), channel_id=1, source_target_pairs={{0,8},{4,12},{8,0},{12,4},{1,9},{5,13},{9,1},{13,5},{2,10},{6,14},... | collective-permute-start | bytes 172040 | tf_op jit(solution)/shard_map/ppermute | solution.py:521
  43.4 5.1 %collective-permute-start.12 = (bf16[8,3584]{1,0:T(8,128)(2,1)S(1)}, bf16[8,3584]{1,0:T(8,128)(2,1)S(1)}, u32[]{:S(2)}, u32[]{:S(2)}) collective-permute-start(bf16[8,3584]{1,0:T(8,128)(2,1)S(1)} %activate.1.refs_0_), channel_id=1, source_target_pairs={{0,4},{4,0},{8,12},{12,8},{1,5},{5,1},{9,13},{13,9},{2,6},{6,2},{1... | collective-permute-start | bytes 172040 | tf_op jit(solution)/shard_map/ppermute | solution.py:521
  51.2 3.6 %collective-permute-start.15 = (bf16[8,2048]{1,0:T(8,128)(2,1)S(1)}, bf16[8,2048]{1,0:T(8,128)(2,1)S(1)}, u32[]{:S(2)}, u32[]{:S(2)}) collective-permute-start(bf16[8,2048]{1,0:T(8,128)(2,1)S(1)} %get-tuple-element.50), channel_id=1, source_target_pairs={{0,3},{1,2},{2,1},{3,0},{4,7},{5,6},{6,5},{7,4},{8,11},{9,10},{10,... | collective-permute-start | bytes 98312 | tf_op jit(solution)/shard_map/ppermute | solution.py:533
  51.2 4.0 %collective-permute-start.16 = (bf16[8,2048]{1,0:T(8,128)(2,1)S(1)}, bf16[8,2048]{1,0:T(8,128)(2,1)S(1)}, u32[]{:S(2)}, u32[]{:S(2)}) collective-permute-start(bf16[8,2048]{1,0:T(8,128)(2,1)S(1)} %get-tuple-element.51), channel_id=1, source_target_pairs={{0,2},{1,3},{2,0},{3,1},{4,6},{5,7},{6,4},{7,5},{8,10},{9,11},{10,... | collective-permute-start | bytes 98312 | tf_op jit(solution)/shard_map/ppermute | solution.py:533
  52.5 2.6 %collective-permute-start.17 = (bf16[8,2048]{1,0:T(8,128)(2,1)S(1)}, bf16[8,2048]{1,0:T(8,128)(2,1)S(1)}, u32[]{:S(2)}, u32[]{:S(2)}) collective-permute-start(bf16[8,2048]{1,0:T(8,128)(2,1)S(1)} %get-tuple-element.52), channel_id=1, source_target_pairs={{0,1},{1,0},{2,3},{3,2},{4,5},{5,4},{6,7},{7,6},{8,9},{9,8},{10,11... | collective-permute-start | bytes 98312 | tf_op jit(solution)/shard_map/ppermute | solution.py:533

commit v6 on v5

--- a/solution.py
+++ b/solution.py
@@ -202,7 +202,7 @@
             )
 
 
-def gate_first(core, residual, gain, weight, *refs):
+def gate_first(core, residual, gain, weight, later, *refs):
     mid, left, sums, ordered = refs[-4:]
     total = residual[lax.axis_index("rep")].astype(F32)
     for ref in refs[:-4]:
@@ -413,14 +413,15 @@
         close[k] = lax.ppermute(
             attended[k % ffn], ("tok", "ffn", "rep"), swap(owners * rep, k * rep + rep - 1)
         )
+    gate_weight = in_vmem(gate_weight)
     close = pl.pallas_call(
         functools.partial(stack, near * ffn),
         out_shape=like(near * ffn, table_rows, feat_width),
-        in_specs=[VMEM] * (near * ffn),
+        in_specs=[VMEM] * (near * ffn + 1),
         out_specs=VMEM,
         compiler_params=limit(3),
         name="stack",
-    )(*close)
+    )(*close, gate_weight)
     gathered = [
         lax.ppermute(close, ("tok", "rep"), swap(tok * rep, k * rep + rep - 1))
         for k in range(0, tok, near)
@@ -439,29 +440,28 @@
     summed = [partials[0]] + [
         lax.ppermute(partials[k], "rep", swap(rep, k)) for k in range(1, rep)
     ]
-    up_weight = in_vmem(up_weight)
     here = pl.pallas_call(
         functools.partial(add, len(summed)),
         out_shape=like(requests, height),
-        in_specs=[VMEM] * (len(summed) + 1),
+        in_specs=[VMEM] * len(summed),
         out_specs=VMEM,
         compiler_params=limit(3),
         name="add",
-    )(*summed, up_weight)
+    )(*summed)
     arrived = [lax.ppermute(here, "ffn", swap(ffn, k)) for k in range(1, ffn)]
-    gate_weight = in_vmem(gate_weight)
     rows = requests // tok
     share = requests // sums
+    up_weight = in_vmem(up_weight)
     own_shapes = [like(requests, height), jax.ShapeDtypeStruct((requests, hidden_here), F32)]
     mid_own, own, own_sums = pl.pallas_call(
         functools.partial(gate_first, rep - 1),
         out_shape=[like(requests, height)] + own_shapes,
-        in_specs=[VMEM] * (3 + ffn),
+        in_specs=[VMEM] * (4 + ffn),
         out_specs=[VMEM] * 3,
         scratch_shapes=[pltpu.VMEM((tok, rows, height), F32)],
         compiler_params=limit(3),
         name="gate_first",
-    )(residual_in, norm_gain, gate_weight, here, *arrived)
+    )(residual_in, norm_gain, gate_weight, up_weight, here, *arrived)
     mids = [mid_own] + [lax.ppermute(mid_own, "rep", swap(rep, k)) for k in range(1, rep)]
     for core in reversed(range(rep - 1)):
         own, own_sums = pl.pallas_call(

time: 56 us -> 55.7 us (level)
  no operation moved by 1% of the time
where the time goes in v6:
time: 55.7 us; the launch traced here: 55.6 us
  waiting for transfers between devices  21.4 us (38%)
  starting transfers between devices  21.3 us (38%)
  Pallas kernels  12.7 us (23%)
    ppermute x3, waiting for transfers between devices, shards(): lax.ppermute(parts[k], 'tok', swap(tok, k))  7.81 us
    ppermute x3, starting transfers between devices, shards(): lax.ppermute(parts[k], 'tok', swap(tok, k))  4.45 us
    ppermute x3, starting transfers between devices, shards(): lax.ppermute(hidden, 'tok', swap(tok, k))  4.45 us
    ppermute x4, starting transfers between devices, shards(): lax.ppermute(attended[k % ffn], ('tok', 'ffn', 'rep'), swap(owners * rep,...  4.43 us
    ppermute x3, waiting for transfers between devices, shards(): lax.ppermute(hidden, 'tok', swap(tok, k))  3.42 us
    pallas_call x1, Pallas kernels, shards(): pl.pallas_call(functools.partial(attend, ffn), out_shape=[like(table_rows...  2.97 us
    ppermute x4, waiting for transfers between devices, shards(): lax.ppermute(attended[k % ffn], ('tok', 'ffn', 'rep'), swap(owners * rep,...  2.86 us
    ppermute x2, starting transfers between devices, shards(): lax.ppermute(close, ('tok', 'rep'), swap(tok * rep, k * rep + rep - 1))  2.77 us
  transfers between devices with their start and end apart: 18, of which 11 were waited for; matrix products, arithmetic and copies ran while one was open for 0% of the time, Pallas kernels for 5%

profile of v6, /device:TPU:0, one launch (start us, length us, event | category | flops | bytes accessed | tf_op | source)
XLA Modules:
  0.0 55.6 jit_solution(1915594126837291712)
XLA Ops:
  0.0 0.0 copy-start
  0.0 3.0 %attend.1 = (bf16[8,512]{1,0:T(8,128)(2,1)S(1)}, bf16[8,512]{1,0:T(8,128)(2,1)S(1)}, s32[1,32]{1,0:T(1,128)S(1)}, bf16[2,32,1024]{2,1,0:T(8,128)(2,1)S(1)}, f32[2,1,1024]{2,1,0:T(1,128)S(1)}) custom-call(s32[4]{0:T(128)} %lens_in.1, bf16[4,2048]{1,0:T(4,128)(2,1)} %queries_in.1, bf16[4,256]{1,0:T(4,128)(2,1)} %new_key_in.1, bf16[4,256]{1,0:T(4,128)(2,1)} %new_value_in.1, ...), custom_call_target="tpu_custom_call" | custom-call | flops 20000000000 | tf_op jit(solution)/shard_map/attend/pallas_call | solution.py:378
  3.0 0.0 copy-start.1
  3.0 2.5 %collective-permute-start.2 = (bf16[8,512]{1,0:T(8,128)(2,1)S(1)}, bf16[8,512]{1,0:T(8,128)(2,1)S(1)}, u32[]{:S(2)}, u32[]{:S(2)}) collective-permute-start(bf16[8,512]{1,0:T(8,128)(2,1)S(1)} %get-tuple-element.32), channel_id=1, source_target_pairs={{0,5},{1,4},{2,7},{3,6},{4,1},{5,0},{6,3},{7,2},{8,13},{9,12},{10,... | collective-permute-start | bytes 24584 | tf_op jit(solution)/shard_map/ppermute | solution.py:413
  5.5 0.7 %collective-permute-start = (bf16[8,512]{1,0:T(8,128)(2,1)S(1)}, bf16[8,512]{1,0:T(8,128)(2,1)S(1)}, u32[]{:S(2)}, u32[]{:S(2)}) collective-permute-start(bf16[8,512]{1,0:T(8,128)(2,1)S(1)} %get-tuple-element.32), channel_id=1, source_target_pairs={{0,1},{1,0},{2,3},{3,2},{4,5},{5,4},{6,7},{7,6},{8,9},{9,8},{10,11... | collective-permute-start | bytes 24584 | tf_op jit(solution)/shard_map/ppermute | solution.py:413
  6.2 1.0 %collective-permute-start.3 = (bf16[8,512]{1,0:T(8,128)(2,1)S(1)}, bf16[8,512]{1,0:T(8,128)(2,1)S(1)}, u32[]{:S(2)}, u32[]{:S(2)}) collective-permute-start(bf16[8,512]{1,0:T(8,128)(2,1)S(1)} %get-tuple-element.33), channel_id=1, source_target_pairs={{0,7},{1,6},{2,5},{3,4},{4,3},{5,2},{6,1},{7,0},{8,15},{9,14},{10,... | collective-permute-start | bytes 24584 | tf_op jit(solution)/shard_map/ppermute | solution.py:413
  7.2 0.2 collective-permute-start.1
  7.4 0.0 collective-permute-done.2.refs_2_
  7.4 0.0 collective-permute-done.refs_0_
  7.4 2.7 %collective-permute-done.3.refs_3_ = bf16[8,512]{1,0:T(8,128)(2,1)S(1)} collective-permute-done((bf16[8,512]{1,0:T(8,128)(2,1)S(1)}, bf16[8,512]{1,0:T(8,128)(2,1)S(1)}, u32[]{:S(2)}, u32[]{:S(2)}) %collective-permute-start.3) | collective-permute-done | bytes 8224 | tf_op jit(solution)/shard_map/ppermute | solution.py:413
  10.2 0.1 collective-permute-done.1.refs_1_
  10.3 0.0 copy-done
  10.3 0.0 slice-start
  10.3 0.0 slice-start.1
  10.3 2.7 %collective-permute-start.5 = (bf16[4,8,512]{2,1,0:T(8,128)(2,1)S(1)}, bf16[4,8,512]{2,1,0:T(8,128)(2,1)S(1)}, u32[]{:S(2)}, u32[]{:S(2)}) collective-permute-start(bf16[4,8,512]{2,1,0:T(8,128)(2,1)S(1)} %stack.1), channel_id=1, source_target_pairs={{0,9},{1,8},{4,13},{5,12},{8,1},{9,0},{12,5},{13,4},{2,11},{3,10},... | collective-permute-start | bytes 98312 | tf_op jit(solution)/shard_map/ppermute | solution.py:426
  13.0 0.0 collective-permute-start.4
  13.1 1.6 %collective-permute-done.5.refs_1_ = bf16[4,8,512]{2,1,0:T(8,128)(2,1)S(1)} collective-permute-done((bf16[4,8,512]{2,1,0:T(8,128)(2,1)S(1)}, bf16[4,8,512]{2,1,0:T(8,128)(2,1)S(1)}, u32[]{:S(2)}, u32[]{:S(2)}) %collective-permute-start.5) | collective-permute-done | bytes 32800 | tf_op jit(solution)/shard_map/ppermute | solution.py:426
  14.6 0.0 collective-permute-done.4.refs_0_
  14.6 0.0 copy-done.1
  14.6 0.0 slice-start.3
  14.7 1.0 %project.1 = (bf16[32,1024]{1,0:T(8,128)(2,1)S(1)}, bf16[32,1024]{1,0:T(8,128)(2,1)S(1)}) custom-call(s32[1,32]{1,0:T(1,128)S(1)} %get-tuple-element.31.slot_of, bf16[2,512,2048]{2,1,0:T(8,128)(2,1)S(1)} %copy-done.1, bf16[4,8,512]{2,1,0:T(8,128)(2,1)S(1)} %collective-permute-done.4.refs_0_, bf16[4,8,512]{2,1,0:T(8,128)(2,1)S(1)} %collective-permute-done.5.refs_1_), custom_call_target="tpu_custom_call" | custom-call | flops 10000000000 | tf_op jit(solution)/shard_map/project/pallas_call | solution.py:430
  15.7 0.5 collective-permute-start.6
  16.2 0.9 %collective-permute-done.6.refs_1_ = bf16[32,1024]{1,0:T(8,128)(2,1)S(1)} collective-permute-done((bf16[32,1024]{1,0:T(8,128)(2,1)S(1)}, bf16[32,1024]{1,0:T(8,128)(2,1)S(1)}, u32[]{:S(2)}, u32[]{:S(2)}) %collective-permute-start.6) | collective-permute-done | bytes 65568 | tf_op jit(solution)/shard_map/ppermute | solution.py:441
  17.1 1.9 %collective-permute-start.7 = (bf16[32,1024]{1,0:T(8,128)(2,1)S(1)}, bf16[32,1024]{1,0:T(8,128)(2,1)S(1)}, u32[]{:S(2)}, u32[]{:S(2)}) collective-permute-start(bf16[32,1024]{1,0:T(8,128)(2,1)S(1)} %add.1.refs_0_), channel_id=1, source_target_pairs={{0,2},{2,0},{1,3},{3,1},{4,6},{6,4},{5,7},{7,5},{8,10},{10,8},{9,1... | collective-permute-start | bytes 196616 | tf_op jit(solution)/shard_map/ppermute | solution.py:451
  19.0 2.6 %collective-permute-done.7.refs_1_ = bf16[32,1024]{1,0:T(8,128)(2,1)S(1)} collective-permute-done((bf16[32,1024]{1,0:T(8,128)(2,1)S(1)}, bf16[32,1024]{1,0:T(8,128)(2,1)S(1)}, u32[]{:S(2)}, u32[]{:S(2)}) %collective-permute-start.7) | collective-permute-done | bytes 65568 | tf_op jit(solution)/shard_map/ppermute | solution.py:451
  21.6 0.0 slice-done
  21.6 0.0 slice-done.1
  21.6 0.0 slice-done.2
  21.6 0.0 slice-done.3
  21.7 0.9 %collective-permute-start.8 = (bf16[32,1024]{1,0:T(8,128)(2,1)S(1)}, bf16[32,1024]{1,0:T(8,128)(2,1)S(1)}, u32[]{:S(2)}, u32[]{:S(2)}) collective-permute-start(bf16[32,1024]{1,0:T(8,128)(2,1)S(1)} %get-tuple-element.36.mid.refs_0_), channel_id=1, source_target_pairs={{0,1},{1,0},{2,3},{3,2},{4,5},{5,4},{6,7},{7,6},{8,9},{9,8},{10,11... | collective-permute-start | bytes 196616 | tf_op jit(solution)/shard_map/ppermute | solution.py:465
  22.6 1.3 %gate_next.1 = (bf16[32,1024]{1,0:T(8,128)(2,1)S(1)}, f32[32,3584]{1,0:T(8,128)S(1)}) custom-call(bf16[32,1024]{1,0:T(8,128)(2,1)S(1)} %get-tuple-element.36.mid.refs_0_, f32[2,1,1024]{2,1,0:T(1,128)S(1)} %get-tuple-element.30.gain.refs_2_, bf16[2048,3584]{1,0:T(8,128)(2,1)S(1)} %copy-done, ...), custom_call_target="tpu_custom_call", output_to_operand_aliasing={{0}: (3, {}), {1}: (4, {})} | custom-call | tf_op jit(solution)/shard_map/gate_next/pallas_call | solution.py:467
  23.9 1.3 %up_own.1.sums = f32[32,3584]{1,0:T(8,128)S(1)} custom-call(bf16[32,1024]{1,0:T(8,128)(2,1)S(1)} %get-tuple-element.41.left, bf16[2048,3584]{1,0:T(8,128)(2,1)S(1)} %bitcast.3), custom_call_target="tpu_custom_call" | custom-call | tf_op jit(solution)/shard_map/up_own/pallas_call | solution.py:477
  25.2 0.0 collective-permute-done.8.refs_1_
  25.2 0.0 slice-start.4
  25.2 0.0 slice-start.5
  25.2 1.3 %gate_rest.1 = (bf16[2,4,8,1024]{3,2,1,0:T(8,128)(2,1)S(1)}, bf16[1,32,1024]{2,1,0:T(8,128)(2,1)S(1)}, bf16[4,8,128]{2,1,0:T(8,128)(2,1)S(1)}, bf16[4,8,3584]{2,1,0:T(8,128)(2,1)S(1)}) custom-call(bf16[32,1024]{1,0:T(8,128)(2,1)S(1)} %get-tuple-element.36.mid.refs_0_, bf16[32,1024]{1,0:T(8,128)(2,1)S(1)} %collective-permute-done.8.refs_1_, ...), custom_call_target="tpu_custom_call" | custom-call | tf_op jit(solution)/shard_map/gate_rest/pallas_call | solution.py:485
  26.5 0.0 slice-start.6
  26.5 0.0 slice-start.7
  26.6 1.3 %up_rest.1 = (bf16[8,7296]{1,0:T(8,128)(2,1)S(1)}, bf16[8,7296]{1,0:T(8,128)(2,1)S(1)}, bf16[8,7296]{1,0:T(8,128)(2,1)S(1)}, bf16[8,7296]{1,0:T(8,128)(2,1)S(1)}) custom-call(f32[32,3584]{1,0:T(8,128)S(1)} %up_own.1.sums, bf16[1,32,1024]{2,1,0:T(8,128)(2,1)S(1)} %get-tuple-element.42.rest, bf16[4,8,128]{2,1,0:T(8,128)(2,1)S(1)} %get-tuple-element.43.stat, ...), custom_call_target="tpu_custom_call" | custom-call | tf_op jit(solution)/shard_map/up_rest/pallas_call | solution.py:502
  27.9 3.4 %collective-permute-start.9 = (bf16[8,7296]{1,0:T(8,128)(2,1)S(1)}, bf16[8,7296]{1,0:T(8,128)(2,1)S(1)}, u32[]{:S(2)}, u32[]{:S(2)}) collective-permute-start(bf16[8,7296]{1,0:T(8,128)(2,1)S(1)} %get-tuple-element.46), channel_id=1, source_target_pairs={{0,12},{4,8},{8,4},{12,0},{1,13},{5,9},{9,5},{13,1},{2,14},{6,10},... | collective-permute-start | bytes 350216 | tf_op jit(solution)/shard_map/ppermute | solution.py:511
  31.3 0.0 collective-permute-start.10
  31.3 1.0 %collective-permute-start.11 = (bf16[8,7296]{1,0:T(8,128)(2,1)S(1)}, bf16[8,7296]{1,0:T(8,128)(2,1)S(1)}, u32[]{:S(2)}, u32[]{:S(2)}) collective-permute-start(bf16[8,7296]{1,0:T(8,128)(2,1)S(1)} %get-tuple-element.48), channel_id=1, source_target_pairs={{0,4},{4,0},{8,12},{12,8},{1,5},{5,1},{9,13},{13,9},{2,6},{6,2},{1... | collective-permute-start | bytes 350216 | tf_op jit(solution)/shard_map/ppermute | solution.py:511
  32.3 2.8 %collective-permute-done.9.refs_1_ = bf16[8,7296]{1,0:T(8,128)(2,1)S(1)} collective-permute-done((bf16[8,7296]{1,0:T(8,128)(2,1)S(1)}, bf16[8,7296]{1,0:T(8,128)(2,1)S(1)}, u32[]{:S(2)}, u32[]{:S(2)}) %collective-permute-start.9) | collective-permute-done | bytes 116768 | tf_op jit(solution)/shard_map/ppermute | solution.py:511
  35.1 5.0 %collective-permute-done.10.refs_2_ = bf16[8,7296]{1,0:T(8,128)(2,1)S(1)} collective-permute-done((bf16[8,7296]{1,0:T(8,128)(2,1)S(1)}, bf16[8,7296]{1,0:T(8,128)(2,1)S(1)}, u32[]{:S(2)}, u32[]{:S(2)}) %collective-permute-start.10) | collective-permute-done | bytes 116768 | tf_op jit(solution)/shard_map/ppermute | solution.py:511
  40.1 0.0 collective-permute-done.11.refs_3_
  40.1 0.2 activate.1.refs_0_
  40.3 2.8 %collective-permute-start.14 = (bf16[8,3584]{1,0:T(8,128)(2,1)S(1)}, bf16[8,3584]{1,0:T(8,128)(2,1)S(1)}, u32[]{:S(2)}, u32[]{:S(2)}) collective-permute-start(bf16[8,3584]{1,0:T(8,128)(2,1)S(1)} %activate.1.refs_0_), channel_id=1, source_target_pairs={{0,12},{4,8},{8,4},{12,0},{1,13},{5,9},{9,5},{13,1},{2,14},{6,10},... | collective-permute-start | bytes 172040 | tf_op jit(solution)/shard_map/ppermute | solution.py:521
  43.1 0.0 collective-permute-start.13
  43.1 1.7 %collective-permute-start.12 = (bf16[8,3584]{1,0:T(8,128)(2,1)S(1)}, bf16[8,3584]{1,0:T(8,128)(2,1)S(1)}, u32[]{:S(2)}, u32[]{:S(2)}) collective-permute-start(bf16[8,3584]{1,0:T(8,128)(2,1)S(1)} %activate.1.refs_0_), channel_id=1, source_target_pairs={{0,4},{4,0},{8,12},{12,8},{1,5},{5,1},{9,13},{13,9},{2,6},{6,2},{1... | collective-permute-start | bytes 172040 | tf_op jit(solution)/shard_map/ppermute | solution.py:521
  44.8 1.6 %collective-permute-done.14.refs_3_ = bf16[8,3584]{1,0:T(8,128)(2,1)S(1)} collective-permute-done((bf16[8,3584]{1,0:T(8,128)(2,1)S(1)}, bf16[8,3584]{1,0:T(8,128)(2,1)S(1)}, u32[]{:S(2)}, u32[]{:S(2)}) %collective-permute-start.14) | collective-permute-done | bytes 57376 | tf_op jit(solution)/shard_map/ppermute | solution.py:521
  46.4 1.8 %collective-permute-done.13.refs_2_ = bf16[8,3584]{1,0:T(8,128)(2,1)S(1)} collective-permute-done((bf16[8,3584]{1,0:T(8,128)(2,1)S(1)}, bf16[8,3584]{1,0:T(8,128)(2,1)S(1)}, u32[]{:S(2)}, u32[]{:S(2)}) %collective-permute-start.13) | collective-permute-done | bytes 57376 | tf_op jit(solution)/shard_map/ppermute | solution.py:521
  48.2 0.0 collective-permute-done.12.refs_1_
  48.2 0.0 slice-done.4
  48.2 0.0 slice-done.5
  48.2 0.0 slice-done.6
  48.2 0.0 slice-done.7
  48.2 2.6 %down.1 = (bf16[8,2048]{1,0:T(8,128)(2,1)S(1)}, bf16[8,2048]{1,0:T(8,128)(2,1)S(1)}, bf16[8,2048]{1,0:T(8,128)(2,1)S(1)}, bf16[8,2048]{1,0:T(8,128)(2,1)S(1)}) custom-call(bf16[8,3584]{1,0:T(8,128)(2,1)S(1)} %activate.1.refs_0_, bf16[8,3584]{1,0:T(8,128)(2,1)S(1)} %collective-permute-done.12.refs_1_, bf16[8,3584]{1,0:T(8,128)(2,1)S(1)} %collective-permute-done.13.refs_2_, ...), custom_call_target="tpu_custom_call" | custom-call | tf_op jit(solution)/shard_map/down/pallas_call | solution.py:523
  50.9 0.0 collective-permute-start.15
  50.9 1.7 %collective-permute-start.16 = (bf16[8,2048]{1,0:T(8,128)(2,1)S(1)}, bf16[8,2048]{1,0:T(8,128)(2,1)S(1)}, u32[]{:S(2)}, u32[]{:S(2)}) collective-permute-start(bf16[8,2048]{1,0:T(8,128)(2,1)S(1)} %get-tuple-element.51), channel_id=1, source_target_pairs={{0,2},{1,3},{2,0},{3,1},{4,6},{5,7},{6,4},{7,5},{8,10},{9,11},{10,... | collective-permute-start | bytes 98312 | tf_op jit(solution)/shard_map/ppermute | solution.py:533
  52.6 0.2 collective-permute-start.17
  52.8 1.7 %collective-permute-done.15.refs_1_ = bf16[8,2048]{1,0:T(8,128)(2,1)S(1)} collective-permute-done((bf16[8,2048]{1,0:T(8,128)(2,1)S(1)}, bf16[8,2048]{1,0:T(8,128)(2,1)S(1)}, u32[]{:S(2)}, u32[]{:S(2)}) %collective-permute-start.15) | collective-permute-done | bytes 32800 | tf_op jit(solution)/shard_map/ppermute | solution.py:533
  54.4 0.5 collective-permute-done.16.refs_2_
  54.9 0.0 collective-permute-done.17.refs_3_
  54.9 0.6 %finish.1 = bf16[8,2048]{1,0:T(8,128)(2,1)} custom-call(bf16[2,4,8,1024]{3,2,1,0:T(8,128)(2,1)S(1)} %get-tuple-element.40.mid, bf16[8,2048]{1,0:T(8,128)(2,1)S(1)} %get-tuple-element.49.refs_0_, bf16[8,2048]{1,0:T(8,128)(2,1)S(1)} %collective-permute-done.15.refs_1_, bf16[8,2048]{1,0:T(8,128)(2,1)S(1)} %collective-permute-done.16.refs_2_, ...), custom_call_target="tpu_custom_call" | custom-call | tf_op jit(solution)/shard_map/finish/pallas_call | solution.py:535
  (6 shorter events, 0.1 us)
Async XLA Ops:
  0.0 10.3 %copy-start = (bf16[2048,3584]{1,0:T(8,128)(2,1)S(1)}, bf16[2048,3584]{1,0:T(8,128)(2,1)}, u32[]{:S(2)}) copy-start(bf16[2048,3584]{1,0:T(8,128)(2,1)} %refs_3_.1) | copy-start | bytes 44040196
  3.0 11.7 %copy-start.1 = (bf16[2,512,2048]{2,1,0:T(8,128)(2,1)S(1)}, bf16[2,512,2048]{2,1,0:T(8,128)(2,1)}, u32[]{:S(2)}) copy-start(bf16[2,512,2048]{2,1,0:T(8,128)(2,1)} %weight.5) | copy-start | bytes 12582916
  3.0 4.4 %collective-permute-start.2 = (bf16[8,512]{1,0:T(8,128)(2,1)S(1)}, bf16[8,512]{1,0:T(8,128)(2,1)S(1)}, u32[]{:S(2)}, u32[]{:S(2)}) collective-permute-start(bf16[8,512]{1,0:T(8,128)(2,1)S(1)} %get-tuple-element.32), channel_id=1, source_target_pairs={{0,5},{1,4},{2,7},{3,6},{4,1},{5,0},{6,3},{7,2},{8,13},{9,12},{10,... | collective-permute-start | bytes 24584 | tf_op jit(solution)/shard_map/ppermute | solution.py:413
  5.5 1.9 %collective-permute-start = (bf16[8,512]{1,0:T(8,128)(2,1)S(1)}, bf16[8,512]{1,0:T(8,128)(2,1)S(1)}, u32[]{:S(2)}, u32[]{:S(2)}) collective-permute-start(bf16[8,512]{1,0:T(8,128)(2,1)S(1)} %get-tuple-element.32), channel_id=1, source_target_pairs={{0,1},{1,0},{2,3},{3,2},{4,5},{5,4},{6,7},{7,6},{8,9},{9,8},{10,11... | collective-permute-start | bytes 24584 | tf_op jit(solution)/shard_map/ppermute | solution.py:413
  6.2 4.0 %collective-permute-start.3 = (bf16[8,512]{1,0:T(8,128)(2,1)S(1)}, bf16[8,512]{1,0:T(8,128)(2,1)S(1)}, u32[]{:S(2)}, u32[]{:S(2)}) collective-permute-start(bf16[8,512]{1,0:T(8,128)(2,1)S(1)} %get-tuple-element.33), channel_id=1, source_target_pairs={{0,7},{1,6},{2,5},{3,4},{4,3},{5,2},{6,1},{7,0},{8,15},{9,14},{10,... | collective-permute-start | bytes 24584 | tf_op jit(solution)/shard_map/ppermute | solution.py:413
  7.2 3.1 %collective-permute-start.1 = (bf16[8,512]{1,0:T(8,128)(2,1)S(1)}, bf16[8,512]{1,0:T(8,128)(2,1)S(1)}, u32[]{:S(2)}, u32[]{:S(2)}) collective-permute-start(bf16[8,512]{1,0:T(8,128)(2,1)S(1)} %get-tuple-element.33), channel_id=1, source_target_pairs={{0,3},{1,2},{2,1},{3,0},{4,7},{5,6},{6,5},{7,4},{8,11},{9,10},{10,... | collective-permute-start | bytes 24584 | tf_op jit(solution)/shard_map/ppermute | solution.py:413
  10.3 11.3 %slice-start = ((s8[14680064]{0:T(1024)(128)(4,1)}), s8[4194304]{0:T(1024)(128)(4,1)S(1)}, s32[]{:S(2)}) async-start(s8[14680064]{0:T(1024)(128)(4,1)} %bitcast.2), calls=%async_computation | async-start | bytes 8388608
  10.3 11.3 %slice-start.1 = ((s8[14680064]{0:T(1024)(128)(4,1)}), s8[4194304]{0:T(1024)(128)(4,1)S(1)}, s32[]{:S(2)}) async-start(s8[14680064]{0:T(1024)(128)(4,1)} %bitcast.2), calls=%async_computation.1 | async-start | bytes 8388608
  10.3 4.3 %collective-permute-start.5 = (bf16[4,8,512]{2,1,0:T(8,128)(2,1)S(1)}, bf16[4,8,512]{2,1,0:T(8,128)(2,1)S(1)}, u32[]{:S(2)}, u32[]{:S(2)}) collective-permute-start(bf16[4,8,512]{2,1,0:T(8,128)(2,1)S(1)} %stack.1), channel_id=1, source_target_pairs={{0,9},{1,8},{4,13},{5,12},{8,1},{9,0},{12,5},{13,4},{2,11},{3,10},... | collective-permute-start | bytes 98312 | tf_op jit(solution)/shard_map/ppermute | solution.py:426
  13.0 1.6 %collective-permute-start.4 = (bf16[4,8,512]{2,1,0:T(8,128)(2,1)S(1)}, bf16[4,8,512]{2,1,0:T(8,128)(2,1)S(1)}, u32[]{:S(2)}, u32[]{:S(2)}) collective-permute-start(bf16[4,8,512]{2,1,0:T(8,128)(2,1)S(1)} %stack.1), channel_id=1, source_target_pairs={{0,1},{1,0},{4,5},{5,4},{8,9},{9,8},{12,13},{13,12},{2,3},{3,2},{6... | collective-permute-start | bytes 98312 | tf_op jit(solution)/shard_map/ppermute | solution.py:426
  14.6 6.9 %slice-start.2 = ((s8[14680064]{0:T(1024)(128)(4,1)}), s8[4194304]{0:T(1024)(128)(4,1)S(1)}, s32[]{:S(2)}) async-start(s8[14680064]{0:T(1024)(128)(4,1)} %bitcast.2), calls=%async_computation.2 | async-start | bytes 8388608
  14.6 6.9 %slice-start.3 = ((s8[14680064]{0:T(1024)(128)(4,1)}), s8[2097152]{0:T(1024)(128)(4,1)S(1)}, s32[]{:S(2)}) async-start(s8[14680064]{0:T(1024)(128)(4,1)} %bitcast.2), calls=%async_computation.3 | async-start | bytes 4194304
  15.7 1.4 %collective-permute-start.6 = (bf16[32,1024]{1,0:T(8,128)(2,1)S(1)}, bf16[32,1024]{1,0:T(8,128)(2,1)S(1)}, u32[]{:S(2)}, u32[]{:S(2)}) collective-permute-start(bf16[32,1024]{1,0:T(8,128)(2,1)S(1)} %get-tuple-element.35), channel_id=1, source_target_pairs={{0,1},{1,0},{2,3},{3,2},{4,5},{5,4},{6,7},{7,6},{8,9},{9,8},{10,11... | collective-permute-start | bytes 196616 | tf_op jit(solution)/shard_map/ppermute | solution.py:441
  17.1 4.5 %collective-permute-start.7 = (bf16[32,1024]{1,0:T(8,128)(2,1)S(1)}, bf16[32,1024]{1,0:T(8,128)(2,1)S(1)}, u32[]{:S(2)}, u32[]{:S(2)}) collective-permute-start(bf16[32,1024]{1,0:T(8,128)(2,1)S(1)} %add.1.refs_0_), channel_id=1, source_target_pairs={{0,2},{2,0},{1,3},{3,1},{4,6},{6,4},{5,7},{7,5},{8,10},{10,8},{9,1... | collective-permute-start | bytes 196616 | tf_op jit(solution)/shard_map/ppermute | solution.py:451
  21.7 3.5 %collective-permute-start.8 = (bf16[32,1024]{1,0:T(8,128)(2,1)S(1)}, bf16[32,1024]{1,0:T(8,128)(2,1)S(1)}, u32[]{:S(2)}, u32[]{:S(2)}) collective-permute-start(bf16[32,1024]{1,0:T(8,128)(2,1)S(1)} %get-tuple-element.36.mid.refs_0_), channel_id=1, source_target_pairs={{0,1},{1,0},{2,3},{3,2},{4,5},{5,4},{6,7},{7,6},{8,9},{9,8},{10,11... | collective-permute-start | bytes 196616 | tf_op jit(solution)/shard_map/ppermute | solution.py:465
  25.2 23.0 %slice-start.4 = ((s8[14680064]{0:T(1024)(128)(4,1)}), s8[4194304]{0:T(1024)(128)(4,1)S(1)}, s32[]{:S(2)}) async-start(s8[14680064]{0:T(1024)(128)(4,1)} %bitcast.4), calls=%async_computation.4 | async-start | bytes 8388608
  25.2 23.0 %slice-start.5 = ((s8[14680064]{0:T(1024)(128)(4,1)}), s8[4194304]{0:T(1024)(128)(4,1)S(1)}, s32[]{:S(2)}) async-start(s8[14680064]{0:T(1024)(128)(4,1)} %bitcast.4), calls=%async_computation.5 | async-start | bytes 8388608
  26.5 21.7 %slice-start.6 = ((s8[14680064]{0:T(1024)(128)(4,1)}), s8[4194304]{0:T(1024)(128)(4,1)S(1)}, s32[]{:S(2)}) async-start(s8[14680064]{0:T(1024)(128)(4,1)} %bitcast.4), calls=%async_computation.6 | async-start | bytes 8388608
  26.5 21.7 %slice-start.7 = ((s8[14680064]{0:T(1024)(128)(4,1)}), s8[2097152]{0:T(1024)(128)(4,1)S(1)}, s32[]{:S(2)}) async-start(s8[14680064]{0:T(1024)(128)(4,1)} %bitcast.4), calls=%async_computation.7 | async-start | bytes 4194304
  27.9 7.2 %collective-permute-start.9 = (bf16[8,7296]{1,0:T(8,128)(2,1)S(1)}, bf16[8,7296]{1,0:T(8,128)(2,1)S(1)}, u32[]{:S(2)}, u32[]{:S(2)}) collective-permute-start(bf16[8,7296]{1,0:T(8,128)(2,1)S(1)} %get-tuple-element.46), channel_id=1, source_target_pairs={{0,12},{4,8},{8,4},{12,0},{1,13},{5,9},{9,5},{13,1},{2,14},{6,10},... | collective-permute-start | bytes 350216 | tf_op jit(solution)/shard_map/ppermute | solution.py:511
  31.3 8.8 %collective-permute-start.10 = (bf16[8,7296]{1,0:T(8,128)(2,1)S(1)}, bf16[8,7296]{1,0:T(8,128)(2,1)S(1)}, u32[]{:S(2)}, u32[]{:S(2)}) collective-permute-start(bf16[8,7296]{1,0:T(8,128)(2,1)S(1)} %get-tuple-element.47), channel_id=1, source_target_pairs={{0,8},{4,12},{8,0},{12,4},{1,9},{5,13},{9,1},{13,5},{2,10},{6,14},... | collective-permute-start | bytes 350216 | tf_op jit(solution)/shard_map/ppermute | solution.py:511
  31.3 8.8 %collective-permute-start.11 = (bf16[8,7296]{1,0:T(8,128)(2,1)S(1)}, bf16[8,7296]{1,0:T(8,128)(2,1)S(1)}, u32[]{:S(2)}, u32[]{:S(2)}) collective-permute-start(bf16[8,7296]{1,0:T(8,128)(2,1)S(1)} %get-tuple-element.48), channel_id=1, source_target_pairs={{0,4},{4,0},{8,12},{12,8},{1,5},{5,1},{9,13},{13,9},{2,6},{6,2},{1... | collective-permute-start | bytes 350216 | tf_op jit(solution)/shard_map/ppermute | solution.py:511
  40.3 6.0 %collective-permute-start.14 = (bf16[8,3584]{1,0:T(8,128)(2,1)S(1)}, bf16[8,3584]{1,0:T(8,128)(2,1)S(1)}, u32[]{:S(2)}, u32[]{:S(2)}) collective-permute-start(bf16[8,3584]{1,0:T(8,128)(2,1)S(1)} %activate.1.refs_0_), channel_id=1, source_target_pairs={{0,12},{4,8},{8,4},{12,0},{1,13},{5,9},{9,5},{13,1},{2,14},{6,10},... | collective-permute-start | bytes 172040 | tf_op jit(solution)/shard_map/ppermute | solution.py:521
  43.1 5.1 %collective-permute-start.13 = (bf16[8,3584]{1,0:T(8,128)(2,1)S(1)}, bf16[8,3584]{1,0:T(8,128)(2,1)S(1)}, u32[]{:S(2)}, u32[]{:S(2)}) collective-permute-start(bf16[8,3584]{1,0:T(8,128)(2,1)S(1)} %activate.1.refs_0_), channel_id=1, source_target_pairs={{0,8},{4,12},{8,0},{12,4},{1,9},{5,13},{9,1},{13,5},{2,10},{6,14},... | collective-permute-start | bytes 172040 | tf_op jit(solution)/shard_map/ppermute | solution.py:521
  43.1 5.1 %collective-permute-start.12 = (bf16[8,3584]{1,0:T(8,128)(2,1)S(1)}, bf16[8,3584]{1,0:T(8,128)(2,1)S(1)}, u32[]{:S(2)}, u32[]{:S(2)}) collective-permute-start(bf16[8,3584]{1,0:T(8,128)(2,1)S(1)} %activate.1.refs_0_), channel_id=1, source_target_pairs={{0,4},{4,0},{8,12},{12,8},{1,5},{5,1},{9,13},{13,9},{2,6},{6,2},{1... | collective-permute-start | bytes 172040 | tf_op jit(solution)/shard_map/ppermute | solution.py:521
  50.9 3.5 %collective-permute-start.15 = (bf16[8,2048]{1,0:T(8,128)(2,1)S(1)}, bf16[8,2048]{1,0:T(8,128)(2,1)S(1)}, u32[]{:S(2)}, u32[]{:S(2)}) collective-permute-start(bf16[8,2048]{1,0:T(8,128)(2,1)S(1)} %get-tuple-element.50), channel_id=1, source_target_pairs={{0,3},{1,2},{2,1},{3,0},{4,7},{5,6},{6,5},{7,4},{8,11},{9,10},{10,... | collective-permute-start | bytes 98312 | tf_op jit(solution)/shard_map/ppermute | solution.py:533
  50.9 4.0 %collective-permute-start.16 = (bf16[8,2048]{1,0:T(8,128)(2,1)S(1)}, bf16[8,2048]{1,0:T(8,128)(2,1)S(1)}, u32[]{:S(2)}, u32[]{:S(2)}) collective-permute-start(bf16[8,2048]{1,0:T(8,128)(2,1)S(1)} %get-tuple-element.51), channel_id=1, source_target_pairs={{0,2},{1,3},{2,0},{3,1},{4,6},{5,7},{6,4},{7,5},{8,10},{9,11},{10,... | collective-permute-start | bytes 98312 | tf_op jit(solution)/shard_map/ppermute | solution.py:533
  52.6 2.4 %collective-permute-start.17 = (bf16[8,2048]{1,0:T(8,128)(2,1)S(1)}, bf16[8,2048]{1,0:T(8,128)(2,1)S(1)}, u32[]{:S(2)}, u32[]{:S(2)}) collective-permute-start(bf16[8,2048]{1,0:T(8,128)(2,1)S(1)} %get-tuple-element.52), channel_id=1, source_target_pairs={{0,1},{1,0},{2,3},{3,2},{4,5},{5,4},{6,7},{7,6},{8,9},{9,8},{10,11... | collective-permute-start | bytes 98312 | tf_op jit(solution)/shard_map/ppermute | solution.py:533

commit v7 on v6

--- a/solution.py
+++ b/solution.py
@@ -140,7 +140,7 @@
 
 
 def project(slots, peers, slot_of, weight, *refs):
-    refs, outs, parts = refs[: -1 - peers], refs[-1 - peers : -1], refs[-1]
+    refs, outs, table_out = refs[:-peers], refs[-peers:-1], refs[-1]
     requests = slot_of.shape[1]
     _, rows, width = refs[0].shape
     kv_here = weight.shape[0]
@@ -150,28 +150,25 @@
     mine = lax.axis_index(("tok", "ffn"))
     where_from = ((slot // slots) ^ mine) * rows + lax.rem(slot, slots)
     row = lax.broadcasted_iota(jnp.int32, (table.shape[0], requests), 0)
-    ordered = []
     for g in range(kv_here):
         pick = (row == where_from + g * slots).astype(F32).astype(BF16)
-        ordered.append(
-            lax.dot_general(
-                pick, table, (((0,), (0,)), ((), ())), preferred_element_type=F32
-            ).astype(BF16)
-        )
-    width = parts.shape[2]
+        table_out[g] = lax.dot_general(
+            pick, table, (((0,), (0,)), ((), ())), preferred_element_type=F32
+        ).astype(BF16)
+    for p, out in enumerate(outs):
+        project_part(p + 1, table_out, weight, out)
+
+
+def project_part(peer, ordered, weight, out):
+    width = out.shape[1]
     step = column_step(width)
-    for p in range(peers):
-        for c in range(0, width, step):
-            at = p * width + c
-            total = jnp.zeros((requests, step), F32)
-            for g in range(kv_here):
-                total += jnp.dot(
-                    ordered[g], weight[g, :, at : at + step], preferred_element_type=F32
-                )
-            parts[p, :, c : c + step] = total
-    core = lax.axis_index("rep")
-    for p, out in enumerate(outs):
-        out[...] = parts[core ^ p].astype(BF16)
+    first = (lax.axis_index("rep") ^ peer) * width
+    for c in range(0, width, step):
+        at = pl.ds(pl.multiple_of(first + c, 128), step)
+        total = jnp.zeros((out.shape[0], step), F32)
+        for g in range(weight.shape[0]):
+            total += jnp.dot(ordered[g], weight[g, :, at], preferred_element_type=F32)
+        out[:, c : c + step] = total.astype(BF16)
 
 
 def by_owner(value, ordered):
@@ -427,19 +424,25 @@
         for k in range(0, tok, near)
     ]
 
-    partials = pl.pallas_call(
+    *given, ordered = pl.pallas_call(
         functools.partial(project, slots, rep),
-        out_shape=[like(requests, height)] * rep,
+        out_shape=[like(requests, height)] * (rep - 1) + [like(kv_here, requests, feat_width)],
         in_specs=[VMEM] * (2 + len(gathered)),
         out_specs=[VMEM] * rep,
-        scratch_shapes=[pltpu.VMEM((rep, requests, height), F32)],
         compiler_params=limit(3),
         cost_estimate=pl.CostEstimate(flops=10000000000, transcendentals=0, bytes_accessed=0),
         name="project",
     )(slot_of, out_weight, *gathered)
-    summed = [partials[0]] + [
-        lax.ppermute(partials[k], "rep", swap(rep, k)) for k in range(1, rep)
-    ]
+    summed = [lax.ppermute(part, "rep", swap(rep, k + 1)) for k, part in enumerate(given)]
+    kept = pl.pallas_call(
+        functools.partial(project_part, 0),
+        out_shape=like(requests, height),
+        in_specs=[VMEM] * 2,
+        out_specs=VMEM,
+        compiler_params=limit(3),
+        name="project_own",
+    )(ordered, out_weight)
+    summed = [kept] + summed
     here = pl.pallas_call(
         functools.partial(add, len(summed)),
         out_shape=like(requests, height),

time: 55.7 us -> 55.3 us (level)
  no operation moved by 1% of the time
where the time goes in v7:
time: 55.3 us; the launch traced here: 55.2 us
  starting transfers between devices  21.2 us (38%)
  waiting for transfers between devices  20.9 us (38%)
  Pallas kernels  12.8 us (23%)
    ppermute x3, waiting for transfers between devices, shards(): lax.ppermute(parts[k], 'tok', swap(tok, k))  7.81 us
    ppermute x3, starting transfers between devices, shards(): lax.ppermute(hidden, 'tok', swap(tok, k))  4.45 us
    ppermute x3, starting transfers between devices, shards(): lax.ppermute(parts[k], 'tok', swap(tok, k))  4.45 us
    ppermute x4, starting transfers between devices, shards(): lax.ppermute(attended[k % ffn], ('tok', 'ffn', 'rep'), swap(owners * rep,...  4.43 us
    ppermute x3, waiting for transfers between devices, shards(): lax.ppermute(hidden, 'tok', swap(tok, k))  3.42 us
    pallas_call x1, Pallas kernels, shards(): pl.pallas_call(functools.partial(attend, ffn), out_shape=[like(table_rows...  2.97 us
    ppermute x4, waiting for transfers between devices, shards(): lax.ppermute(attended[k % ffn], ('tok', 'ffn', 'rep'), swap(owners * rep,...  2.86 us
    ppermute x2, starting transfers between devices, shards(): lax.ppermute(close, ('tok', 'rep'), swap(tok * rep, k * rep + rep - 1))  2.77 us
  transfers between devices with their start and end apart: 18, of which 11 were waited for; matrix products, arithmetic and copies ran while one was open for 0% of the time, Pallas kernels for 5%

profile of v7, /device:TPU:0, one launch (start us, length us, event | category | flops | bytes accessed | tf_op | source)
XLA Modules:
  0.0 55.2 jit_solution(11878369740210534445)
XLA Ops:
  0.0 0.0 copy-start
  0.0 3.0 %attend.1 = (bf16[8,512]{1,0:T(8,128)(2,1)S(1)}, bf16[8,512]{1,0:T(8,128)(2,1)S(1)}, s32[1,32]{1,0:T(1,128)S(1)}, bf16[2,32,1024]{2,1,0:T(8,128)(2,1)S(1)}, f32[2,1,1024]{2,1,0:T(1,128)S(1)}) custom-call(s32[4]{0:T(128)} %lens_in.1, bf16[4,2048]{1,0:T(4,128)(2,1)} %queries_in.1, bf16[4,256]{1,0:T(4,128)(2,1)} %new_key_in.1, bf16[4,256]{1,0:T(4,128)(2,1)} %new_value_in.1, ...), custom_call_target="tpu_custom_call" | custom-call | flops 20000000000 | tf_op jit(solution)/shard_map/attend/pallas_call | solution.py:375
  3.0 0.0 copy-start.1
  3.0 2.5 %collective-permute-start.2 = (bf16[8,512]{1,0:T(8,128)(2,1)S(1)}, bf16[8,512]{1,0:T(8,128)(2,1)S(1)}, u32[]{:S(2)}, u32[]{:S(2)}) collective-permute-start(bf16[8,512]{1,0:T(8,128)(2,1)S(1)} %get-tuple-element.32), channel_id=1, source_target_pairs={{0,5},{1,4},{2,7},{3,6},{4,1},{5,0},{6,3},{7,2},{8,13},{9,12},{10,... | collective-permute-start | bytes 24584 | tf_op jit(solution)/shard_map/ppermute | solution.py:410
  5.5 0.7 %collective-permute-start = (bf16[8,512]{1,0:T(8,128)(2,1)S(1)}, bf16[8,512]{1,0:T(8,128)(2,1)S(1)}, u32[]{:S(2)}, u32[]{:S(2)}) collective-permute-start(bf16[8,512]{1,0:T(8,128)(2,1)S(1)} %get-tuple-element.32), channel_id=1, source_target_pairs={{0,1},{1,0},{2,3},{3,2},{4,5},{5,4},{6,7},{7,6},{8,9},{9,8},{10,11... | collective-permute-start | bytes 24584 | tf_op jit(solution)/shard_map/ppermute | solution.py:410
  6.2 1.0 %collective-permute-start.3 = (bf16[8,512]{1,0:T(8,128)(2,1)S(1)}, bf16[8,512]{1,0:T(8,128)(2,1)S(1)}, u32[]{:S(2)}, u32[]{:S(2)}) collective-permute-start(bf16[8,512]{1,0:T(8,128)(2,1)S(1)} %get-tuple-element.33), channel_id=1, source_target_pairs={{0,7},{1,6},{2,5},{3,4},{4,3},{5,2},{6,1},{7,0},{8,15},{9,14},{10,... | collective-permute-start | bytes 24584 | tf_op jit(solution)/shard_map/ppermute | solution.py:410
  7.2 0.2 collective-permute-start.1
  7.4 0.0 collective-permute-done.2.refs_2_
  7.4 0.0 collective-permute-done.refs_0_
  7.4 2.7 %collective-permute-done.3.refs_3_ = bf16[8,512]{1,0:T(8,128)(2,1)S(1)} collective-permute-done((bf16[8,512]{1,0:T(8,128)(2,1)S(1)}, bf16[8,512]{1,0:T(8,128)(2,1)S(1)}, u32[]{:S(2)}, u32[]{:S(2)}) %collective-permute-start.3) | collective-permute-done | bytes 8224 | tf_op jit(solution)/shard_map/ppermute | solution.py:410
  10.2 0.1 collective-permute-done.1.refs_1_
  10.3 0.0 copy-done
  10.3 0.0 slice-start
  10.3 2.7 %collective-permute-start.5 = (bf16[4,8,512]{2,1,0:T(8,128)(2,1)S(1)}, bf16[4,8,512]{2,1,0:T(8,128)(2,1)S(1)}, u32[]{:S(2)}, u32[]{:S(2)}) collective-permute-start(bf16[4,8,512]{2,1,0:T(8,128)(2,1)S(1)} %stack.1), channel_id=1, source_target_pairs={{0,9},{1,8},{4,13},{5,12},{8,1},{9,0},{12,5},{13,4},{2,11},{3,10},... | collective-permute-start | bytes 98312 | tf_op jit(solution)/shard_map/ppermute | solution.py:423
  13.0 0.0 collective-permute-start.4
  13.1 1.6 %collective-permute-done.5.refs_1_ = bf16[4,8,512]{2,1,0:T(8,128)(2,1)S(1)} collective-permute-done((bf16[4,8,512]{2,1,0:T(8,128)(2,1)S(1)}, bf16[4,8,512]{2,1,0:T(8,128)(2,1)S(1)}, u32[]{:S(2)}, u32[]{:S(2)}) %collective-permute-start.5) | collective-permute-done | bytes 32800 | tf_op jit(solution)/shard_map/ppermute | solution.py:423
  14.6 0.0 collective-permute-done.4.refs_0_
  14.6 0.0 copy-done.1
  14.6 0.0 slice-start.3
  14.7 0.6 %project.1 = (bf16[32,1024]{1,0:T(8,128)(2,1)S(1)}, bf16[2,32,512]{2,1,0:T(8,128)(2,1)S(1)}) custom-call(s32[1,32]{1,0:T(1,128)S(1)} %get-tuple-element.31.slot_of, bf16[2,512,2048]{2,1,0:T(8,128)(2,1)S(1)} %copy-done.1, bf16[4,8,512]{2,1,0:T(8,128)(2,1)S(1)} %collective-permute-done.4.refs_0_, bf16[4,8,512]{2,1,0:T(8,128)(2,1)S(1)} %collective-permute-done.5.refs_1_), custom_call_target="tpu_custom_call" | custom-call | flops 10000000000 | tf_op jit(solution)/shard_map/project/pallas_call | solution.py:427
  15.3 0.5 collective-permute-start.6
  15.8 0.5 project_own.1.refs_0_
  16.2 0.4 collective-permute-done.6.refs_1_
  16.7 1.9 %collective-permute-start.7 = (bf16[32,1024]{1,0:T(8,128)(2,1)S(1)}, bf16[32,1024]{1,0:T(8,128)(2,1)S(1)}, u32[]{:S(2)}, u32[]{:S(2)}) collective-permute-start(bf16[32,1024]{1,0:T(8,128)(2,1)S(1)} %add.1.refs_0_), channel_id=1, source_target_pairs={{0,2},{2,0},{1,3},{3,1},{4,6},{6,4},{5,7},{7,5},{8,10},{10,8},{9,1... | collective-permute-start | bytes 196616 | tf_op jit(solution)/shard_map/ppermute | solution.py:454
  18.5 2.6 %collective-permute-done.7.refs_1_ = bf16[32,1024]{1,0:T(8,128)(2,1)S(1)} collective-permute-done((bf16[32,1024]{1,0:T(8,128)(2,1)S(1)}, bf16[32,1024]{1,0:T(8,128)(2,1)S(1)}, u32[]{:S(2)}, u32[]{:S(2)}) %collective-permute-start.7) | collective-permute-done | bytes 65568 | tf_op jit(solution)/shard_map/ppermute | solution.py:454
  21.1 0.0 slice-done
  21.1 0.0 slice-done.1
  21.1 0.0 slice-done.2
  21.2 0.0 slice-done.3
  21.2 0.9 %collective-permute-start.8 = (bf16[32,1024]{1,0:T(8,128)(2,1)S(1)}, bf16[32,1024]{1,0:T(8,128)(2,1)S(1)}, u32[]{:S(2)}, u32[]{:S(2)}) collective-permute-start(bf16[32,1024]{1,0:T(8,128)(2,1)S(1)} %get-tuple-element.36.mid.refs_0_), channel_id=1, source_target_pairs={{0,1},{1,0},{2,3},{3,2},{4,5},{5,4},{6,7},{7,6},{8,9},{9,8},{10,11... | collective-permute-start | bytes 196616 | tf_op jit(solution)/shard_map/ppermute | solution.py:468
  22.2 1.3 %gate_next.1 = (bf16[32,1024]{1,0:T(8,128)(2,1)S(1)}, f32[32,3584]{1,0:T(8,128)S(1)}) custom-call(bf16[32,1024]{1,0:T(8,128)(2,1)S(1)} %get-tuple-element.36.mid.refs_0_, f32[2,1,1024]{2,1,0:T(1,128)S(1)} %get-tuple-element.30.gain.refs_2_, bf16[2048,3584]{1,0:T(8,128)(2,1)S(1)} %copy-done, ...), custom_call_target="tpu_custom_call", output_to_operand_aliasing={{0}: (3, {}), {1}: (4, {})} | custom-call | tf_op jit(solution)/shard_map/gate_next/pallas_call | solution.py:470
  23.4 1.3 %up_own.1.sums = f32[32,3584]{1,0:T(8,128)S(1)} custom-call(bf16[32,1024]{1,0:T(8,128)(2,1)S(1)} %get-tuple-element.41.left, bf16[2048,3584]{1,0:T(8,128)(2,1)S(1)} %bitcast.3), custom_call_target="tpu_custom_call" | custom-call | tf_op jit(solution)/shard_map/up_own/pallas_call | solution.py:480
  24.7 0.0 collective-permute-done.8.refs_1_
  24.7 0.0 slice-start.4
  24.8 0.0 slice-start.5
  24.8 1.3 %gate_rest.1 = (bf16[2,4,8,1024]{3,2,1,0:T(8,128)(2,1)S(1)}, bf16[1,32,1024]{2,1,0:T(8,128)(2,1)S(1)}, bf16[4,8,128]{2,1,0:T(8,128)(2,1)S(1)}, bf16[4,8,3584]{2,1,0:T(8,128)(2,1)S(1)}) custom-call(bf16[32,1024]{1,0:T(8,128)(2,1)S(1)} %get-tuple-element.36.mid.refs_0_, bf16[32,1024]{1,0:T(8,128)(2,1)S(1)} %collective-permute-done.8.refs_1_, ...), custom_call_target="tpu_custom_call" | custom-call | tf_op jit(solution)/shard_map/gate_rest/pallas_call | solution.py:488
  26.1 0.0 slice-start.6
  26.1 0.0 slice-start.7
  26.1 1.3 %up_rest.1 = (bf16[8,7296]{1,0:T(8,128)(2,1)S(1)}, bf16[8,7296]{1,0:T(8,128)(2,1)S(1)}, bf16[8,7296]{1,0:T(8,128)(2,1)S(1)}, bf16[8,7296]{1,0:T(8,128)(2,1)S(1)}) custom-call(f32[32,3584]{1,0:T(8,128)S(1)} %up_own.1.sums, bf16[1,32,1024]{2,1,0:T(8,128)(2,1)S(1)} %get-tuple-element.42.rest, bf16[4,8,128]{2,1,0:T(8,128)(2,1)S(1)} %get-tuple-element.43.stat, ...), custom_call_target="tpu_custom_call" | custom-call | tf_op jit(solution)/shard_map/up_rest/pallas_call | solution.py:505
  27.4 3.4 %collective-permute-start.9 = (bf16[8,7296]{1,0:T(8,128)(2,1)S(1)}, bf16[8,7296]{1,0:T(8,128)(2,1)S(1)}, u32[]{:S(2)}, u32[]{:S(2)}) collective-permute-start(bf16[8,7296]{1,0:T(8,128)(2,1)S(1)} %get-tuple-element.46), channel_id=1, source_target_pairs={{0,12},{4,8},{8,4},{12,0},{1,13},{5,9},{9,5},{13,1},{2,14},{6,10},... | collective-permute-start | bytes 350216 | tf_op jit(solution)/shard_map/ppermute | solution.py:514
  30.9 0.0 collective-permute-start.10
  30.9 1.0 %collective-permute-start.11 = (bf16[8,7296]{1,0:T(8,128)(2,1)S(1)}, bf16[8,7296]{1,0:T(8,128)(2,1)S(1)}, u32[]{:S(2)}, u32[]{:S(2)}) collective-permute-start(bf16[8,7296]{1,0:T(8,128)(2,1)S(1)} %get-tuple-element.48), channel_id=1, source_target_pairs={{0,4},{4,0},{8,12},{12,8},{1,5},{5,1},{9,13},{13,9},{2,6},{6,2},{1... | collective-permute-start | bytes 350216 | tf_op jit(solution)/shard_map/ppermute | solution.py:514
  31.9 2.8 %collective-permute-done.9.refs_1_ = bf16[8,7296]{1,0:T(8,128)(2,1)S(1)} collective-permute-done((bf16[8,7296]{1,0:T(8,128)(2,1)S(1)}, bf16[8,7296]{1,0:T(8,128)(2,1)S(1)}, u32[]{:S(2)}, u32[]{:S(2)}) %collective-permute-start.9) | collective-permute-done | bytes 116768 | tf_op jit(solution)/shard_map/ppermute | solution.py:514
  34.7 5.0 %collective-permute-done.10.refs_2_ = bf16[8,7296]{1,0:T(8,128)(2,1)S(1)} collective-permute-done((bf16[8,7296]{1,0:T(8,128)(2,1)S(1)}, bf16[8,7296]{1,0:T(8,128)(2,1)S(1)}, u32[]{:S(2)}, u32[]{:S(2)}) %collective-permute-start.10) | collective-permute-done | bytes 116768 | tf_op jit(solution)/shard_map/ppermute | solution.py:514
  39.7 0.0 collective-permute-done.11.refs_3_
  39.7 0.2 activate.1.refs_0_
  39.9 2.8 %collective-permute-start.14 = (bf16[8,3584]{1,0:T(8,128)(2,1)S(1)}, bf16[8,3584]{1,0:T(8,128)(2,1)S(1)}, u32[]{:S(2)}, u32[]{:S(2)}) collective-permute-start(bf16[8,3584]{1,0:T(8,128)(2,1)S(1)} %activate.1.refs_0_), channel_id=1, source_target_pairs={{0,12},{4,8},{8,4},{12,0},{1,13},{5,9},{9,5},{13,1},{2,14},{6,10},... | collective-permute-start | bytes 172040 | tf_op jit(solution)/shard_map/ppermute | solution.py:524
  42.7 0.0 collective-permute-start.13
  42.7 1.7 %collective-permute-start.12 = (bf16[8,3584]{1,0:T(8,128)(2,1)S(1)}, bf16[8,3584]{1,0:T(8,128)(2,1)S(1)}, u32[]{:S(2)}, u32[]{:S(2)}) collective-permute-start(bf16[8,3584]{1,0:T(8,128)(2,1)S(1)} %activate.1.refs_0_), channel_id=1, source_target_pairs={{0,4},{4,0},{8,12},{12,8},{1,5},{5,1},{9,13},{13,9},{2,6},{6,2},{1... | collective-permute-start | bytes 172040 | tf_op jit(solution)/shard_map/ppermute | solution.py:524
  44.3 1.6 %collective-permute-done.14.refs_3_ = bf16[8,3584]{1,0:T(8,128)(2,1)S(1)} collective-permute-done((bf16[8,3584]{1,0:T(8,128)(2,1)S(1)}, bf16[8,3584]{1,0:T(8,128)(2,1)S(1)}, u32[]{:S(2)}, u32[]{:S(2)}) %collective-permute-start.14) | collective-permute-done | bytes 57376 | tf_op jit(solution)/shard_map/ppermute | solution.py:524
  45.9 1.8 %collective-permute-done.13.refs_2_ = bf16[8,3584]{1,0:T(8,128)(2,1)S(1)} collective-permute-done((bf16[8,3584]{1,0:T(8,128)(2,1)S(1)}, bf16[8,3584]{1,0:T(8,128)(2,1)S(1)}, u32[]{:S(2)}, u32[]{:S(2)}) %collective-permute-start.13) | collective-permute-done | bytes 57376 | tf_op jit(solution)/shard_map/ppermute | solution.py:524
  47.8 0.0 collective-permute-done.12.refs_1_
  47.8 0.0 slice-done.4
  47.8 0.0 slice-done.5
  47.8 0.0 slice-done.6
  47.8 0.0 slice-done.7
  47.8 2.6 %down.1 = (bf16[8,2048]{1,0:T(8,128)(2,1)S(1)}, bf16[8,2048]{1,0:T(8,128)(2,1)S(1)}, bf16[8,2048]{1,0:T(8,128)(2,1)S(1)}, bf16[8,2048]{1,0:T(8,128)(2,1)S(1)}) custom-call(bf16[8,3584]{1,0:T(8,128)(2,1)S(1)} %activate.1.refs_0_, bf16[8,3584]{1,0:T(8,128)(2,1)S(1)} %collective-permute-done.12.refs_1_, bf16[8,3584]{1,0:T(8,128)(2,1)S(1)} %collective-permute-done.13.refs_2_, ...), custom_call_target="tpu_custom_call" | custom-call | tf_op jit(solution)/shard_map/down/pallas_call | solution.py:526
  50.4 0.0 collective-permute-start.15
  50.5 1.7 %collective-permute-start.16 = (bf16[8,2048]{1,0:T(8,128)(2,1)S(1)}, bf16[8,2048]{1,0:T(8,128)(2,1)S(1)}, u32[]{:S(2)}, u32[]{:S(2)}) collective-permute-start(bf16[8,2048]{1,0:T(8,128)(2,1)S(1)} %get-tuple-element.51), channel_id=1, source_target_pairs={{0,2},{1,3},{2,0},{3,1},{4,6},{5,7},{6,4},{7,5},{8,10},{9,11},{10,... | collective-permute-start | bytes 98312 | tf_op jit(solution)/shard_map/ppermute | solution.py:536
  52.1 0.2 collective-permute-start.17
  52.3 1.7 %collective-permute-done.15.refs_1_ = bf16[8,2048]{1,0:T(8,128)(2,1)S(1)} collective-permute-done((bf16[8,2048]{1,0:T(8,128)(2,1)S(1)}, bf16[8,2048]{1,0:T(8,128)(2,1)S(1)}, u32[]{:S(2)}, u32[]{:S(2)}) %collective-permute-start.15) | collective-permute-done | bytes 32800 | tf_op jit(solution)/shard_map/ppermute | solution.py:536
  54.0 0.5 collective-permute-done.16.refs_2_
  54.5 0.0 collective-permute-done.17.refs_3_
  54.5 0.6 %finish.1 = bf16[8,2048]{1,0:T(8,128)(2,1)} custom-call(bf16[2,4,8,1024]{3,2,1,0:T(8,128)(2,1)S(1)} %get-tuple-element.40.mid, bf16[8,2048]{1,0:T(8,128)(2,1)S(1)} %get-tuple-element.49.refs_0_, bf16[8,2048]{1,0:T(8,128)(2,1)S(1)} %collective-permute-done.15.refs_1_, bf16[8,2048]{1,0:T(8,128)(2,1)S(1)} %collective-permute-done.16.refs_2_, ...), custom_call_target="tpu_custom_call" | custom-call | tf_op jit(solution)/shard_map/finish/pallas_call | solution.py:538
  (7 shorter events, 0.1 us)
Async XLA Ops:
  0.0 10.3 %copy-start = (bf16[2048,3584]{1,0:T(8,128)(2,1)S(1)}, bf16[2048,3584]{1,0:T(8,128)(2,1)}, u32[]{:S(2)}) copy-start(bf16[2048,3584]{1,0:T(8,128)(2,1)} %refs_3_.1) | copy-start | bytes 44040196
  3.0 11.7 %copy-start.1 = (bf16[2,512,2048]{2,1,0:T(8,128)(2,1)S(1)}, bf16[2,512,2048]{2,1,0:T(8,128)(2,1)}, u32[]{:S(2)}) copy-start(bf16[2,512,2048]{2,1,0:T(8,128)(2,1)} %weight.7) | copy-start | bytes 12582916
  3.0 4.4 %collective-permute-start.2 = (bf16[8,512]{1,0:T(8,128)(2,1)S(1)}, bf16[8,512]{1,0:T(8,128)(2,1)S(1)}, u32[]{:S(2)}, u32[]{:S(2)}) collective-permute-start(bf16[8,512]{1,0:T(8,128)(2,1)S(1)} %get-tuple-element.32), channel_id=1, source_target_pairs={{0,5},{1,4},{2,7},{3,6},{4,1},{5,0},{6,3},{7,2},{8,13},{9,12},{10,... | collective-permute-start | bytes 24584 | tf_op jit(solution)/shard_map/ppermute | solution.py:410
  5.5 1.9 %collective-permute-start = (bf16[8,512]{1,0:T(8,128)(2,1)S(1)}, bf16[8,512]{1,0:T(8,128)(2,1)S(1)}, u32[]{:S(2)}, u32[]{:S(2)}) collective-permute-start(bf16[8,512]{1,0:T(8,128)(2,1)S(1)} %get-tuple-element.32), channel_id=1, source_target_pairs={{0,1},{1,0},{2,3},{3,2},{4,5},{5,4},{6,7},{7,6},{8,9},{9,8},{10,11... | collective-permute-start | bytes 24584 | tf_op jit(solution)/shard_map/ppermute | solution.py:410
  6.2 4.0 %collective-permute-start.3 = (bf16[8,512]{1,0:T(8,128)(2,1)S(1)}, bf16[8,512]{1,0:T(8,128)(2,1)S(1)}, u32[]{:S(2)}, u32[]{:S(2)}) collective-permute-start(bf16[8,512]{1,0:T(8,128)(2,1)S(1)} %get-tuple-element.33), channel_id=1, source_target_pairs={{0,7},{1,6},{2,5},{3,4},{4,3},{5,2},{6,1},{7,0},{8,15},{9,14},{10,... | collective-permute-start | bytes 24584 | tf_op jit(solution)/shard_map/ppermute | solution.py:410
  7.2 3.1 %collective-permute-start.1 = (bf16[8,512]{1,0:T(8,128)(2,1)S(1)}, bf16[8,512]{1,0:T(8,128)(2,1)S(1)}, u32[]{:S(2)}, u32[]{:S(2)}) collective-permute-start(bf16[8,512]{1,0:T(8,128)(2,1)S(1)} %get-tuple-element.33), channel_id=1, source_target_pairs={{0,3},{1,2},{2,1},{3,0},{4,7},{5,6},{6,5},{7,4},{8,11},{9,10},{10,... | collective-permute-start | bytes 24584 | tf_op jit(solution)/shard_map/ppermute | solution.py:410
  10.3 10.9 %slice-start = ((s8[14680064]{0:T(1024)(128)(4,1)}), s8[4194304]{0:T(1024)(128)(4,1)S(1)}, s32[]{:S(2)}) async-start(s8[14680064]{0:T(1024)(128)(4,1)} %bitcast.2), calls=%async_computation | async-start | bytes 8388608
  10.3 10.9 %slice-start.1 = ((s8[14680064]{0:T(1024)(128)(4,1)}), s8[4194304]{0:T(1024)(128)(4,1)S(1)}, s32[]{:S(2)}) async-start(s8[14680064]{0:T(1024)(128)(4,1)} %bitcast.2), calls=%async_computation.1 | async-start | bytes 8388608
  10.3 4.3 %collective-permute-start.5 = (bf16[4,8,512]{2,1,0:T(8,128)(2,1)S(1)}, bf16[4,8,512]{2,1,0:T(8,128)(2,1)S(1)}, u32[]{:S(2)}, u32[]{:S(2)}) collective-permute-start(bf16[4,8,512]{2,1,0:T(8,128)(2,1)S(1)} %stack.1), channel_id=1, source_target_pairs={{0,9},{1,8},{4,13},{5,12},{8,1},{9,0},{12,5},{13,4},{2,11},{3,10},... | collective-permute-start | bytes 98312 | tf_op jit(solution)/shard_map/ppermute | solution.py:423
  13.0 1.6 %collective-permute-start.4 = (bf16[4,8,512]{2,1,0:T(8,128)(2,1)S(1)}, bf16[4,8,512]{2,1,0:T(8,128)(2,1)S(1)}, u32[]{:S(2)}, u32[]{:S(2)}) collective-permute-start(bf16[4,8,512]{2,1,0:T(8,128)(2,1)S(1)} %stack.1), channel_id=1, source_target_pairs={{0,1},{1,0},{4,5},{5,4},{8,9},{9,8},{12,13},{13,12},{2,3},{3,2},{6... | collective-permute-start | bytes 98312 | tf_op jit(solution)/shard_map/ppermute | solution.py:423
  14.6 6.5 %slice-start.2 = ((s8[14680064]{0:T(1024)(128)(4,1)}), s8[4194304]{0:T(1024)(128)(4,1)S(1)}, s32[]{:S(2)}) async-start(s8[14680064]{0:T(1024)(128)(4,1)} %bitcast.2), calls=%async_computation.2 | async-start | bytes 8388608
  14.6 6.5 %slice-start.3 = ((s8[14680064]{0:T(1024)(128)(4,1)}), s8[2097152]{0:T(1024)(128)(4,1)S(1)}, s32[]{:S(2)}) async-start(s8[14680064]{0:T(1024)(128)(4,1)} %bitcast.2), calls=%async_computation.3 | async-start | bytes 4194304
  15.3 1.4 %collective-permute-start.6 = (bf16[32,1024]{1,0:T(8,128)(2,1)S(1)}, bf16[32,1024]{1,0:T(8,128)(2,1)S(1)}, u32[]{:S(2)}, u32[]{:S(2)}) collective-permute-start(bf16[32,1024]{1,0:T(8,128)(2,1)S(1)} %get-tuple-element.35), channel_id=1, source_target_pairs={{0,1},{1,0},{2,3},{3,2},{4,5},{5,4},{6,7},{7,6},{8,9},{9,8},{10,11... | collective-permute-start | bytes 196616 | tf_op jit(solution)/shard_map/ppermute | solution.py:436
  16.7 4.5 %collective-permute-start.7 = (bf16[32,1024]{1,0:T(8,128)(2,1)S(1)}, bf16[32,1024]{1,0:T(8,128)(2,1)S(1)}, u32[]{:S(2)}, u32[]{:S(2)}) collective-permute-start(bf16[32,1024]{1,0:T(8,128)(2,1)S(1)} %add.1.refs_0_), channel_id=1, source_target_pairs={{0,2},{2,0},{1,3},{3,1},{4,6},{6,4},{5,7},{7,5},{8,10},{10,8},{9,1... | collective-permute-start | bytes 196616 | tf_op jit(solution)/shard_map/ppermute | solution.py:454
  21.2 3.5 %collective-permute-start.8 = (bf16[32,1024]{1,0:T(8,128)(2,1)S(1)}, bf16[32,1024]{1,0:T(8,128)(2,1)S(1)}, u32[]{:S(2)}, u32[]{:S(2)}) collective-permute-start(bf16[32,1024]{1,0:T(8,128)(2,1)S(1)} %get-tuple-element.36.mid.refs_0_), channel_id=1, source_target_pairs={{0,1},{1,0},{2,3},{3,2},{4,5},{5,4},{6,7},{7,6},{8,9},{9,8},{10,11... | collective-permute-start | bytes 196616 | tf_op jit(solution)/shard_map/ppermute | solution.py:468
  24.7 23.0 %slice-start.4 = ((s8[14680064]{0:T(1024)(128)(4,1)}), s8[4194304]{0:T(1024)(128)(4,1)S(1)}, s32[]{:S(2)}) async-start(s8[14680064]{0:T(1024)(128)(4,1)} %bitcast.4), calls=%async_computation.4 | async-start | bytes 8388608
  24.8 23.0 %slice-start.5 = ((s8[14680064]{0:T(1024)(128)(4,1)}), s8[4194304]{0:T(1024)(128)(4,1)S(1)}, s32[]{:S(2)}) async-start(s8[14680064]{0:T(1024)(128)(4,1)} %bitcast.4), calls=%async_computation.5 | async-start | bytes 8388608
  26.1 21.7 %slice-start.6 = ((s8[14680064]{0:T(1024)(128)(4,1)}), s8[4194304]{0:T(1024)(128)(4,1)S(1)}, s32[]{:S(2)}) async-start(s8[14680064]{0:T(1024)(128)(4,1)} %bitcast.4), calls=%async_computation.6 | async-start | bytes 8388608
  26.1 21.7 %slice-start.7 = ((s8[14680064]{0:T(1024)(128)(4,1)}), s8[2097152]{0:T(1024)(128)(4,1)S(1)}, s32[]{:S(2)}) async-start(s8[14680064]{0:T(1024)(128)(4,1)} %bitcast.4), calls=%async_computation.7 | async-start | bytes 4194304
  27.4 7.3 %collective-permute-start.9 = (bf16[8,7296]{1,0:T(8,128)(2,1)S(1)}, bf16[8,7296]{1,0:T(8,128)(2,1)S(1)}, u32[]{:S(2)}, u32[]{:S(2)}) collective-permute-start(bf16[8,7296]{1,0:T(8,128)(2,1)S(1)} %get-tuple-element.46), channel_id=1, source_target_pairs={{0,12},{4,8},{8,4},{12,0},{1,13},{5,9},{9,5},{13,1},{2,14},{6,10},... | collective-permute-start | bytes 350216 | tf_op jit(solution)/shard_map/ppermute | solution.py:514
  30.9 8.8 %collective-permute-start.10 = (bf16[8,7296]{1,0:T(8,128)(2,1)S(1)}, bf16[8,7296]{1,0:T(8,128)(2,1)S(1)}, u32[]{:S(2)}, u32[]{:S(2)}) collective-permute-start(bf16[8,7296]{1,0:T(8,128)(2,1)S(1)} %get-tuple-element.47), channel_id=1, source_target_pairs={{0,8},{4,12},{8,0},{12,4},{1,9},{5,13},{9,1},{13,5},{2,10},{6,14},... | collective-permute-start | bytes 350216 | tf_op jit(solution)/shard_map/ppermute | solution.py:514
  30.9 8.8 %collective-permute-start.11 = (bf16[8,7296]{1,0:T(8,128)(2,1)S(1)}, bf16[8,7296]{1,0:T(8,128)(2,1)S(1)}, u32[]{:S(2)}, u32[]{:S(2)}) collective-permute-start(bf16[8,7296]{1,0:T(8,128)(2,1)S(1)} %get-tuple-element.48), channel_id=1, source_target_pairs={{0,4},{4,0},{8,12},{12,8},{1,5},{5,1},{9,13},{13,9},{2,6},{6,2},{1... | collective-permute-start | bytes 350216 | tf_op jit(solution)/shard_map/ppermute | solution.py:514
  39.9 6.0 %collective-permute-start.14 = (bf16[8,3584]{1,0:T(8,128)(2,1)S(1)}, bf16[8,3584]{1,0:T(8,128)(2,1)S(1)}, u32[]{:S(2)}, u32[]{:S(2)}) collective-permute-start(bf16[8,3584]{1,0:T(8,128)(2,1)S(1)} %activate.1.refs_0_), channel_id=1, source_target_pairs={{0,12},{4,8},{8,4},{12,0},{1,13},{5,9},{9,5},{13,1},{2,14},{6,10},... | collective-permute-start | bytes 172040 | tf_op jit(solution)/shard_map/ppermute | solution.py:524
  42.7 5.1 %collective-permute-start.13 = (bf16[8,3584]{1,0:T(8,128)(2,1)S(1)}, bf16[8,3584]{1,0:T(8,128)(2,1)S(1)}, u32[]{:S(2)}, u32[]{:S(2)}) collective-permute-start(bf16[8,3584]{1,0:T(8,128)(2,1)S(1)} %activate.1.refs_0_), channel_id=1, source_target_pairs={{0,8},{4,12},{8,0},{12,4},{1,9},{5,13},{9,1},{13,5},{2,10},{6,14},... | collective-permute-start | bytes 172040 | tf_op jit(solution)/shard_map/ppermute | solution.py:524
  42.7 5.1 %collective-permute-start.12 = (bf16[8,3584]{1,0:T(8,128)(2,1)S(1)}, bf16[8,3584]{1,0:T(8,128)(2,1)S(1)}, u32[]{:S(2)}, u32[]{:S(2)}) collective-permute-start(bf16[8,3584]{1,0:T(8,128)(2,1)S(1)} %activate.1.refs_0_), channel_id=1, source_target_pairs={{0,4},{4,0},{8,12},{12,8},{1,5},{5,1},{9,13},{13,9},{2,6},{6,2},{1... | collective-permute-start | bytes 172040 | tf_op jit(solution)/shard_map/ppermute | solution.py:524
  50.4 3.5 %collective-permute-start.15 = (bf16[8,2048]{1,0:T(8,128)(2,1)S(1)}, bf16[8,2048]{1,0:T(8,128)(2,1)S(1)}, u32[]{:S(2)}, u32[]{:S(2)}) collective-permute-start(bf16[8,2048]{1,0:T(8,128)(2,1)S(1)} %get-tuple-element.50), channel_id=1, source_target_pairs={{0,3},{1,2},{2,1},{3,0},{4,7},{5,6},{6,5},{7,4},{8,11},{9,10},{10,... | collective-permute-start | bytes 98312 | tf_op jit(solution)/shard_map/ppermute | solution.py:536
  50.5 4.0 %collective-permute-start.16 = (bf16[8,2048]{1,0:T(8,128)(2,1)S(1)}, bf16[8,2048]{1,0:T(8,128)(2,1)S(1)}, u32[]{:S(2)}, u32[]{:S(2)}) collective-permute-start(bf16[8,2048]{1,0:T(8,128)(2,1)S(1)} %get-tuple-element.51), channel_id=1, source_target_pairs={{0,2},{1,3},{2,0},{3,1},{4,6},{5,7},{6,4},{7,5},{8,10},{9,11},{10,... | collective-permute-start | bytes 98312 | tf_op jit(solution)/shard_map/ppermute | solution.py:536
  52.1 2.4 %collective-permute-start.17 = (bf16[8,2048]{1,0:T(8,128)(2,1)S(1)}, bf16[8,2048]{1,0:T(8,128)(2,1)S(1)}, u32[]{:S(2)}, u32[]{:S(2)}) collective-permute-start(bf16[8,2048]{1,0:T(8,128)(2,1)S(1)} %get-tuple-element.52), channel_id=1, source_target_pairs={{0,1},{1,0},{2,3},{3,2},{4,5},{5,4},{6,7},{7,6},{8,9},{9,8},{10,11... | collective-permute-start | bytes 98312 | tf_op jit(solution)/shard_map/ppermute | solution.py:536

commit v8 on v7

--- a/solution.py
+++ b/solution.py
@@ -36,7 +36,7 @@
     slots, span, width = key_buf.shape
     kv_here = width // HEAD_DIM
     group = queries.shape[1] // width
-    rows = group * slots
+    rows = kv_here * group * slots
     small = [(lens_in, lens), (queries_in, queries), (new_key_in, new_key)]
     small.append((new_value_in, new_value))
     pairs = small + [(keys.at[s], key_buf.at[s]) for s in range(slots)]
@@ -59,61 +59,49 @@
     for s in range(slots):
         live_len = jnp.where(slot_id == s, lens[s], live_len)
     live = lax.broadcasted_iota(jnp.int32, (rows, span), 1) < live_len
+    kv_id = lax.broadcasted_iota(jnp.int32, (rows, width), 0) // (group * slots)
+    mine = kv_id == lax.broadcasted_iota(jnp.int32, (rows, width), 1) // HEAD_DIM
     q_all = queries[...].astype(F32)
-    own_k = new_key[...].astype(F32)
-    own_v = new_value[...].astype(F32)
-    heads_q, own_score = [], []
-    for g in range(kv_here):
-        cols = slice(g * HEAD_DIM, (g + 1) * HEAD_DIM)
-        first = g * group
-        q = jnp.concatenate(
-            [
-                q_all[:, (first + h) * HEAD_DIM : (first + h + 1) * HEAD_DIM]
-                for h in range(group)
-            ],
-            axis=0,
-        )
-        k = jnp.concatenate([own_k[:, cols]] * group, axis=0)
-        own_score.append(jnp.sum(q * k, axis=1, keepdims=True) * scale)
-        heads_q.append(q.astype(BF16))
-    scores = [jnp.zeros((rows, span), F32) for _ in range(kv_here)]
+    heads = kv_here * group
+    heads_q = jnp.concatenate(
+        [q_all[:, h * HEAD_DIM : (h + 1) * HEAD_DIM] for h in range(heads)], axis=0
+    )
+    heads_q = jnp.where(mine, jnp.concatenate([heads_q] * kv_here, axis=1), 0.0)
+    own_k = jnp.concatenate([new_key[...].astype(F32)] * heads, axis=0)
+    own_v = jnp.concatenate([new_value[...].astype(F32)] * heads, axis=0)
+    own_score = jnp.sum(heads_q * own_k, axis=1, keepdims=True) * scale
+    heads_q = heads_q.astype(BF16)
+    scores = jnp.zeros((rows, span), F32)
     for s in range(slots):
         loads[s].wait()
-        for g in range(kv_here):
-            here = lax.dot_general(
-                heads_q[g],
-                key_buf[s, :, g * HEAD_DIM : (g + 1) * HEAD_DIM],
-                (((1,), (1,)), ((), ())),
-                preferred_element_type=F32,
-            )
-            scores[g] = jnp.where(slot_id == s, here, scores[g])
-    probs, totals = [], []
-    for g in range(kv_here):
-        masked = jnp.where(live, scores[g] * scale, -jnp.inf)
-        top = jnp.maximum(jnp.max(masked, axis=1, keepdims=True), own_score[g])
-        exp_cache = jnp.exp(masked - top)
-        exp_own = jnp.exp(own_score[g] - top)
-        total = jnp.sum(exp_cache, axis=1, keepdims=True) + exp_own
-        probs.append((exp_cache / total).astype(BF16))
-        own = jnp.concatenate(
-            [own_v[:, g * HEAD_DIM : (g + 1) * HEAD_DIM]] * group, axis=0
+        here = lax.dot_general(
+            heads_q, key_buf[s], (((1,), (1,)), ((), ())), preferred_element_type=F32
         )
-        totals.append((exp_own / total).astype(BF16).astype(F32) * own)
+        scores = jnp.where(slot_id == s, here, scores)
+    masked = jnp.where(live, scores * scale, -jnp.inf)
+    top = jnp.maximum(jnp.max(masked, axis=1, keepdims=True), own_score)
+    exp_cache = jnp.exp(masked - top)
+    exp_own = jnp.exp(own_score - top)
+    total = jnp.sum(exp_cache, axis=1, keepdims=True) + exp_own
+    probs = (exp_cache / total).astype(BF16)
+    sums = (exp_own / total).astype(BF16).astype(F32) * own_v
     for s in range(slots):
         loads[slots + s].wait()
-        for g in range(kv_here):
-            here = jnp.where(slot_id == s, probs[g], jnp.zeros_like(probs[g]))
-            totals[g] += jnp.dot(
-                here,
-                value_buf[s, :, g * HEAD_DIM : (g + 1) * HEAD_DIM],
-                preferred_element_type=F32,
-            )
+        here = jnp.where(slot_id == s, probs, jnp.zeros_like(probs))
+        sums += jnp.dot(here, value_buf[s], preferred_element_type=F32)
     heads_out = group // peers
     for f in range(peers):
         shares[f] = jnp.concatenate(
             [
                 jnp.concatenate(
-                    [totals[g][h * slots : (h + 1) * slots] for g in range(kv_here)], axis=0
+                    [
+                        sums[
+                            (g * group + h) * slots : (g * group + h + 1) * slots,
+                            g * HEAD_DIM : (g + 1) * HEAD_DIM,
+                        ]
+                        for g in range(kv_here)
+                    ],
+                    axis=0,
                 )
                 for h in range(f * heads_out, (f + 1) * heads_out)
             ],

time: 55.3 us -> 55.3 us (level)
  no operation moved by 1% of the time
where the time goes in v8:
time: 55.3 us; the launch traced here: 55.1 us
  starting transfers between devices  21.2 us (38%)
  waiting for transfers between devices  20.9 us (38%)
  Pallas kernels  12.7 us (23%)
    ppermute x3, waiting for transfers between devices, shards(): lax.ppermute(parts[k], 'tok', swap(tok, k))  7.8 us
    ppermute x3, starting transfers between devices, shards(): lax.ppermute(parts[k], 'tok', swap(tok, k))  4.45 us
    ppermute x3, starting transfers between devices, shards(): lax.ppermute(hidden, 'tok', swap(tok, k))  4.45 us
    ppermute x4, starting transfers between devices, shards(): lax.ppermute(attended[k % ffn], ('tok', 'ffn', 'rep'), swap(owners * rep,...  4.43 us
    ppermute x3, waiting for transfers between devices, shards(): lax.ppermute(hidden, 'tok', swap(tok, k))  3.43 us
    pallas_call x1, Pallas kernels, shards(): pl.pallas_call(functools.partial(attend, ffn), out_shape=[like(table_rows...  2.91 us
    ppermute x4, waiting for transfers between devices, shards(): lax.ppermute(attended[k % ffn], ('tok', 'ffn', 'rep'), swap(owners * rep,...  2.86 us
    ppermute x2, starting transfers between devices, shards(): lax.ppermute(close, ('tok', 'rep'), swap(tok * rep, k * rep + rep - 1))  2.77 us
  transfers between devices with their start and end apart: 18, of which 11 were waited for; matrix products, arithmetic and copies ran while one was open for 0% of the time, Pallas kernels for 5%

profile of v8, /device:TPU:0, one launch (start us, length us, event | category | flops | bytes accessed | tf_op | source)
XLA Modules:
  0.0 55.1 jit_solution(15427099185373734738)
XLA Ops:
  0.0 0.0 copy-start
  0.0 2.9 %attend.1 = (bf16[8,512]{1,0:T(8,128)(2,1)S(1)}, bf16[8,512]{1,0:T(8,128)(2,1)S(1)}, s32[1,32]{1,0:T(1,128)S(1)}, bf16[2,32,1024]{2,1,0:T(8,128)(2,1)S(1)}, f32[2,1,1024]{2,1,0:T(1,128)S(1)}) custom-call(s32[4]{0:T(128)} %lens_in.1, bf16[4,2048]{1,0:T(4,128)(2,1)} %queries_in.1, bf16[4,256]{1,0:T(4,128)(2,1)} %new_key_in.1, bf16[4,256]{1,0:T(4,128)(2,1)} %new_value_in.1, ...), custom_call_target="tpu_custom_call" | custom-call | flops 20000000000 | tf_op jit(solution)/shard_map/attend/pallas_call | solution.py:363
  2.9 0.0 copy-start.1
  2.9 2.5 %collective-permute-start.2 = (bf16[8,512]{1,0:T(8,128)(2,1)S(1)}, bf16[8,512]{1,0:T(8,128)(2,1)S(1)}, u32[]{:S(2)}, u32[]{:S(2)}) collective-permute-start(bf16[8,512]{1,0:T(8,128)(2,1)S(1)} %get-tuple-element.32), channel_id=1, source_target_pairs={{0,5},{1,4},{2,7},{3,6},{4,1},{5,0},{6,3},{7,2},{8,13},{9,12},{10,... | collective-permute-start | bytes 24584 | tf_op jit(solution)/shard_map/ppermute | solution.py:398
  5.5 0.7 %collective-permute-start = (bf16[8,512]{1,0:T(8,128)(2,1)S(1)}, bf16[8,512]{1,0:T(8,128)(2,1)S(1)}, u32[]{:S(2)}, u32[]{:S(2)}) collective-permute-start(bf16[8,512]{1,0:T(8,128)(2,1)S(1)} %get-tuple-element.32), channel_id=1, source_target_pairs={{0,1},{1,0},{2,3},{3,2},{4,5},{5,4},{6,7},{7,6},{8,9},{9,8},{10,11... | collective-permute-start | bytes 24584 | tf_op jit(solution)/shard_map/ppermute | solution.py:398
  6.1 1.0 %collective-permute-start.3 = (bf16[8,512]{1,0:T(8,128)(2,1)S(1)}, bf16[8,512]{1,0:T(8,128)(2,1)S(1)}, u32[]{:S(2)}, u32[]{:S(2)}) collective-permute-start(bf16[8,512]{1,0:T(8,128)(2,1)S(1)} %get-tuple-element.33), channel_id=1, source_target_pairs={{0,7},{1,6},{2,5},{3,4},{4,3},{5,2},{6,1},{7,0},{8,15},{9,14},{10,... | collective-permute-start | bytes 24584 | tf_op jit(solution)/shard_map/ppermute | solution.py:398
  7.1 0.2 collective-permute-start.1
  7.4 0.0 collective-permute-done.2.refs_2_
  7.4 0.0 collective-permute-done.refs_0_
  7.4 2.7 %collective-permute-done.3.refs_3_ = bf16[8,512]{1,0:T(8,128)(2,1)S(1)} collective-permute-done((bf16[8,512]{1,0:T(8,128)(2,1)S(1)}, bf16[8,512]{1,0:T(8,128)(2,1)S(1)}, u32[]{:S(2)}, u32[]{:S(2)}) %collective-permute-start.3) | collective-permute-done | bytes 8224 | tf_op jit(solution)/shard_map/ppermute | solution.py:398
  10.1 0.1 collective-permute-done.1.refs_1_
  10.2 0.0 copy-done
  10.2 0.0 slice-start
  10.2 2.7 %collective-permute-start.5 = (bf16[4,8,512]{2,1,0:T(8,128)(2,1)S(1)}, bf16[4,8,512]{2,1,0:T(8,128)(2,1)S(1)}, u32[]{:S(2)}, u32[]{:S(2)}) collective-permute-start(bf16[4,8,512]{2,1,0:T(8,128)(2,1)S(1)} %stack.1), channel_id=1, source_target_pairs={{0,9},{1,8},{4,13},{5,12},{8,1},{9,0},{12,5},{13,4},{2,11},{3,10},... | collective-permute-start | bytes 98312 | tf_op jit(solution)/shard_map/ppermute | solution.py:411
  13.0 0.0 collective-permute-start.4
  13.0 1.6 %collective-permute-done.5.refs_1_ = bf16[4,8,512]{2,1,0:T(8,128)(2,1)S(1)} collective-permute-done((bf16[4,8,512]{2,1,0:T(8,128)(2,1)S(1)}, bf16[4,8,512]{2,1,0:T(8,128)(2,1)S(1)}, u32[]{:S(2)}, u32[]{:S(2)}) %collective-permute-start.5) | collective-permute-done | bytes 32800 | tf_op jit(solution)/shard_map/ppermute | solution.py:411
  14.6 0.0 collective-permute-done.4.refs_0_
  14.6 0.0 copy-done.1
  14.6 0.0 slice-start.3
  14.6 0.6 %project.1 = (bf16[32,1024]{1,0:T(8,128)(2,1)S(1)}, bf16[2,32,512]{2,1,0:T(8,128)(2,1)S(1)}) custom-call(s32[1,32]{1,0:T(1,128)S(1)} %get-tuple-element.31.slot_of, bf16[2,512,2048]{2,1,0:T(8,128)(2,1)S(1)} %copy-done.1, bf16[4,8,512]{2,1,0:T(8,128)(2,1)S(1)} %collective-permute-done.4.refs_0_, bf16[4,8,512]{2,1,0:T(8,128)(2,1)S(1)} %collective-permute-done.5.refs_1_), custom_call_target="tpu_custom_call" | custom-call | flops 10000000000 | tf_op jit(solution)/shard_map/project/pallas_call | solution.py:415
  15.2 0.5 collective-permute-start.6
  15.7 0.5 project_own.1.refs_0_
  16.2 0.4 collective-permute-done.6.refs_1_
  16.6 1.9 %collective-permute-start.7 = (bf16[32,1024]{1,0:T(8,128)(2,1)S(1)}, bf16[32,1024]{1,0:T(8,128)(2,1)S(1)}, u32[]{:S(2)}, u32[]{:S(2)}) collective-permute-start(bf16[32,1024]{1,0:T(8,128)(2,1)S(1)} %add.1.refs_0_), channel_id=1, source_target_pairs={{0,2},{2,0},{1,3},{3,1},{4,6},{6,4},{5,7},{7,5},{8,10},{10,8},{9,1... | collective-permute-start | bytes 196616 | tf_op jit(solution)/shard_map/ppermute | solution.py:442
  18.5 2.6 %collective-permute-done.7.refs_1_ = bf16[32,1024]{1,0:T(8,128)(2,1)S(1)} collective-permute-done((bf16[32,1024]{1,0:T(8,128)(2,1)S(1)}, bf16[32,1024]{1,0:T(8,128)(2,1)S(1)}, u32[]{:S(2)}, u32[]{:S(2)}) %collective-permute-start.7) | collective-permute-done | bytes 65568 | tf_op jit(solution)/shard_map/ppermute | solution.py:442
  21.1 0.0 slice-done
  21.1 0.0 slice-done.1
  21.1 0.0 slice-done.2
  21.1 0.0 slice-done.3
  21.2 0.9 %collective-permute-start.8 = (bf16[32,1024]{1,0:T(8,128)(2,1)S(1)}, bf16[32,1024]{1,0:T(8,128)(2,1)S(1)}, u32[]{:S(2)}, u32[]{:S(2)}) collective-permute-start(bf16[32,1024]{1,0:T(8,128)(2,1)S(1)} %get-tuple-element.36.mid.refs_0_), channel_id=1, source_target_pairs={{0,1},{1,0},{2,3},{3,2},{4,5},{5,4},{6,7},{7,6},{8,9},{9,8},{10,11... | collective-permute-start | bytes 196616 | tf_op jit(solution)/shard_map/ppermute | solution.py:456
  22.1 1.3 %gate_next.1 = (bf16[32,1024]{1,0:T(8,128)(2,1)S(1)}, f32[32,3584]{1,0:T(8,128)S(1)}) custom-call(bf16[32,1024]{1,0:T(8,128)(2,1)S(1)} %get-tuple-element.36.mid.refs_0_, f32[2,1,1024]{2,1,0:T(1,128)S(1)} %get-tuple-element.30.gain.refs_2_, bf16[2048,3584]{1,0:T(8,128)(2,1)S(1)} %copy-done, ...), custom_call_target="tpu_custom_call", output_to_operand_aliasing={{0}: (3, {}), {1}: (4, {})} | custom-call | tf_op jit(solution)/shard_map/gate_next/pallas_call | solution.py:458
  23.4 1.3 %up_own.1.sums = f32[32,3584]{1,0:T(8,128)S(1)} custom-call(bf16[32,1024]{1,0:T(8,128)(2,1)S(1)} %get-tuple-element.41.left, bf16[2048,3584]{1,0:T(8,128)(2,1)S(1)} %bitcast.3), custom_call_target="tpu_custom_call" | custom-call | tf_op jit(solution)/shard_map/up_own/pallas_call | solution.py:468
  24.7 0.0 collective-permute-done.8.refs_1_
  24.7 0.0 slice-start.4
  24.7 0.0 slice-start.5
  24.7 1.3 %gate_rest.1 = (bf16[2,4,8,1024]{3,2,1,0:T(8,128)(2,1)S(1)}, bf16[1,32,1024]{2,1,0:T(8,128)(2,1)S(1)}, bf16[4,8,128]{2,1,0:T(8,128)(2,1)S(1)}, bf16[4,8,3584]{2,1,0:T(8,128)(2,1)S(1)}) custom-call(bf16[32,1024]{1,0:T(8,128)(2,1)S(1)} %get-tuple-element.36.mid.refs_0_, bf16[32,1024]{1,0:T(8,128)(2,1)S(1)} %collective-permute-done.8.refs_1_, ...), custom_call_target="tpu_custom_call" | custom-call | tf_op jit(solution)/shard_map/gate_rest/pallas_call | solution.py:476
  26.0 0.0 slice-start.6
  26.1 0.0 slice-start.7
  26.1 1.3 %up_rest.1 = (bf16[8,7296]{1,0:T(8,128)(2,1)S(1)}, bf16[8,7296]{1,0:T(8,128)(2,1)S(1)}, bf16[8,7296]{1,0:T(8,128)(2,1)S(1)}, bf16[8,7296]{1,0:T(8,128)(2,1)S(1)}) custom-call(f32[32,3584]{1,0:T(8,128)S(1)} %up_own.1.sums, bf16[1,32,1024]{2,1,0:T(8,128)(2,1)S(1)} %get-tuple-element.42.rest, bf16[4,8,128]{2,1,0:T(8,128)(2,1)S(1)} %get-tuple-element.43.stat, ...), custom_call_target="tpu_custom_call" | custom-call | tf_op jit(solution)/shard_map/up_rest/pallas_call | solution.py:493
  27.4 3.4 %collective-permute-start.9 = (bf16[8,7296]{1,0:T(8,128)(2,1)S(1)}, bf16[8,7296]{1,0:T(8,128)(2,1)S(1)}, u32[]{:S(2)}, u32[]{:S(2)}) collective-permute-start(bf16[8,7296]{1,0:T(8,128)(2,1)S(1)} %get-tuple-element.46), channel_id=1, source_target_pairs={{0,12},{4,8},{8,4},{12,0},{1,13},{5,9},{9,5},{13,1},{2,14},{6,10},... | collective-permute-start | bytes 350216 | tf_op jit(solution)/shard_map/ppermute | solution.py:502
  30.8 0.0 collective-permute-start.10
  30.8 1.0 %collective-permute-start.11 = (bf16[8,7296]{1,0:T(8,128)(2,1)S(1)}, bf16[8,7296]{1,0:T(8,128)(2,1)S(1)}, u32[]{:S(2)}, u32[]{:S(2)}) collective-permute-start(bf16[8,7296]{1,0:T(8,128)(2,1)S(1)} %get-tuple-element.48), channel_id=1, source_target_pairs={{0,4},{4,0},{8,12},{12,8},{1,5},{5,1},{9,13},{13,9},{2,6},{6,2},{1... | collective-permute-start | bytes 350216 | tf_op jit(solution)/shard_map/ppermute | solution.py:502
  31.8 2.8 %collective-permute-done.9.refs_1_ = bf16[8,7296]{1,0:T(8,128)(2,1)S(1)} collective-permute-done((bf16[8,7296]{1,0:T(8,128)(2,1)S(1)}, bf16[8,7296]{1,0:T(8,128)(2,1)S(1)}, u32[]{:S(2)}, u32[]{:S(2)}) %collective-permute-start.9) | collective-permute-done | bytes 116768 | tf_op jit(solution)/shard_map/ppermute | solution.py:502
  34.6 5.0 %collective-permute-done.10.refs_2_ = bf16[8,7296]{1,0:T(8,128)(2,1)S(1)} collective-permute-done((bf16[8,7296]{1,0:T(8,128)(2,1)S(1)}, bf16[8,7296]{1,0:T(8,128)(2,1)S(1)}, u32[]{:S(2)}, u32[]{:S(2)}) %collective-permute-start.10) | collective-permute-done | bytes 116768 | tf_op jit(solution)/shard_map/ppermute | solution.py:502
  39.6 0.0 collective-permute-done.11.refs_3_
  39.6 0.2 activate.1.refs_0_
  39.8 2.8 %collective-permute-start.14 = (bf16[8,3584]{1,0:T(8,128)(2,1)S(1)}, bf16[8,3584]{1,0:T(8,128)(2,1)S(1)}, u32[]{:S(2)}, u32[]{:S(2)}) collective-permute-start(bf16[8,3584]{1,0:T(8,128)(2,1)S(1)} %activate.1.refs_0_), channel_id=1, source_target_pairs={{0,12},{4,8},{8,4},{12,0},{1,13},{5,9},{9,5},{13,1},{2,14},{6,10},... | collective-permute-start | bytes 172040 | tf_op jit(solution)/shard_map/ppermute | solution.py:512
  42.6 0.0 collective-permute-start.13
  42.6 1.6 %collective-permute-start.12 = (bf16[8,3584]{1,0:T(8,128)(2,1)S(1)}, bf16[8,3584]{1,0:T(8,128)(2,1)S(1)}, u32[]{:S(2)}, u32[]{:S(2)}) collective-permute-start(bf16[8,3584]{1,0:T(8,128)(2,1)S(1)} %activate.1.refs_0_), channel_id=1, source_target_pairs={{0,4},{4,0},{8,12},{12,8},{1,5},{5,1},{9,13},{13,9},{2,6},{6,2},{1... | collective-permute-start | bytes 172040 | tf_op jit(solution)/shard_map/ppermute | solution.py:512
  44.3 1.6 %collective-permute-done.14.refs_3_ = bf16[8,3584]{1,0:T(8,128)(2,1)S(1)} collective-permute-done((bf16[8,3584]{1,0:T(8,128)(2,1)S(1)}, bf16[8,3584]{1,0:T(8,128)(2,1)S(1)}, u32[]{:S(2)}, u32[]{:S(2)}) %collective-permute-start.14) | collective-permute-done | bytes 57376 | tf_op jit(solution)/shard_map/ppermute | solution.py:512
  45.9 1.8 %collective-permute-done.13.refs_2_ = bf16[8,3584]{1,0:T(8,128)(2,1)S(1)} collective-permute-done((bf16[8,3584]{1,0:T(8,128)(2,1)S(1)}, bf16[8,3584]{1,0:T(8,128)(2,1)S(1)}, u32[]{:S(2)}, u32[]{:S(2)}) %collective-permute-start.13) | collective-permute-done | bytes 57376 | tf_op jit(solution)/shard_map/ppermute | solution.py:512
  47.7 0.0 collective-permute-done.12.refs_1_
  47.7 0.0 slice-done.4
  47.7 0.0 slice-done.5
  47.7 0.0 slice-done.6
  47.7 0.0 slice-done.7
  47.8 2.6 %down.1 = (bf16[8,2048]{1,0:T(8,128)(2,1)S(1)}, bf16[8,2048]{1,0:T(8,128)(2,1)S(1)}, bf16[8,2048]{1,0:T(8,128)(2,1)S(1)}, bf16[8,2048]{1,0:T(8,128)(2,1)S(1)}) custom-call(bf16[8,3584]{1,0:T(8,128)(2,1)S(1)} %activate.1.refs_0_, bf16[8,3584]{1,0:T(8,128)(2,1)S(1)} %collective-permute-done.12.refs_1_, bf16[8,3584]{1,0:T(8,128)(2,1)S(1)} %collective-permute-done.13.refs_2_, ...), custom_call_target="tpu_custom_call" | custom-call | tf_op jit(solution)/shard_map/down/pallas_call | solution.py:514
  50.4 0.0 collective-permute-start.15
  50.4 1.7 %collective-permute-start.16 = (bf16[8,2048]{1,0:T(8,128)(2,1)S(1)}, bf16[8,2048]{1,0:T(8,128)(2,1)S(1)}, u32[]{:S(2)}, u32[]{:S(2)}) collective-permute-start(bf16[8,2048]{1,0:T(8,128)(2,1)S(1)} %get-tuple-element.51), channel_id=1, source_target_pairs={{0,2},{1,3},{2,0},{3,1},{4,6},{5,7},{6,4},{7,5},{8,10},{9,11},{10,... | collective-permute-start | bytes 98312 | tf_op jit(solution)/shard_map/ppermute | solution.py:524
  52.1 0.2 collective-permute-start.17
  52.3 1.7 %collective-permute-done.15.refs_1_ = bf16[8,2048]{1,0:T(8,128)(2,1)S(1)} collective-permute-done((bf16[8,2048]{1,0:T(8,128)(2,1)S(1)}, bf16[8,2048]{1,0:T(8,128)(2,1)S(1)}, u32[]{:S(2)}, u32[]{:S(2)}) %collective-permute-start.15) | collective-permute-done | bytes 32800 | tf_op jit(solution)/shard_map/ppermute | solution.py:524
  53.9 0.5 collective-permute-done.16.refs_2_
  54.5 0.0 collective-permute-done.17.refs_3_
  54.5 0.6 %finish.1 = bf16[8,2048]{1,0:T(8,128)(2,1)} custom-call(bf16[2,4,8,1024]{3,2,1,0:T(8,128)(2,1)S(1)} %get-tuple-element.40.mid, bf16[8,2048]{1,0:T(8,128)(2,1)S(1)} %get-tuple-element.49.refs_0_, bf16[8,2048]{1,0:T(8,128)(2,1)S(1)} %collective-permute-done.15.refs_1_, bf16[8,2048]{1,0:T(8,128)(2,1)S(1)} %collective-permute-done.16.refs_2_, ...), custom_call_target="tpu_custom_call" | custom-call | tf_op jit(solution)/shard_map/finish/pallas_call | solution.py:526
  (7 shorter events, 0.1 us)
Async XLA Ops:
  0.0 10.2 %copy-start = (bf16[2048,3584]{1,0:T(8,128)(2,1)S(1)}, bf16[2048,3584]{1,0:T(8,128)(2,1)}, u32[]{:S(2)}) copy-start(bf16[2048,3584]{1,0:T(8,128)(2,1)} %refs_3_.1) | copy-start | bytes 44040196
  2.9 11.7 %copy-start.1 = (bf16[2,512,2048]{2,1,0:T(8,128)(2,1)S(1)}, bf16[2,512,2048]{2,1,0:T(8,128)(2,1)}, u32[]{:S(2)}) copy-start(bf16[2,512,2048]{2,1,0:T(8,128)(2,1)} %weight.7) | copy-start | bytes 12582916
  2.9 4.4 %collective-permute-start.2 = (bf16[8,512]{1,0:T(8,128)(2,1)S(1)}, bf16[8,512]{1,0:T(8,128)(2,1)S(1)}, u32[]{:S(2)}, u32[]{:S(2)}) collective-permute-start(bf16[8,512]{1,0:T(8,128)(2,1)S(1)} %get-tuple-element.32), channel_id=1, source_target_pairs={{0,5},{1,4},{2,7},{3,6},{4,1},{5,0},{6,3},{7,2},{8,13},{9,12},{10,... | collective-permute-start | bytes 24584 | tf_op jit(solution)/shard_map/ppermute | solution.py:398
  5.5 1.9 %collective-permute-start = (bf16[8,512]{1,0:T(8,128)(2,1)S(1)}, bf16[8,512]{1,0:T(8,128)(2,1)S(1)}, u32[]{:S(2)}, u32[]{:S(2)}) collective-permute-start(bf16[8,512]{1,0:T(8,128)(2,1)S(1)} %get-tuple-element.32), channel_id=1, source_target_pairs={{0,1},{1,0},{2,3},{3,2},{4,5},{5,4},{6,7},{7,6},{8,9},{9,8},{10,11... | collective-permute-start | bytes 24584 | tf_op jit(solution)/shard_map/ppermute | solution.py:398
  6.1 4.0 %collective-permute-start.3 = (bf16[8,512]{1,0:T(8,128)(2,1)S(1)}, bf16[8,512]{1,0:T(8,128)(2,1)S(1)}, u32[]{:S(2)}, u32[]{:S(2)}) collective-permute-start(bf16[8,512]{1,0:T(8,128)(2,1)S(1)} %get-tuple-element.33), channel_id=1, source_target_pairs={{0,7},{1,6},{2,5},{3,4},{4,3},{5,2},{6,1},{7,0},{8,15},{9,14},{10,... | collective-permute-start | bytes 24584 | tf_op jit(solution)/shard_map/ppermute | solution.py:398
  7.1 3.1 %collective-permute-start.1 = (bf16[8,512]{1,0:T(8,128)(2,1)S(1)}, bf16[8,512]{1,0:T(8,128)(2,1)S(1)}, u32[]{:S(2)}, u32[]{:S(2)}) collective-permute-start(bf16[8,512]{1,0:T(8,128)(2,1)S(1)} %get-tuple-element.33), channel_id=1, source_target_pairs={{0,3},{1,2},{2,1},{3,0},{4,7},{5,6},{6,5},{7,4},{8,11},{9,10},{10,... | collective-permute-start | bytes 24584 | tf_op jit(solution)/shard_map/ppermute | solution.py:398
  10.2 10.9 %slice-start = ((s8[14680064]{0:T(1024)(128)(4,1)}), s8[4194304]{0:T(1024)(128)(4,1)S(1)}, s32[]{:S(2)}) async-start(s8[14680064]{0:T(1024)(128)(4,1)} %bitcast.2), calls=%async_computation | async-start | bytes 8388608
  10.2 10.9 %slice-start.1 = ((s8[14680064]{0:T(1024)(128)(4,1)}), s8[4194304]{0:T(1024)(128)(4,1)S(1)}, s32[]{:S(2)}) async-start(s8[14680064]{0:T(1024)(128)(4,1)} %bitcast.2), calls=%async_computation.1 | async-start | bytes 8388608
  10.2 4.3 %collective-permute-start.5 = (bf16[4,8,512]{2,1,0:T(8,128)(2,1)S(1)}, bf16[4,8,512]{2,1,0:T(8,128)(2,1)S(1)}, u32[]{:S(2)}, u32[]{:S(2)}) collective-permute-start(bf16[4,8,512]{2,1,0:T(8,128)(2,1)S(1)} %stack.1), channel_id=1, source_target_pairs={{0,9},{1,8},{4,13},{5,12},{8,1},{9,0},{12,5},{13,4},{2,11},{3,10},... | collective-permute-start | bytes 98312 | tf_op jit(solution)/shard_map/ppermute | solution.py:411
  13.0 1.6 %collective-permute-start.4 = (bf16[4,8,512]{2,1,0:T(8,128)(2,1)S(1)}, bf16[4,8,512]{2,1,0:T(8,128)(2,1)S(1)}, u32[]{:S(2)}, u32[]{:S(2)}) collective-permute-start(bf16[4,8,512]{2,1,0:T(8,128)(2,1)S(1)} %stack.1), channel_id=1, source_target_pairs={{0,1},{1,0},{4,5},{5,4},{8,9},{9,8},{12,13},{13,12},{2,3},{3,2},{6... | collective-permute-start | bytes 98312 | tf_op jit(solution)/shard_map/ppermute | solution.py:411
  14.6 6.5 %slice-start.2 = ((s8[14680064]{0:T(1024)(128)(4,1)}), s8[4194304]{0:T(1024)(128)(4,1)S(1)}, s32[]{:S(2)}) async-start(s8[14680064]{0:T(1024)(128)(4,1)} %bitcast.2), calls=%async_computation.2 | async-start | bytes 8388608
  14.6 6.5 %slice-start.3 = ((s8[14680064]{0:T(1024)(128)(4,1)}), s8[2097152]{0:T(1024)(128)(4,1)S(1)}, s32[]{:S(2)}) async-start(s8[14680064]{0:T(1024)(128)(4,1)} %bitcast.2), calls=%async_computation.3 | async-start | bytes 4194304
  15.2 1.4 %collective-permute-start.6 = (bf16[32,1024]{1,0:T(8,128)(2,1)S(1)}, bf16[32,1024]{1,0:T(8,128)(2,1)S(1)}, u32[]{:S(2)}, u32[]{:S(2)}) collective-permute-start(bf16[32,1024]{1,0:T(8,128)(2,1)S(1)} %get-tuple-element.35), channel_id=1, source_target_pairs={{0,1},{1,0},{2,3},{3,2},{4,5},{5,4},{6,7},{7,6},{8,9},{9,8},{10,11... | collective-permute-start | bytes 196616 | tf_op jit(solution)/shard_map/ppermute | solution.py:424
  16.6 4.5 %collective-permute-start.7 = (bf16[32,1024]{1,0:T(8,128)(2,1)S(1)}, bf16[32,1024]{1,0:T(8,128)(2,1)S(1)}, u32[]{:S(2)}, u32[]{:S(2)}) collective-permute-start(bf16[32,1024]{1,0:T(8,128)(2,1)S(1)} %add.1.refs_0_), channel_id=1, source_target_pairs={{0,2},{2,0},{1,3},{3,1},{4,6},{6,4},{5,7},{7,5},{8,10},{10,8},{9,1... | collective-permute-start | bytes 196616 | tf_op jit(solution)/shard_map/ppermute | solution.py:442
  21.2 3.5 %collective-permute-start.8 = (bf16[32,1024]{1,0:T(8,128)(2,1)S(1)}, bf16[32,1024]{1,0:T(8,128)(2,1)S(1)}, u32[]{:S(2)}, u32[]{:S(2)}) collective-permute-start(bf16[32,1024]{1,0:T(8,128)(2,1)S(1)} %get-tuple-element.36.mid.refs_0_), channel_id=1, source_target_pairs={{0,1},{1,0},{2,3},{3,2},{4,5},{5,4},{6,7},{7,6},{8,9},{9,8},{10,11... | collective-permute-start | bytes 196616 | tf_op jit(solution)/shard_map/ppermute | solution.py:456
  24.7 23.0 %slice-start.4 = ((s8[14680064]{0:T(1024)(128)(4,1)}), s8[4194304]{0:T(1024)(128)(4,1)S(1)}, s32[]{:S(2)}) async-start(s8[14680064]{0:T(1024)(128)(4,1)} %bitcast.4), calls=%async_computation.4 | async-start | bytes 8388608
  24.7 23.0 %slice-start.5 = ((s8[14680064]{0:T(1024)(128)(4,1)}), s8[4194304]{0:T(1024)(128)(4,1)S(1)}, s32[]{:S(2)}) async-start(s8[14680064]{0:T(1024)(128)(4,1)} %bitcast.4), calls=%async_computation.5 | async-start | bytes 8388608
  26.0 21.7 %slice-start.6 = ((s8[14680064]{0:T(1024)(128)(4,1)}), s8[4194304]{0:T(1024)(128)(4,1)S(1)}, s32[]{:S(2)}) async-start(s8[14680064]{0:T(1024)(128)(4,1)} %bitcast.4), calls=%async_computation.6 | async-start | bytes 8388608
  26.1 21.7 %slice-start.7 = ((s8[14680064]{0:T(1024)(128)(4,1)}), s8[2097152]{0:T(1024)(128)(4,1)S(1)}, s32[]{:S(2)}) async-start(s8[14680064]{0:T(1024)(128)(4,1)} %bitcast.4), calls=%async_computation.7 | async-start | bytes 4194304
  27.4 7.2 %collective-permute-start.9 = (bf16[8,7296]{1,0:T(8,128)(2,1)S(1)}, bf16[8,7296]{1,0:T(8,128)(2,1)S(1)}, u32[]{:S(2)}, u32[]{:S(2)}) collective-permute-start(bf16[8,7296]{1,0:T(8,128)(2,1)S(1)} %get-tuple-element.46), channel_id=1, source_target_pairs={{0,12},{4,8},{8,4},{12,0},{1,13},{5,9},{9,5},{13,1},{2,14},{6,10},... | collective-permute-start | bytes 350216 | tf_op jit(solution)/shard_map/ppermute | solution.py:502
  30.8 8.8 %collective-permute-start.10 = (bf16[8,7296]{1,0:T(8,128)(2,1)S(1)}, bf16[8,7296]{1,0:T(8,128)(2,1)S(1)}, u32[]{:S(2)}, u32[]{:S(2)}) collective-permute-start(bf16[8,7296]{1,0:T(8,128)(2,1)S(1)} %get-tuple-element.47), channel_id=1, source_target_pairs={{0,8},{4,12},{8,0},{12,4},{1,9},{5,13},{9,1},{13,5},{2,10},{6,14},... | collective-permute-start | bytes 350216 | tf_op jit(solution)/shard_map/ppermute | solution.py:502
  30.8 8.8 %collective-permute-start.11 = (bf16[8,7296]{1,0:T(8,128)(2,1)S(1)}, bf16[8,7296]{1,0:T(8,128)(2,1)S(1)}, u32[]{:S(2)}, u32[]{:S(2)}) collective-permute-start(bf16[8,7296]{1,0:T(8,128)(2,1)S(1)} %get-tuple-element.48), channel_id=1, source_target_pairs={{0,4},{4,0},{8,12},{12,8},{1,5},{5,1},{9,13},{13,9},{2,6},{6,2},{1... | collective-permute-start | bytes 350216 | tf_op jit(solution)/shard_map/ppermute | solution.py:502
  39.8 6.0 %collective-permute-start.14 = (bf16[8,3584]{1,0:T(8,128)(2,1)S(1)}, bf16[8,3584]{1,0:T(8,128)(2,1)S(1)}, u32[]{:S(2)}, u32[]{:S(2)}) collective-permute-start(bf16[8,3584]{1,0:T(8,128)(2,1)S(1)} %activate.1.refs_0_), channel_id=1, source_target_pairs={{0,12},{4,8},{8,4},{12,0},{1,13},{5,9},{9,5},{13,1},{2,14},{6,10},... | collective-permute-start | bytes 172040 | tf_op jit(solution)/shard_map/ppermute | solution.py:512
  42.6 5.1 %collective-permute-start.13 = (bf16[8,3584]{1,0:T(8,128)(2,1)S(1)}, bf16[8,3584]{1,0:T(8,128)(2,1)S(1)}, u32[]{:S(2)}, u32[]{:S(2)}) collective-permute-start(bf16[8,3584]{1,0:T(8,128)(2,1)S(1)} %activate.1.refs_0_), channel_id=1, source_target_pairs={{0,8},{4,12},{8,0},{12,4},{1,9},{5,13},{9,1},{13,5},{2,10},{6,14},... | collective-permute-start | bytes 172040 | tf_op jit(solution)/shard_map/ppermute | solution.py:512
  42.6 5.1 %collective-permute-start.12 = (bf16[8,3584]{1,0:T(8,128)(2,1)S(1)}, bf16[8,3584]{1,0:T(8,128)(2,1)S(1)}, u32[]{:S(2)}, u32[]{:S(2)}) collective-permute-start(bf16[8,3584]{1,0:T(8,128)(2,1)S(1)} %activate.1.refs_0_), channel_id=1, source_target_pairs={{0,4},{4,0},{8,12},{12,8},{1,5},{5,1},{9,13},{13,9},{2,6},{6,2},{1... | collective-permute-start | bytes 172040 | tf_op jit(solution)/shard_map/ppermute | solution.py:512
  50.4 3.5 %collective-permute-start.15 = (bf16[8,2048]{1,0:T(8,128)(2,1)S(1)}, bf16[8,2048]{1,0:T(8,128)(2,1)S(1)}, u32[]{:S(2)}, u32[]{:S(2)}) collective-permute-start(bf16[8,2048]{1,0:T(8,128)(2,1)S(1)} %get-tuple-element.50), channel_id=1, source_target_pairs={{0,3},{1,2},{2,1},{3,0},{4,7},{5,6},{6,5},{7,4},{8,11},{9,10},{10,... | collective-permute-start | bytes 98312 | tf_op jit(solution)/shard_map/ppermute | solution.py:524
  50.4 4.0 %collective-permute-start.16 = (bf16[8,2048]{1,0:T(8,128)(2,1)S(1)}, bf16[8,2048]{1,0:T(8,128)(2,1)S(1)}, u32[]{:S(2)}, u32[]{:S(2)}) collective-permute-start(bf16[8,2048]{1,0:T(8,128)(2,1)S(1)} %get-tuple-element.51), channel_id=1, source_target_pairs={{0,2},{1,3},{2,0},{3,1},{4,6},{5,7},{6,4},{7,5},{8,10},{9,11},{10,... | collective-permute-start | bytes 98312 | tf_op jit(solution)/shard_map/ppermute | solution.py:524
  52.1 2.4 %collective-permute-start.17 = (bf16[8,2048]{1,0:T(8,128)(2,1)S(1)}, bf16[8,2048]{1,0:T(8,128)(2,1)S(1)}, u32[]{:S(2)}, u32[]{:S(2)}) collective-permute-start(bf16[8,2048]{1,0:T(8,128)(2,1)S(1)} %get-tuple-element.52), channel_id=1, source_target_pairs={{0,1},{1,0},{2,3},{3,2},{4,5},{5,4},{6,7},{7,6},{8,9},{9,8},{10,11... | collective-permute-start | bytes 98312 | tf_op jit(solution)/shard_map/ppermute | solution.py:524
